TPU v7x, 128 devices: a whole 4x4x4 slice. The times are simulated.
128 devices in a mesh: section: 2 (over x_lo), replica: 4 (over x_hi, core), shard: 16 (over z, y).
Axes of the slice: x: 4 (x_hi: 2, x_lo: 2; x = x_hi * 2 + x_lo), y: 4, z: 4, core: 2. Of those that a mesh axis runs over, the one named last changes fastest.
Arguments:
- layer_input: bfloat16 [2, 64, 128, 1024], P(None, ('replica', 'shard')), may hold values from -6 to 6
- cotangent: bfloat16 [2, 64, 128, 1024], P(None, ('replica', 'shard')), may hold values from -6 to 6
- project_weight: bfloat16 [2, 1024, 3072], P('section', 'shard'), may hold values from -0.1875 to 0.1875
- output_weight: bfloat16 [2, 1024, 1024], P('section', 'shard'), may hold values from -0.5 to 0.5
- up_weight: bfloat16 [2, 1024, 4096], P('section', 'shard'), may hold values from -0.1875 to 0.1875
- down_weight: bfloat16 [2, 4096, 1024], P('section', 'shard'), may hold values from -0.09375 to 0.09375
- query_bias: bfloat16 [2, 1024], P('section', 'shard'), may hold values from -3 to 3
- value_bias: bfloat16 [2, 1024], P('section', 'shard'), may hold values from -3 to 3
- output_bias: bfloat16 [2, 1024], P('section', 'shard'), may hold values from -3 to 3
- up_bias: bfloat16 [2, 4096], P('section', 'shard'), may hold values from -3 to 3
- down_bias: bfloat16 [2, 1024], P('section', 'shard'), may hold values from -3 to 3
- first_gain: bfloat16 [2, 1024], P('section', 'shard'), may hold values from 0.5 to 1.5
- first_shift: bfloat16 [2, 1024], P('section', 'shard'), may hold values from -2 to 2
- second_gain: bfloat16 [2, 1024], P('section', 'shard'), may hold values from 0.5 to 1.5
- second_shift: bfloat16 [2, 1024], P('section', 'shard'), may hold values from -2 to 2
Outputs:
- layer_output: bfloat16 [2, 2, 64, 128, 1024], P('section', None, ('replica', 'shard'))
- input_grad: bfloat16 [2, 2, 64, 128, 1024], P('section', None, ('replica', 'shard'))
- project_grad: float32 [2, 1024, 3072], P('section', 'shard')
- output_grad: float32 [2, 1024, 1024], P('section', 'shard')
- up_grad: float32 [2, 1024, 4096], P('section', 'shard')
- down_grad: float32 [2, 4096, 1024], P('section', 'shard')
- query_bias_grad: float32 [2, 1024], P('section', 'shard')
- value_bias_grad: float32 [2, 1024], P('section', 'shard')
- output_bias_grad: float32 [2, 1024], P('section', 'shard')
- up_bias_grad: float32 [2, 4096], P('section', 'shard')
- down_bias_grad: float32 [2, 1024], P('section', 'shard')
- first_gain_grad: float32 [2, 1024], P('section', 'shard')
- first_shift_grad: float32 [2, 1024], P('section', 'shard')
- second_gain_grad: float32 [2, 1024], P('section', 'shard')
- second_shift_grad: float32 [2, 1024], P('section', 'shard')
All inputs are finite; a program needn't handle non-finite values.
Results may differ from a plain program's by a relative error of at most 0.02.
Values may be sent and summed in bfloat16 or wider, within the bound.
No kernel may reach another device: no remote copies, remote signals or barrier semaphores. Data moves between devices by JAX's collectives and lax.ppermute only.
A program may use at most 192 MiB of HBM per device.

v0:
```python
import functools

import jax
import jax.numpy as jnp
from jax import lax
from jax.experimental import pallas as pl
from jax.experimental.pallas import tpu as pltpu
from jax.sharding import Mesh
from jax.sharding import PartitionSpec as P

HEADS = 16
HEAD_DIM = 64
LEN = 128
ROWS = 256
WIDTH = 1024
HIDDEN = 4096
BLOCK = 1024
SCALE = HEAD_DIM ** (-0.5)
EPSILON = 1e-06
ROOT_HALF = 0.5**0.5
NORMAL_PEAK = 0.3989422804014327
LIMIT = 48 * 1024 * 1024

VECTORS_AT = 12288
GATHERED = 12416
Z_AT, O_AT, FIRST_HALF = 2048, 2560, 3072
DOWN_AT, OUTPUT_AT, FIRST_ALL = 2048, 4096, 4608
EXTRA_AT, LAST_ALL, FAR_HALF, CUT = 1536, 1792, 896, 384

F32 = jnp.float32
BF16 = jnp.bfloat16


def dot(left, right):
    return jnp.dot(left, right, preferred_element_type=F32)


def dot_back(left, right):
    return lax.dot_general(left, right, (((1,), (1,)), ((), ())), preferred_element_type=F32)


def dot_rows(left, right):
    return lax.dot_general(left, right, (((0,), (0,)), ((), ())), preferred_element_type=F32)


def swap_cores(value):
    return lax.ppermute(value, "core", [(0, 1), (1, 0)])


def swap_far(value):
    return lax.ppermute(value, "far", [(0, 1), (1, 0)])


def mean(values):
    return jnp.mean(values, -1, keepdims=True)


def normalise(totals):
    centred = totals - mean(totals)
    inverse = lax.rsqrt(mean(centred * centred) + EPSILON)
    return centred * inverse, inverse


def norm_backward(upstream, normed, inverse, gain_row):
    scaled = upstream * gain_row
    return inverse * (scaled - mean(scaled) - normed * mean(scaled * normed))


def stacked(values):
    low = lax.broadcasted_iota(jnp.int32, values.shape, 1) < HEAD_DIM
    zeros = jnp.zeros_like(values)
    return jnp.concatenate([jnp.where(low, values, zeros), jnp.where(low, zeros, values)], 0)


def beside(values):
    low = lax.broadcasted_iota(jnp.int32, (LEN, 128), 1) < HEAD_DIM
    return jnp.where(low, values[:LEN], values[LEN:])


def soft_of(queries, keys):
    scores = dot_back(queries, keys)
    weights = jnp.exp((scores - jnp.max(scores, -1, keepdims=True)) * SCALE)
    return weights * (1.0 / jnp.sum(weights, -1, keepdims=True))


def pair_of(ref, rows, part, pair):
    at = part * WIDTH + pair * 128
    return ref[rows, at : at + 128]


def down_rows(block):
    return jnp.concatenate(
        [
            block[32 * part : 32 * part + 32, WIDTH * group : WIDTH * (group + 1)]
            for part in range(8)
            for group in range(4)
        ],
        0,
    )


def forward_kernel(keep, x_ref, column_ref, row_ref, bias_ref, pairs_ref, y_ref, p_ref, c_ref, hidden_ref, *others):
    step = pl.program_id(0)
    total_ref = others[-1]
    if keep:
        e_ref, slope_ref, n_one_ref, r_one_ref, n_two_ref, r_two_ref = others[:-1]

    @pl.when(step < 3)
    def _():
        at = pl.multiple_of(step * BLOCK, BLOCK)
        p_ref[:, pl.ds(at, BLOCK)] = (dot(x_ref[...], column_ref[...]) + bias_ref[...]).astype(BF16)

    @pl.when(step == 3)
    def _():
        for seq in range(ROWS // LEN):
            rows = slice(seq * LEN, (seq + 1) * LEN)
            softs = [
                soft_of(stacked(pair_of(p_ref, rows, 0, pair)), pair_of(p_ref, rows, 1, pair)).astype(BF16)
                for pair in range(HEADS // 2)
            ]
            for pair, soft in enumerate(softs):
                c_ref[rows, pair * 128 : (pair + 1) * 128] = beside(
                    dot(soft, pair_of(p_ref, rows, 2, pair))
                ).astype(BF16)
        normed, inverse = normalise(
            x_ref[...].astype(F32) + (dot(c_ref[...], column_ref[...]) + bias_ref[...])
        )
        hidden = normed * pairs_ref[4:5] + pairs_ref[5:6]
        hidden_ref[...] = hidden.astype(BF16)
        total_ref[...] = hidden + pairs_ref[3:4]
        if keep:
            n_one_ref[...] = normed
            r_one_ref[...] = jnp.broadcast_to(inverse, (ROWS, 128))

    @pl.when(step >= 4)
    def _():
        upper = dot(hidden_ref[...], column_ref[...]) + bias_ref[...]
        share = 0.5 * (1.0 + lax.erf(upper * ROOT_HALF))
        active = (upper * share).astype(BF16)
        if keep:
            e_ref[...] = active
            slope_ref[...] = (
                share + upper * (NORMAL_PEAK * jnp.exp(-0.5 * upper * upper))
            ).astype(BF16)
        total_ref[...] += dot(active, down_rows(row_ref[...]))

    @pl.when(step == 7)
    def _():
        normed, inverse = normalise(total_ref[...])
        y_ref[...] = (normed * pairs_ref[6:7] + pairs_ref[7:8]).astype(BF16)
        if keep:
            n_two_ref[...] = normed
            r_two_ref[...] = jnp.broadcast_to(inverse, (ROWS, 128))


def whole(shape):
    return pl.BlockSpec(shape, lambda step: (0,) * len(shape))


def shaped(*dims, kind=BF16):
    return jax.ShapeDtypeStruct(dims, kind)


def layer_forward(rows16, gathered, biases, pairs, keep):
    later = lambda step: (0, jnp.maximum(step - 4, 0))
    results = [
        (whole((ROWS, WIDTH)), shaped(ROWS, WIDTH)),
        (whole((ROWS, 3 * WIDTH)), shaped(ROWS, 3 * WIDTH)),
        (whole((ROWS, WIDTH)), shaped(ROWS, WIDTH)),
        (whole((ROWS, WIDTH)), shaped(ROWS, WIDTH)),
    ]
    scratch = [pltpu.VMEM((ROWS, WIDTH), F32)]
    if keep:
        results += [
            (pl.BlockSpec((ROWS, BLOCK), later), shaped(ROWS, HIDDEN)),
            (pl.BlockSpec((ROWS, BLOCK), later), shaped(ROWS, HIDDEN)),
            (whole((ROWS, WIDTH)), shaped(ROWS, WIDTH, kind=F32)),
            (whole((ROWS, 128)), shaped(ROWS, 128, kind=F32)),
            (whole((ROWS, WIDTH)), shaped(ROWS, WIDTH, kind=F32)),
            (whole((ROWS, 128)), shaped(ROWS, 128, kind=F32)),
        ]
    else:
        scratch = [pltpu.VMEM(shape.shape, BF16) for _, shape in results[1:]] + scratch
        results = results[:1]
    return pl.pallas_call(
        functools.partial(forward_kernel, keep),
        grid=(8,),
        in_specs=[
            whole((ROWS, WIDTH)),
            pl.BlockSpec((WIDTH, BLOCK), lambda step: (0, step)),
            pl.BlockSpec((256, HIDDEN), lambda step: (jnp.maximum(step - 4, 0), 2)),
            pl.BlockSpec((1, BLOCK), lambda step: (0, step)),
            whole((8, WIDTH)),
        ],
        out_specs=[spec for spec, _ in results],
        out_shape=[shape for _, shape in results],
        scratch_shapes=scratch,
        compiler_params=pltpu.CompilerParams(vmem_limit_bytes=LIMIT),
        cost_estimate=pl.CostEstimate(
            flops=2 * ROWS * 12 * WIDTH * WIDTH, bytes_accessed=32 << 20, transcendentals=0
        ),
        name="layer_forward",
    )(rows16, gathered, gathered, biases, pairs)


def column_sums(values):
    return jnp.sum(values, 0, keepdims=True)


def put_half(core, half, mine_ref, theirs_ref, columns, values):
    @pl.when(core == half)
    def _():
        mine_ref[:, columns] = values

    @pl.when(core != half)
    def _():
        theirs_ref[:, columns] = values


def hidden_begin(keep, core, upstream_ref, pairs_ref, n_two_ref, r_two_ref, z_ref, total_ref, kept):
    upstream = upstream_ref[...].astype(F32)
    normed = n_two_ref[...]
    grad = norm_backward(upstream, normed, r_two_ref[:, 0:1], pairs_ref[6:7])
    total_ref[...] = grad
    rounded = grad.astype(BF16)
    z_ref[...] = rounded
    if keep:
        mine_ref, theirs_ref, pair_grads_ref, _ = kept
        pair_grads_ref[6:7] = column_sums(upstream * normed)
        pair_grads_ref[7:8] = column_sums(upstream)
        pair_grads_ref[3:4] = column_sums(rounded.astype(F32))
        for half in range(2):
            put_half(
                core, half, mine_ref, theirs_ref, pl.ds(Z_AT, 512),
                rounded[:, half * 512 : half * 512 + 512],
            )


def hidden_step(keep, core, step, column_ref, row_ref, slope_ref, z_ref, total_ref, kept):
    active_grad = dot_back(z_ref[...], down_rows(row_ref[...]))
    upper_grad = (active_grad * slope_ref[...].astype(F32)).astype(BF16)
    if keep:
        mine_ref, theirs_ref, _, up_grads_ref = kept
        up_grads_ref[...] = column_sums(upper_grad.astype(F32))
        at = pl.multiple_of(lax.rem(step, 2) * BLOCK, BLOCK)
        put_half(core, step // 2, mine_ref, theirs_ref, pl.ds(at, BLOCK), upper_grad)
    total_ref[...] += dot_back(upper_grad, column_ref[...])


def hidden_end(keep, core, pairs_ref, n_one_ref, r_one_ref, total_ref, kept):
    hidden_grad = total_ref[...]
    normed = n_one_ref[...]
    grad = norm_backward(hidden_grad, normed, r_one_ref[:, 0:1], pairs_ref[4:5])
    if keep:
        mine_ref, theirs_ref, pair_grads_ref, _ = kept
        pair_grads_ref[4:5] = column_sums(hidden_grad * normed)
        pair_grads_ref[5:6] = column_sums(hidden_grad)
        rounded = grad.astype(BF16)
        pair_grads_ref[2:3] = column_sums(rounded.astype(F32))
        for half in range(2):
            put_half(
                core, half, mine_ref, theirs_ref, pl.ds(O_AT, 512),
                rounded[:, half * 512 : half * 512 + 512],
            )
    return grad


def attention_step(keep, core, grad, column_ref, p_ref, z_ref, p_grad_ref, total_ref, kept):
    rounded = grad.astype(BF16)
    z_ref[...] = dot_back(rounded, column_ref[...]).astype(BF16)
    for seq in range(ROWS // LEN):
        rows = slice(seq * LEN, (seq + 1) * LEN)
        pairs = range(HEADS // 2)
        softs = [
            soft_of(stacked(pair_of(p_ref, rows, 0, pair)), pair_of(p_ref, rows, 1, pair))
            for pair in pairs
        ]
        soft_grads = [
            dot_back(stacked(pair_of(z_ref, rows, 0, pair)), pair_of(p_ref, rows, 2, pair))
            for pair in pairs
        ]
        scores_grads = []
        for soft, soft_grad in zip(softs, soft_grads):
            weighed = soft_grad * soft
            scores_grads.append(
                (weighed - soft * jnp.sum(weighed, -1, keepdims=True)).astype(BF16)
            )
        for pair in pairs:
            grads = (
                beside(dot(scores_grads[pair], pair_of(p_ref, rows, 1, pair))) * SCALE,
                dot_rows(scores_grads[pair], stacked(pair_of(p_ref, rows, 0, pair))) * SCALE,
                dot_rows(softs[pair].astype(BF16), stacked(pair_of(z_ref, rows, 0, pair))),
            )
            for part in range(3):
                at = part * WIDTH + pair * 128
                p_grad_ref[rows, at : at + 128] = grads[part].astype(BF16)
    if keep:
        mine_ref, theirs_ref, pair_grads_ref = kept
        for half in range(2):
            put_half(
                core, half, mine_ref, theirs_ref, pl.ds(0, EXTRA_AT),
                p_grad_ref[:, half * EXTRA_AT : (half + 1) * EXTRA_AT],
            )
        pair_grads_ref[0:1] = column_sums(p_grad_ref[:, :WIDTH].astype(F32))
        pair_grads_ref[1:2] = column_sums(p_grad_ref[:, 2 * WIDTH :].astype(F32))
    total_ref[...] = grad


def project_step(step, column_ref, p_grad_ref, total_ref):
    at = pl.multiple_of(step * BLOCK, BLOCK)
    total_ref[...] += dot_back(p_grad_ref[:, pl.ds(at, BLOCK)], column_ref[...])


def through_kernel(
    upstream_ref, column_ref, row_ref, pairs_ref, p_ref, slope_ref,
    n_one_ref, r_one_ref, n_two_ref, r_two_ref, x_grad_ref, z_ref, p_grad_ref, total_ref
):
    step = pl.program_id(0)

    @pl.when(step == 0)
    def _():
        hidden_begin(False, None, upstream_ref, pairs_ref, n_two_ref, r_two_ref, z_ref, total_ref, None)

    @pl.when(step < 4)
    def _():
        hidden_step(False, None, step, column_ref, row_ref, slope_ref, z_ref, total_ref, None)

    @pl.when(step == 4)
    def _():
        grad = hidden_end(False, None, pairs_ref, n_one_ref, r_one_ref, total_ref, None)
        attention_step(False, None, grad, column_ref, p_ref, z_ref, p_grad_ref, total_ref, None)

    @pl.when(step >= 5)
    def _():
        project_step(step - 5, column_ref, p_grad_ref, total_ref)

    @pl.when(step == 7)
    def _():
        x_grad_ref[...] = total_ref[...].astype(BF16)


def cost(share):
    return pl.CostEstimate(
        flops=int(2 * ROWS * 12 * WIDTH * WIDTH * share),
        bytes_accessed=int(share * (32 << 20)),
        transcendentals=0,
    )


SMALL = pl.CostEstimate(flops=1, bytes_accessed=1, transcendentals=0)


def layer_through(upstream, gathered, pairs, kept):
    p, slope, n_one, r_one, n_two, r_two = kept
    column = lambda step: (0, jnp.where(step < 4, step + 4, jnp.where(step < 5, 3, step - 5)))
    return pl.pallas_call(
        through_kernel,
        grid=(8,),
        in_specs=[
            whole((ROWS, WIDTH)),
            pl.BlockSpec((WIDTH, BLOCK), column),
            pl.BlockSpec((256, HIDDEN), lambda step: (jnp.minimum(step, 3), 2)),
            whole((8, WIDTH)),
            whole((ROWS, 3 * WIDTH)),
            pl.BlockSpec((ROWS, BLOCK), lambda step: (0, jnp.minimum(step, 3))),
            whole((ROWS, WIDTH)),
            whole((ROWS, 128)),
            whole((ROWS, WIDTH)),
            whole((ROWS, 128)),
        ],
        out_specs=whole((ROWS, WIDTH)),
        out_shape=shaped(ROWS, WIDTH),
        scratch_shapes=[
            pltpu.VMEM((ROWS, WIDTH), BF16),
            pltpu.VMEM((ROWS, 3 * WIDTH), BF16),
            pltpu.VMEM((ROWS, WIDTH), F32),
        ],
        compiler_params=pltpu.CompilerParams(vmem_limit_bytes=LIMIT),
        cost_estimate=cost(1.0),
        name="layer_through",
    )(upstream, gathered, gathered, pairs, p, slope, n_one, r_one, n_two, r_two)


def hidden_kernel(
    core_ref, upstream_ref, column_ref, row_ref, pairs_ref, slope_ref,
    n_one_ref, r_one_ref, n_two_ref, r_two_ref,
    branch_ref, mine_ref, theirs_ref, pair_grads_ref, up_grads_ref, z_ref, total_ref
):
    step = pl.program_id(0)
    core = core_ref[0]
    kept = (mine_ref, theirs_ref, pair_grads_ref, up_grads_ref)

    @pl.when(step == 0)
    def _():
        pair_grads_ref[...] = jnp.zeros_like(pair_grads_ref)
        hidden_begin(True, core, upstream_ref, pairs_ref, n_two_ref, r_two_ref, z_ref, total_ref, kept)

    hidden_step(True, core, step, column_ref, row_ref, slope_ref, z_ref, total_ref, kept)

    @pl.when(step == 3)
    def _():
        branch_ref[...] = hidden_end(True, core, pairs_ref, n_one_ref, r_one_ref, total_ref, kept)


def hidden_backward(core, upstream, gathered, pairs, kept):
    _, slope, n_one, r_one, n_two, r_two = kept
    return pl.pallas_call(
        hidden_kernel,
        grid=(4,),
        in_specs=[
            pl.BlockSpec(memory_space=pltpu.SMEM),
            whole((ROWS, WIDTH)),
            pl.BlockSpec((WIDTH, BLOCK), lambda step: (0, step + 4)),
            pl.BlockSpec((256, HIDDEN), lambda step: (step, 2)),
            whole((8, WIDTH)),
            pl.BlockSpec((ROWS, BLOCK), lambda step: (0, step)),
            whole((ROWS, WIDTH)),
            whole((ROWS, 128)),
            whole((ROWS, WIDTH)),
            whole((ROWS, 128)),
        ],
        out_specs=[
            whole((ROWS, WIDTH)),
            whole((ROWS, FIRST_HALF)),
            whole((ROWS, FIRST_HALF)),
            whole((8, WIDTH)),
            pl.BlockSpec((1, BLOCK), lambda step: (0, step)),
        ],
        out_shape=[
            shaped(ROWS, WIDTH, kind=F32),
            shaped(ROWS, FIRST_HALF),
            shaped(ROWS, FIRST_HALF),
            shaped(8, WIDTH, kind=F32),
            shaped(1, HIDDEN, kind=F32),
        ],
        scratch_shapes=[pltpu.VMEM((ROWS, WIDTH), BF16), pltpu.VMEM((ROWS, WIDTH), F32)],
        compiler_params=pltpu.CompilerParams(vmem_limit_bytes=LIMIT),
        cost_estimate=cost(0.6),
        name="hidden_backward",
    )(core, upstream, gathered, gathered, pairs, slope, n_one, r_one, n_two, r_two)


def attention_kernel(
    core_ref, branch_ref, column_ref, p_ref,
    x_grad_ref, mine_ref, theirs_ref, pair_grads_ref, z_ref, p_grad_ref, total_ref
):
    step = pl.program_id(0)
    kept = (mine_ref, theirs_ref, pair_grads_ref)

    @pl.when(step == 0)
    def _():
        pair_grads_ref[...] = jnp.zeros_like(pair_grads_ref)
        attention_step(
            True, core_ref[0], branch_ref[...], column_ref, p_ref, z_ref, p_grad_ref, total_ref, kept
        )

    @pl.when(step >= 1)
    def _():
        project_step(step - 1, column_ref, p_grad_ref, total_ref)

    @pl.when(step == 3)
    def _():
        x_grad_ref[...] = total_ref[...].astype(BF16)


def attention_backward(core, branch, gathered, p):
    return pl.pallas_call(
        attention_kernel,
        grid=(4,),
        in_specs=[
            pl.BlockSpec(memory_space=pltpu.SMEM),
            whole((ROWS, WIDTH)),
            pl.BlockSpec((WIDTH, BLOCK), lambda step: (0, jnp.where(step < 1, 3, step - 1))),
            whole((ROWS, 3 * WIDTH)),
        ],
        out_specs=[
            whole((ROWS, WIDTH)),
            whole((ROWS, EXTRA_AT)),
            whole((ROWS, EXTRA_AT)),
            whole((8, WIDTH)),
        ],
        out_shape=[
            shaped(ROWS, WIDTH),
            shaped(ROWS, EXTRA_AT),
            shaped(ROWS, EXTRA_AT),
            shaped(8, WIDTH, kind=F32),
        ],
        scratch_shapes=[
            pltpu.VMEM((ROWS, WIDTH), BF16),
            pltpu.VMEM((ROWS, 3 * WIDTH), BF16),
            pltpu.VMEM((ROWS, WIDTH), F32),
        ],
        compiler_params=pltpu.CompilerParams(vmem_limit_bytes=LIMIT),
        cost_estimate=cost(0.5),
        name="attention_backward",
    )(core, branch, gathered, p)


def product(left_refs, right_refs, at=0, end=None):
    return (
        dot_rows(left_refs[0][...], right_refs[0][:, at:end])
        + dot_rows(left_refs[1][...], right_refs[1][:, at:end])
    ).astype(BF16)


def first_grads_kernel(h_ref, e_ref, c_ref, left_ref, h2_ref, e2_ref, c2_ref, right_ref, out_ref):
    both = (left_ref, right_ref)
    out_ref[:, :DOWN_AT] = product((h_ref, h2_ref), both, 0, Z_AT)
    down = product((e_ref, e2_ref), both, Z_AT, O_AT)
    for part in range(4):
        for group in range(4):
            at = part * 256 + group * 64
            out_ref[
                part * 64 : part * 64 + 64, DOWN_AT + group * 512 : DOWN_AT + (group + 1) * 512
            ] = down[at : at + 64]
    out_ref[:, OUTPUT_AT:] = product((c_ref, c2_ref), both, O_AT, FIRST_HALF)


NARROW = pl.BlockSpec((ROWS, 256), lambda step: (0, step))
WIDE = pl.BlockSpec((ROWS, 1024), lambda step: (0, step))


def first_grads(own, own_half, other, other_half):
    tokens = [NARROW, WIDE, NARROW, whole((ROWS, FIRST_HALF))]
    return pl.pallas_call(
        first_grads_kernel,
        grid=(4,),
        in_specs=[*tokens, *tokens],
        out_specs=pl.BlockSpec((256, FIRST_ALL), lambda step: (step, 0)),
        out_shape=shaped(WIDTH, FIRST_ALL),
        compiler_params=pltpu.CompilerParams(vmem_limit_bytes=LIMIT),
        cost_estimate=cost(0.7),
        name="first_grads",
    )(*own, own_half, *other, other_half)


def last_grads_kernel(far_ref, x_ref, left_ref, x2_ref, right_ref, extra_ref, near_out, far_out):
    both = (left_ref, right_ref)
    low = product((x_ref, x2_ref), both, 0, FAR_HALF)
    high = product((x_ref, x2_ref), both, FAR_HALF, EXTRA_AT)
    at = EXTRA_AT - FAR_HALF

    def put(low_ref, high_ref):
        low_ref[...] = low
        high_ref[:, :at] = high
        high_ref[:, at : at + 128] = extra_ref[...]
        high_ref[:, at + 128 :] = jnp.zeros((256, LAST_ALL - EXTRA_AT - 128), BF16)

    @pl.when(far_ref[0] == 0)
    def _():
        put(near_out, far_out)

    @pl.when(far_ref[0] != 0)
    def _():
        put(far_out, near_out)


def last_grads(far, own, own_half, other, other_half, extra):
    tokens = [NARROW, whole((ROWS, EXTRA_AT))]
    rows = lambda step: (step, 0)
    return pl.pallas_call(
        last_grads_kernel,
        grid=(4,),
        in_specs=[
            pl.BlockSpec(memory_space=pltpu.SMEM), *tokens, *tokens, pl.BlockSpec((256, 128), rows)
        ],
        out_specs=[pl.BlockSpec((256, FAR_HALF), rows)] * 2,
        out_shape=[shaped(WIDTH, FAR_HALF)] * 2,
        compiler_params=pltpu.CompilerParams(vmem_limit_bytes=LIMIT),
        cost_estimate=cost(0.35),
        name="last_grads",
    )(far, own, own_half, other, other_half, extra)


def split_kernel(place_ref, near_ref, far_ref, *refs):
    left_out, right_out = refs[:4], refs[4:8]
    for k in range(4):
        rows = pl.ds(pl.multiple_of(lax.rem(place_ref[0] + k, 4) * 256, 256), 256)
        left_out[k][...] = (
            near_ref[rows, :CUT].astype(F32) + far_ref[rows, :CUT].astype(F32)
        ).astype(BF16)
        for z in range(4):
            at = z * 256 + lax.rem(place_ref[1] + k, 4) * 64
            rows = pl.ds(pl.multiple_of(at, 64), 64)
            right_out[k][z] = (
                near_ref[rows, CUT:].astype(F32) + far_ref[rows, CUT:].astype(F32)
            ).astype(BF16)


def split(place, near, far):
    vmem = pl.BlockSpec(memory_space=pltpu.VMEM)
    results = pl.pallas_call(
        split_kernel,
        in_specs=[pl.BlockSpec(memory_space=pltpu.SMEM), vmem, vmem],
        out_specs=[vmem] * 8,
        out_shape=[shaped(256, CUT)] * 4 + [shaped(4, 64, FAR_HALF - CUT)] * 4,
        compiler_params=pltpu.CompilerParams(vmem_limit_bytes=LIMIT),
        cost_estimate=cost(0.1),
        name="split",
    )(place, near, far)
    return results[:4], results[4:]


def halfway_kernel(place_ref, *refs):
    lefts, rights = refs[:4], refs[4:8]
    left_out, right_out = refs[8:12], refs[12:16]
    left_ref, right_ref = refs[16:]

    def total(parts):
        return sum([part[...].astype(F32) for part in parts[1:]], parts[0][...].astype(F32)).astype(BF16)

    left_ref[...] = total(lefts)
    right_ref[...] = total(rights)
    for k in range(4):
        y = pl.multiple_of(lax.rem(place_ref[1] + k, 4) * 64, 64)
        left_out[k][...] = left_ref[pl.ds(y, 64)]
        right_out[k][...] = right_ref[lax.rem(place_ref[0] + k, 4)]


def halfway(place, lefts, rights):
    width = rights[0].shape[2]
    vmem = pl.BlockSpec(memory_space=pltpu.VMEM)
    results = pl.pallas_call(
        halfway_kernel,
        in_specs=[pl.BlockSpec(memory_space=pltpu.SMEM)] + [vmem] * 8,
        out_specs=[vmem] * 8,
        out_shape=[shaped(64, CUT)] * 4 + [shaped(64, width)] * 4,
        scratch_shapes=[pltpu.VMEM((256, CUT), BF16), pltpu.VMEM((4, 64, width), BF16)],
        compiler_params=pltpu.CompilerParams(vmem_limit_bytes=LIMIT),
        cost_estimate=cost(0.1),
        name="halfway",
    )(place, *lefts, *rights)
    return results[:4], results[4:]


def finish_kernel(
    core_ref, far_ref, first_in, first2_in, near_in, near2_in, away_in, away2_in,
    project_ref, output_ref, up_ref, down_ref
):
    def put(half, first, low, high):
        at = half * EXTRA_AT
        project_ref[:, at : at + FAR_HALF] = low[...].astype(F32)
        project_ref[:, at + FAR_HALF : at + EXTRA_AT] = high[:, : EXTRA_AT - FAR_HALF].astype(F32)
        output_ref[:, half * 512 : (half + 1) * 512] = first[:, OUTPUT_AT:]
        up_ref[:, half * 2048 : (half + 1) * 2048] = first[:, :DOWN_AT]
        for group in range(4):
            at = DOWN_AT + group * 512
            down_ref[group * 64 : group * 64 + 64, half * 512 : (half + 1) * 512] = first[
                :, at : at + 512
            ]

    for core in range(2):
        for far in range(2):

            @pl.when((core_ref[0] == core) & (far_ref[0] == far))
            def _():
                for half, first, near, away in (
                    (core, first_in, near_in, away_in),
                    (1 - core, first2_in, near2_in, away2_in),
                ):
                    put(half, first, *((near, away) if far == 0 else (away, near)))


def finish(core, far, *totals):
    vmem = pl.BlockSpec(memory_space=pltpu.VMEM)
    smem = pl.BlockSpec(memory_space=pltpu.SMEM)
    return pl.pallas_call(
        finish_kernel,
        in_specs=[smem, smem] + [vmem] * 6,
        out_specs=[vmem] * 4,
        out_shape=[
            shaped(64, 3 * WIDTH, kind=F32),
            shaped(64, WIDTH, kind=F32),
            shaped(64, HIDDEN, kind=F32),
            shaped(256, WIDTH, kind=F32),
        ],
        compiler_params=pltpu.CompilerParams(vmem_limit_bytes=LIMIT),
        name="finish",
    )(core, far, *totals)


def gather_weights(project, output, upward, downward, vectors):
    core = lax.axis_index("core")
    half = lax.dynamic_slice_in_dim(
        jnp.concatenate([project, output, upward], 1), core * 32, 32, 0
    )
    down = lax.dynamic_slice_in_dim(downward, core * 128, 128, 0)
    down = down.reshape(4, 32, WIDTH).transpose(1, 0, 2).reshape(32, HIDDEN)
    flat = jnp.concatenate(vectors).reshape(6, 128)
    extra = jnp.concatenate([flat, jnp.zeros((26, 128), BF16)], 0)
    packed = jnp.concatenate([half, down, extra], 1)
    gathered = lax.all_gather(packed, ("z", "y", "core"), axis=0, tiled=True)
    rows = gathered[:, VECTORS_AT:].reshape(16, 64, 128)[:, :6].astype(F32)
    pairs = rows[:, :4].reshape(16, 8, 64).transpose(1, 0, 2).reshape(8, WIDTH)
    ups = rows[:, 4:].reshape(1, HIDDEN)
    biases = jnp.concatenate(
        [pairs[0:1], jnp.zeros((1, WIDTH), F32), pairs[1:2], pairs[2:3], ups], 1
    )
    return gathered, biases, pairs


def send_around(blocks, axis):
    return [blocks[0]] + [
        lax.ppermute(blocks[k], axis, [(i, (i + k) % 4) for i in range(4)]) for k in (1, 2, 3)
    ]


def after_kernel(value_ref, earlier_ref, out_ref):
    pass


def after(value, earlier):
    memory = pl.BlockSpec(memory_space=pl.ANY)
    return pl.pallas_call(
        after_kernel,
        in_specs=[memory, memory],
        out_specs=memory,
        out_shape=jax.ShapeDtypeStruct(value.shape, value.dtype),
        input_output_aliases={0: 0},
        cost_estimate=SMALL,
        name="after",
    )(value, earlier)


def scatter_direct(place, lefts, rights):
    lefts, rights = halfway(place, send_around(lefts, "z"), send_around(rights, "y"))
    middle = lefts[0]

    def total(parts):
        return sum(part.astype(F32) for part in parts).astype(BF16)

    owned = jnp.concatenate([total(send_around(lefts, "y")), total(send_around(rights, "z"))], 1)
    return lax.optimization_barrier(owned), middle


def over_replicas(owned, earlier):
    owned = lax.optimization_barrier(owned)
    total = owned.astype(F32) + after(swap_far(owned), earlier).astype(F32)
    total = lax.optimization_barrier(total)
    return total, swap_cores(total)


def gradients(core, own, other, upstream, gathered, pairs, kept):
    rows16, c, hidden, e = own
    rows16_2, c_2, hidden_2, e_2 = other
    place = jnp.stack([lax.axis_index("z"), lax.axis_index("y")]).astype(jnp.int32)
    far = lax.axis_index("far").astype(jnp.int32).reshape(1)
    branch, mine, theirs, pair_grads, up_grads = hidden_backward(
        core, upstream, gathered, pairs, kept
    )
    packed = first_grads((hidden, e, c), mine, (hidden_2, e_2, c_2), swap_cores(theirs))
    owned = lax.psum_scatter(packed, ("z", "y"), scatter_dimension=0, tiled=True)

    rows_grad, mine, theirs, more_grads = attention_backward(core, branch, gathered, kept[0])
    pair_grads = pair_grads + more_grads
    rows = jnp.concatenate(
        [
            pair_grads.reshape(8, 16, 64).transpose(1, 0, 2).reshape(16, 4, 128),
            up_grads.reshape(16, 2, 128),
        ],
        1,
    ).astype(BF16)
    extra = jnp.concatenate([rows, jnp.zeros((16, 58, 128), BF16)], 1).reshape(WIDTH, 128)
    near_part, far_part = last_grads(far, rows16, mine, rows16_2, swap_cores(theirs), extra)
    near, middle = scatter_direct(place, *split(place, near_part, swap_far(far_part)))
    away = swap_far(near)
    near2, away2 = swap_cores(near), swap_cores(away)
    first, first2 = over_replicas(after(owned, middle), away)
    project, output, upward, downward = finish(
        core, far, first, first2, near, near2, away, away2
    )
    at = EXTRA_AT - FAR_HALF
    sums = [
        (one[:6, at : at + 128].astype(F32) + two[:6, at : at + 128].astype(F32))
        for one, two in ((near, near2), (away, away2))
    ]
    vectors = jnp.where(far[0] == 1, *sums).reshape(768)
    narrow = [vectors[64 * k : 64 * (k + 1)][None] for k in range(8)]
    query, value, output_b, down_b, gain_one, shift_one, gain_two, shift_two = narrow
    return rows_grad, (
        project[None],
        output[None],
        upward[None],
        downward[None],
        query,
        value,
        output_b,
        vectors[512:768][None],
        down_b,
        gain_one,
        shift_one,
        gain_two,
        shift_two,
    )


def on_device(
    layer_input,
    cotangent,
    project_weight,
    output_weight,
    up_weight,
    down_weight,
    query_bias,
    value_bias,
    output_bias,
    up_bias,
    down_bias,
    first_gain,
    first_shift,
    second_gain,
    second_shift,
):
    first_section = lax.axis_index("section") == 0
    gathered, biases, pairs = gather_weights(
        project_weight[0],
        output_weight[0],
        up_weight[0],
        down_weight[0],
        (
            query_bias[0],
            value_bias[0],
            output_bias[0],
            down_bias[0],
            first_gain[0],
            first_shift[0],
            second_gain[0],
            second_shift[0],
            up_bias[0],
        ),
    )
    shape = layer_input.shape
    own_rows = layer_input.reshape(-1, WIDTH)
    own_grad = cotangent.reshape(-1, WIDTH)

    early = layer_forward(own_rows, gathered, biases, pairs, False)[0]
    received = lax.ppermute(early, "section", [(0, 1)])
    rows16 = jnp.where(first_section, own_rows, received)
    result, p, c, hidden, e, slope, n_one, r_one, n_two, r_two = layer_forward(
        rows16, gathered, biases, pairs, True
    )
    kept = (p, slope, n_one, r_one, n_two, r_two)
    own = (rows16, c, hidden, e)
    other = tuple(swap_cores(array) for array in own)

    early_grad = layer_through(own_grad, gathered, pairs, kept)
    back = lax.ppermute(early_grad, "section", [(1, 0)])
    upstream = jnp.where(first_section, back, own_grad)
    core = lax.axis_index("core").astype(jnp.int32).reshape(1)
    rows_grad, grads = gradients(core, own, other, upstream, gathered, pairs, kept)
    return (result.reshape(1, *shape), rows_grad.reshape(1, *shape), *grads)


def solution(mesh):
    devices = mesh.devices.reshape(2, 2, 2, 4, 4)
    fine = Mesh(devices, ("section", "far", "core", "z", "y"))
    shard = ("z", "y")
    seqs = P(None, ("far", "core", "z", "y"), None, None)
    matrix = P("section", shard, None)
    vector = P("section", shard)
    rows = P("section", None, ("far", "core", "z", "y"), None, None)
    return jax.shard_map(
        on_device,
        mesh=fine,
        in_specs=(seqs, seqs, *([matrix] * 4), *([vector] * 9)),
        out_specs=(rows, rows, *([matrix] * 4), *([vector] * 9)),
        check_vma=False,
    )
```

profile of v0, /device:TPU:1, one launch (start us, length us, event | category | flops | bytes accessed | tf_op | source)
XLA Modules:
  0.0 354.3 jit_solution(375033868386251719)
XLA Ops:
  7.3 0.9 copy-done
  8.3 0.7 reduce
  9.0 1.1 fusion.3
  10.2 0.1 concatenate.26
  10.3 0.9 fusion.1
  11.3 96.6 %all-gather.2.cloned.1.call-done.column_ref.row_ref = bf16[1024,12416]{1,0:T(8,128)(2,1)} async-done(((bf16[32,12416]{1,0:T(8,128)(2,1)}), bf16[1024,12416]{1,0:T(8,128)(2,1)}) %all-gather.2.cloned.1.call-update) | async-done | bytes 25427984 | tf_op jit(solution)/shard_map/all_gather | solution.py:692
  107.9 1.0 slice.93
  109.4 15.8 %layer_forward.2 = bf16[256,1024]{1,0:T(8,128)(2,1)S(1)} custom-call(bf16[256,1024]{1,0:T(8,128)(2,1)S(1)} %bitcast.61, bf16[1024,12416]{1,0:T(8,128)(2,1)} %all-gather.2.cloned.1.call-done.column_ref.row_ref, bf16[1024,12416]{1,0:T(8,128)(2,1)} %all-gather.2.cloned.1.call-done.column_ref.row_ref, f32[1,8192]{1,0:T(1,128)S(1)} %constant_dynamic-update-slice_fusion.bias_ref, ...), custom_call_target="tpu_custom_call" | custom-call | flops 6442450944 | bytes 33554432 | tf_op jit(solution)/shard_map/layer_forward/pallas_call | solution.py:185
  125.2 3.3 collective-permute-start
  128.5 10.8 %collective-permute-done = bf16[256,1024]{1,0:T(8,128)(2,1)S(1)} collective-permute-done((bf16[256,1024]{1,0:T(8,128)(2,1)S(1)}, bf16[256,1024]{1,0:T(8,128)(2,1)S(1)}, u32[]{:S(2)}, u32[]{:S(2)}) %collective-permute-start) | collective-permute-done | bytes 524320 | tf_op jit(solution)/shard_map/ppermute | solution.py:837
  139.5 17.8 %layer_forward.3 = (bf16[256,1024]{1,0:T(8,128)(2,1)}, bf16[256,3072]{1,0:T(8,128)(2,1)S(1)}, bf16[256,1024]{1,0:T(8,128)(2,1)S(1)}, bf16[256,1024]{1,0:T(8,128)...) custom-call(bf16[256,1024]{1,0:T(8,128)(2,1)S(1)} %broadcast_select_, ...), custom_call_target="tpu_custom_call" | custom-call | flops 6442450944 | bytes 33554432 | tf_op jit(solution)/shard_map/layer_forward/pallas_call | solution.py:185
  157.3 17.2 %layer_through.1 = bf16[256,1024]{1,0:T(8,128)(2,1)S(1)} custom-call(bf16[256,1024]{1,0:T(8,128)(2,1)S(1)} %bitcast.62, bf16[1024,12416]{1,0:T(8,128)(2,1)} %all-gather.2.cloned.1.call-done.column_ref.row_ref, bf16[1024,12416]{1,0:T(8,128)(2,1)} %all-gather.2.cloned.1.call-done.column_ref.row_ref, f32[8,1024]{1,0:T(8,128)S(1)} %reshape.101.pairs_ref, ...), custom_call_target="tpu_custom_call" | custom-call | flops 6442450944 | bytes 33554432 | tf_op jit(solution)/shard_map/layer_through/pallas_call | solution.py:356
  174.5 1.3 collective-permute-start.1
  175.8 1.4 collective-permute-start.3
  177.2 11.8 %collective-permute-done.1 = bf16[256,1024]{1,0:T(8,128)(2,1)S(1)} collective-permute-done((bf16[256,1024]{1,0:T(8,128)(2,1)S(1)}, bf16[256,1024]{1,0:T(8,128)(2,1)S(1)}, u32[]{:S(2)}, u32[]{:S(2)}) %collective-permute-start.1) | collective-permute-done | bytes 524320 | tf_op jit(solution)/shard_map/ppermute | solution.py:847
  189.1 12.3 %hidden_backward.1 = (f32[256,1024]{1,0:T(8,128)S(1)}, bf16[256,3072]{1,0:T(8,128)(2,1)S(1)}, bf16[256,3072]{1,0:T(8,128)(2,1)}, f32[8,1024]{1,0:T(8,128)S(1)}, f32[1,4096]{1,0:T(1,128)S(1)}) custom-call(s32[1]{0:T(128)} %bitcast.20.core_ref, bf16[256,1024]{1,0:T(8,128)(2,1)S(1)} %broadcast_select_fusion.upstream_ref, ...), custom_call_target="tpu_custom_call" | custom-call | flops 3865470464 | bytes 20132660 | tf_op jit(solution)/shard_map/hidden_backward/pallas_call | solution.py:407
  201.4 1.8 collective-permute-start.5
  203.3 0.5 collective-permute-start.4
  203.8 3.1 collective-permute-done.2.h2_ref
  206.9 0.7 collective-permute-done.4.c2_ref
  207.7 0.3 collective-permute-done.5.right_ref
  208.0 1.3 copy-done.13
  209.3 9.0 %first_grads.1 = bf16[1024,4608]{1,0:T(8,128)(2,1)} custom-call(bf16[256,1024]{1,0:T(8,128)(2,1)S(1)} %get-tuple-element.65.h_ref, bf16[256,4096]{1,0:T(8,128)(2,1)} %get-tuple-element.66.e_ref, bf16[256,1024]{1,0:T(8,128)(2,1)S(1)} %get-tuple-element.67.c_ref, bf16[256,3072]{1,0:T(8,128)(2,1)S(1)} %get-tuple-element.68.left_ref, ...), custom_call_target="tpu_custom_call" | custom-call | flops 4509715456 | bytes 23488102 | tf_op jit(solution)/shard_map/first_grads/pallas_call | solution.py:525
  218.4 10.5 %attention_backward.1 = (bf16[256,1024]{1,0:T(8,128)(2,1)}, bf16[256,1536]{1,0:T(8,128)(2,1)S(1)}, bf16[256,1536]{1,0:T(8,128)(2,1)}, f32[8,1024]{1,0:T(8,128)S(1)}) custom-call(s32[1]{0:T(128)} %bitcast.20.core_ref, f32[256,1024]{1,0:T(8,128)S(1)} %get-tuple-element.63.branch_ref, bf16[1024,12416]{1,0:T(8,128)(2,1)} %all-gather.2.cloned.1.call-done.column_ref.row_ref, ...), custom_call_target="tpu_custom_call" | custom-call | flops 3221225472 | bytes 16777216 | tf_op jit(solution)/shard_map/attention_backward/pallas_call | solution.py:467
  228.9 0.9 copy-done.9
  229.8 0.3 collective-permute-start.7
  230.1 0.2 collective-permute-start.6
  230.3 0.1 reshape.107
  230.6 2.2 collective-permute-done.6.x2_ref
  232.8 1.1 copy-done.10
  234.0 4.0 %last_grads.1 = (bf16[1024,896]{1,0:T(8,128)(2,1)S(1)}, bf16[1024,896]{1,0:T(8,128)(2,1)}) custom-call(s32[1]{0:T(128)} %bitcast.24.far_ref, bf16[256,1024]{1,0:T(8,128)(2,1)S(1)} %broadcast_select_fusion.1.x_ref, bf16[256,1536]{1,0:T(8,128)(2,1)S(1)} %copy-done.10, bf16[256,1024]{1,0:T(8,128)(2,1)S(1)} %collective-permute-done.6.x2_ref, ...), custom_call_target="tpu_custom_call" | custom-call | flops 2254857728 | bytes 11744051 | tf_op jit(solution)/shard_map/last_grads/pallas_call | solution.py:561
  238.0 1.2 copy-done.4
  239.2 2.6 collective-permute-start.8
  241.9 40.5 %collective-permute-done.8.far_ref = bf16[1024,896]{1,0:T(8,128)(2,1)S(1)} collective-permute-done((bf16[1024,896]{1,0:T(8,128)(2,1)}, bf16[1024,896]{1,0:T(8,128)(2,1)S(1)}, u32[]{:S(2)}, u32[]{:S(2)}) %collective-permute-start.8) | collective-permute-done | bytes 1835040 | tf_op jit(solution)/shard_map/ppermute | solution.py:51
  282.5 1.5 copy-done.5
  284.0 1.0 split.1
  284.9 2.1 collective-permute-start.10
  287.1 2.4 collective-permute-start.13
  289.5 1.2 collective-permute-start.14
  290.7 1.1 collective-permute-start.11
  291.7 1.9 collective-permute-done.10.refs_2_
  293.7 7.6 %collective-permute-done.11.refs_3_ = bf16[256,384]{1,0:T(8,128)(2,1)S(1)} collective-permute-done((bf16[256,384]{1,0:T(8,128)(2,1)S(1)}, bf16[256,384]{1,0:T(8,128)(2,1)S(1)}, u32[]{:S(2)}, u32[]{:S(2)}) %collective-permute-start.11) | collective-permute-done | bytes 196640 | tf_op jit(solution)/shard_map/ppermute | solution.py:704
  301.2 0.6 collective-permute-done.9.refs_1_
  301.9 7.0 %collective-permute-done.13.refs_6_ = bf16[4,64,512]{2,1,0:T(8,128)(2,1)S(1)} collective-permute-done((bf16[4,64,512]{2,1,0:T(8,128)(2,1)S(1)}, bf16[4,64,512]{2,1,0:T(8,128)(2,1)S(1)}, u32[]{:S(2)}, u32[]{:S(2)}) %collective-permute-start.13) | collective-permute-done | bytes 262176 | tf_op jit(solution)/shard_map/ppermute | solution.py:704
  308.9 1.0 halfway.1
  309.9 0.6 copy-done.8
  310.5 3.8 %collective-permute-start.17 = (bf16[64,384]{1,0:T(8,128)(2,1)S(1)}, bf16[64,384]{1,0:T(8,128)(2,1)S(1)}, u32[]{:S(2)}, u32[]{:S(2)}) collective-permute-start(bf16[64,384]{1,0:T(8,128)(2,1)S(1)} %get-tuple-element.87), channel_id=1, source_target_pairs={{0,2},{1,3},{2,0},{3,1},{4,6},{5,7},{6,4},{7,5},{8,10},{9,11},{10,... | collective-permute-start | bytes 147464 | tf_op jit(solution)/shard_map/ppermute | solution.py:704
  314.4 2.1 collective-permute-start.18
  316.4 0.2 collective-permute-start.20
  316.7 2.5 collective-permute-start.21
  319.2 2.5 collective-permute-start.15
  321.7 0.8 add_convert_fusion.1
  322.6 2.0 collective-permute-start.22
  324.6 9.7 %collective-permute-done.22.earlier_ref.away_in = bf16[64,896]{1,0:T(8,128)(2,1)S(1)} collective-permute-done((bf16[64,896]{1,0:T(8,128)(2,1)S(1)}, bf16[64,896]{1,0:T(8,128)(2,1)S(1)}, u32[]{:S(2)}, u32[]{:S(2)}) %collective-permute-start.22) | collective-permute-done | bytes 114720 | tf_op jit(solution)/shard_map/ppermute | solution.py:51
  334.3 0.6 copy-done.6
  335.0 1.2 convert_add_fusion.first_in
  336.2 4.9 %collective-permute-start.23 = (f32[64,4608]{1,0:T(8,128)S(1)}, f32[64,4608]{1,0:T(8,128)S(1)}, u32[]{:S(2)}, u32[]{:S(2)}) collective-permute-start(f32[64,4608]{1,0:T(8,128)S(1)} %convert_add_fusion.first_in), channel_id=1, source_target_pairs={{0,16},{16,0},{1,17},{17,1},{2,18},{18,2},{3,19},{19,3},{4,20},{20... | collective-permute-start | bytes 3538952 | tf_op jit(solution)/shard_map/ppermute | solution.py:47
  341.1 0.1 collective-permute-start.24
  341.2 0.4 collective-permute-start.25
  341.6 2.1 collective-permute-done.24.near2_in
  343.7 0.2 collective-permute-done.25.away2_in
  343.9 0.6 slice.87
  344.5 0.6 slice_bitcast_fusion
  345.1 1.9 finish.1
  (88 shorter events, 1.3 us)
Async XLA Ops:
  7.2 1.1 copy-start
  7.2 2.9 copy-start.18
  7.2 2.9 copy-start.19
  7.2 2.9 copy-start.20
  7.2 2.9 copy-start.21
  7.2 2.9 copy-start.14
  7.3 2.9 copy-start.15
  7.3 2.9 copy-start.16
  7.3 2.9 copy-start.17
  7.3 100.6 %all-gather.2.cloned.1.call-start = ((), (), s32[]{:S(2)}) async-start(), calls=%async_computation.1 | async-start | bytes 26222592 | tf_op jit(solution)/shard_map/all_gather | solution.py:692
  10.3 99.1 %copy-start.2 = (bf16[2,1,128,1024]{3,2,1,0:T(8,128)(2,1)S(1)}, bf16[2,1,128,1024]{3,2,1,0:T(8,128)(2,1)}, u32[]{:S(2)}) copy-start(bf16[2,1,128,1024]{3,2,1,0:T(8,128)(2,1)} %param.15) | copy-start | bytes 1572868
  11.2 305.4 %reduce-scatter.2.cloned.1.call-start = ((), (), s32[]{:S(2)}) async-start(), calls=%async_computation.2 | async-start | bytes 10027008 | tf_op jit(solution)/shard_map/reduce_scatter | solution.py:752
  125.2 14.2 %collective-permute-start = (bf16[256,1024]{1,0:T(8,128)(2,1)S(1)}, bf16[256,1024]{1,0:T(8,128)(2,1)S(1)}, u32[]{:S(2)}, u32[]{:S(2)}) collective-permute-start(bf16[256,1024]{1,0:T(8,128)(2,1)S(1)} %layer_forward.2), channel_id=1, source_target_pairs={{0,64},{1,65},{2,66},{3,67},{4,68},{5,69},{6,70},{7,71},{8,72},{9,... | collective-permute-start | bytes 1572872 | tf_op jit(solution)/shard_map/ppermute | solution.py:837
  139.5 17.8 %copy-start.3 = (bf16[2,1,128,1024]{3,2,1,0:T(8,128)(2,1)S(1)}, bf16[2,1,128,1024]{3,2,1,0:T(8,128)(2,1)}, u32[]{:S(2)}) copy-start(bf16[2,1,128,1024]{3,2,1,0:T(8,128)(2,1)} %param.16) | copy-start | bytes 1572868
  157.3 18.5 %copy-start.12 = (bf16[256,4096]{1,0:T(8,128)(2,1)S(1)}, bf16[256,4096]{1,0:T(8,128)(2,1)}, u32[]{:S(2)}) copy-start(bf16[256,4096]{1,0:T(8,128)(2,1)} %get-tuple-element.66.e_ref) | copy-start | bytes 6291460
  174.5 14.5 %collective-permute-start.1 = (bf16[256,1024]{1,0:T(8,128)(2,1)S(1)}, bf16[256,1024]{1,0:T(8,128)(2,1)S(1)}, u32[]{:S(2)}, u32[]{:S(2)}) collective-permute-start(bf16[256,1024]{1,0:T(8,128)(2,1)S(1)} %layer_through.1), channel_id=1, source_target_pairs={{64,0},{65,1},{66,2},{67,3},{68,4},{69,5},{70,6},{71,7},{72,8},{73... | collective-permute-start | bytes 1572872 | tf_op jit(solution)/shard_map/ppermute | solution.py:847
  175.8 32.2 %collective-permute-start.3 = (bf16[256,4096]{1,0:T(8,128)(2,1)S(1)}, bf16[256,4096]{1,0:T(8,128)(2,1)S(1)}, u32[]{:S(2)}, u32[]{:S(2)}) collective-permute-start(bf16[256,4096]{1,0:T(8,128)(2,1)S(1)} %copy-done.12), channel_id=1, source_target_pairs={{0,16},{16,0},{1,17},{17,1},{2,18},{18,2},{3,19},{19,3},{4,20},{20... | collective-permute-start | bytes 6291464 | tf_op jit(solution)/shard_map/ppermute | solution.py:47
  201.4 6.6 %collective-permute-start.5 = (bf16[256,3072]{1,0:T(8,128)(2,1)}, bf16[256,3072]{1,0:T(8,128)(2,1)S(1)}, u32[]{:S(2)}, u32[]{:S(2)}) collective-permute-start(bf16[256,3072]{1,0:T(8,128)(2,1)} %get-tuple-element.69), channel_id=1, source_target_pairs={{0,16},{16,0},{1,17},{17,1},{2,18},{18,2},{3,19},{19,3},{4,20},{20... | collective-permute-start | bytes 4718600 | tf_op jit(solution)/shard_map/ppermute | solution.py:47
  203.3 3.7 %collective-permute-start.2 = (bf16[256,1024]{1,0:T(8,128)(2,1)S(1)}, bf16[256,1024]{1,0:T(8,128)(2,1)S(1)}, u32[]{:S(2)}, u32[]{:S(2)}) collective-permute-start(bf16[256,1024]{1,0:T(8,128)(2,1)S(1)} %get-tuple-element.65.h_ref), channel_id=1, source_target_pairs={{0,16},{16,0},{1,17},{17,1},{2,18},{18,2},{3,19},{19,3},{4,20},{20... | collective-permute-start | bytes 1572872 | tf_op jit(solution)/shard_map/ppermute | solution.py:47
  203.3 4.4 %collective-permute-start.4 = (bf16[256,1024]{1,0:T(8,128)(2,1)S(1)}, bf16[256,1024]{1,0:T(8,128)(2,1)S(1)}, u32[]{:S(2)}, u32[]{:S(2)}) collective-permute-start(bf16[256,1024]{1,0:T(8,128)(2,1)S(1)} %get-tuple-element.67.c_ref), channel_id=1, source_target_pairs={{0,16},{16,0},{1,17},{17,1},{2,18},{18,2},{3,19},{19,3},{4,20},{20... | collective-permute-start | bytes 1572872 | tf_op jit(solution)/shard_map/ppermute | solution.py:47
  208.0 1.3 copy-start.13
  228.9 0.9 copy-start.9
  229.8 3.0 collective-permute-start.7
  230.1 2.7 collective-permute-start.6
  232.8 1.2 copy-start.10
  238.0 1.2 copy-start.4
  239.2 43.2 %collective-permute-start.8 = (bf16[1024,896]{1,0:T(8,128)(2,1)}, bf16[1024,896]{1,0:T(8,128)(2,1)S(1)}, u32[]{:S(2)}, u32[]{:S(2)}) collective-permute-start(bf16[1024,896]{1,0:T(8,128)(2,1)} %get-tuple-element.76), channel_id=1, source_target_pairs={{0,32},{32,0},{1,33},{33,1},{2,34},{34,2},{3,35},{35,3},{4,36},{36... | collective-permute-start | bytes 5505032 | tf_op jit(solution)/shard_map/ppermute | solution.py:51
  282.5 1.5 copy-start.5
  284.9 8.7 %collective-permute-start.10 = (bf16[256,384]{1,0:T(8,128)(2,1)S(1)}, bf16[256,384]{1,0:T(8,128)(2,1)S(1)}, u32[]{:S(2)}, u32[]{:S(2)}) collective-permute-start(bf16[256,384]{1,0:T(8,128)(2,1)S(1)} %get-tuple-element.79), channel_id=1, source_target_pairs={{0,8},{4,12},{8,0},{12,4},{1,9},{5,13},{9,1},{13,5},{2,10},{6,14},... | collective-permute-start | bytes 589832 | tf_op jit(solution)/shard_map/ppermute | solution.py:704
  287.1 14.8 %collective-permute-start.12 = (bf16[4,64,512]{2,1,0:T(8,128)(2,1)S(1)}, bf16[4,64,512]{2,1,0:T(8,128)(2,1)S(1)}, u32[]{:S(2)}, u32[]{:S(2)}) collective-permute-start(bf16[4,64,512]{2,1,0:T(8,128)(2,1)S(1)} %get-tuple-element.82), channel_id=1, source_target_pairs={{0,1},{1,2},{2,3},{3,0},{4,5},{5,6},{6,7},{7,4},{8,9},{9,10},{10,1... | collective-permute-start | bytes 786440 | tf_op jit(solution)/shard_map/ppermute | solution.py:704
  287.1 21.8 %collective-permute-start.13 = (bf16[4,64,512]{2,1,0:T(8,128)(2,1)S(1)}, bf16[4,64,512]{2,1,0:T(8,128)(2,1)S(1)}, u32[]{:S(2)}, u32[]{:S(2)}) collective-permute-start(bf16[4,64,512]{2,1,0:T(8,128)(2,1)S(1)} %get-tuple-element.83), channel_id=1, source_target_pairs={{0,2},{1,3},{2,0},{3,1},{4,6},{5,7},{6,4},{7,5},{8,10},{9,11},{10,... | collective-permute-start | bytes 786440 | tf_op jit(solution)/shard_map/ppermute | solution.py:704
  289.5 19.4 %collective-permute-start.14 = (bf16[4,64,512]{2,1,0:T(8,128)(2,1)S(1)}, bf16[4,64,512]{2,1,0:T(8,128)(2,1)S(1)}, u32[]{:S(2)}, u32[]{:S(2)}) collective-permute-start(bf16[4,64,512]{2,1,0:T(8,128)(2,1)S(1)} %get-tuple-element.84), channel_id=1, source_target_pairs={{0,3},{1,0},{2,1},{3,2},{4,7},{5,4},{6,5},{7,6},{8,11},{9,8},{10,9... | collective-permute-start | bytes 786440 | tf_op jit(solution)/shard_map/ppermute | solution.py:704
  290.7 10.6 %collective-permute-start.11 = (bf16[256,384]{1,0:T(8,128)(2,1)S(1)}, bf16[256,384]{1,0:T(8,128)(2,1)S(1)}, u32[]{:S(2)}, u32[]{:S(2)}) collective-permute-start(bf16[256,384]{1,0:T(8,128)(2,1)S(1)} %get-tuple-element.80), channel_id=1, source_target_pairs={{0,12},{4,0},{8,4},{12,8},{1,13},{5,1},{9,5},{13,9},{2,14},{6,2},{... | collective-permute-start | bytes 589832 | tf_op jit(solution)/shard_map/ppermute | solution.py:704
  293.7 8.2 %collective-permute-start.9 = (bf16[256,384]{1,0:T(8,128)(2,1)S(1)}, bf16[256,384]{1,0:T(8,128)(2,1)S(1)}, u32[]{:S(2)}, u32[]{:S(2)}) collective-permute-start(bf16[256,384]{1,0:T(8,128)(2,1)S(1)} %get-tuple-element.78), channel_id=1, source_target_pairs={{0,4},{4,8},{8,12},{12,0},{1,5},{5,9},{9,13},{13,1},{2,6},{6,10},{... | collective-permute-start | bytes 589832 | tf_op jit(solution)/shard_map/ppermute | solution.py:704
  309.9 0.6 copy-start.8
  310.5 6.1 %collective-permute-start.16 = (bf16[64,384]{1,0:T(8,128)(2,1)S(1)}, bf16[64,384]{1,0:T(8,128)(2,1)S(1)}, u32[]{:S(2)}, u32[]{:S(2)}) collective-permute-start(bf16[64,384]{1,0:T(8,128)(2,1)S(1)} %get-tuple-element.86), channel_id=1, source_target_pairs={{0,1},{1,2},{2,3},{3,0},{4,5},{5,6},{6,7},{7,4},{8,9},{9,10},{10,1... | collective-permute-start | bytes 147464 | tf_op jit(solution)/shard_map/ppermute | solution.py:704
  310.5 8.6 %collective-permute-start.17 = (bf16[64,384]{1,0:T(8,128)(2,1)S(1)}, bf16[64,384]{1,0:T(8,128)(2,1)S(1)}, u32[]{:S(2)}, u32[]{:S(2)}) collective-permute-start(bf16[64,384]{1,0:T(8,128)(2,1)S(1)} %get-tuple-element.87), channel_id=1, source_target_pairs={{0,2},{1,3},{2,0},{3,1},{4,6},{5,7},{6,4},{7,5},{8,10},{9,11},{10,... | collective-permute-start | bytes 147464 | tf_op jit(solution)/shard_map/ppermute | solution.py:704
  314.4 7.3 %collective-permute-start.18 = (bf16[64,384]{1,0:T(8,128)(2,1)S(1)}, bf16[64,384]{1,0:T(8,128)(2,1)S(1)}, u32[]{:S(2)}, u32[]{:S(2)}) collective-permute-start(bf16[64,384]{1,0:T(8,128)(2,1)S(1)} %get-tuple-element.88), channel_id=1, source_target_pairs={{0,3},{1,0},{2,1},{3,2},{4,7},{5,4},{6,5},{7,6},{8,11},{9,8},{10,9... | collective-permute-start | bytes 147464 | tf_op jit(solution)/shard_map/ppermute | solution.py:704
  316.4 6.1 %collective-permute-start.19 = (bf16[64,512]{1,0:T(8,128)(2,1)S(1)}, bf16[64,512]{1,0:T(8,128)(2,1)S(1)}, u32[]{:S(2)}, u32[]{:S(2)}) collective-permute-start(bf16[64,512]{1,0:T(8,128)(2,1)S(1)} %get-tuple-element.90), channel_id=1, source_target_pairs={{0,4},{4,8},{8,12},{12,0},{1,5},{5,9},{9,13},{13,1},{2,6},{6,10},{... | collective-permute-start | bytes 196616 | tf_op jit(solution)/shard_map/ppermute | solution.py:704
  316.4 6.1 %collective-permute-start.20 = (bf16[64,512]{1,0:T(8,128)(2,1)S(1)}, bf16[64,512]{1,0:T(8,128)(2,1)S(1)}, u32[]{:S(2)}, u32[]{:S(2)}) collective-permute-start(bf16[64,512]{1,0:T(8,128)(2,1)S(1)} %get-tuple-element.91), channel_id=1, source_target_pairs={{0,8},{4,12},{8,0},{12,4},{1,9},{5,13},{9,1},{13,5},{2,10},{6,14},... | collective-permute-start | bytes 196616 | tf_op jit(solution)/shard_map/ppermute | solution.py:704
  316.6 18.3 %copy-start.11 = (bf16[64,4608]{1,0:T(8,128)(2,1)S(1)}, bf16[64,4608]{1,0:T(8,128)(2,1)}, u32[]{:S(2)}) copy-start(bf16[64,4608]{1,0:T(8,128)(2,1)} %after.2) | copy-start | bytes 1769476
  316.7 5.8 %collective-permute-start.21 = (bf16[64,512]{1,0:T(8,128)(2,1)S(1)}, bf16[64,512]{1,0:T(8,128)(2,1)S(1)}, u32[]{:S(2)}, u32[]{:S(2)}) collective-permute-start(bf16[64,512]{1,0:T(8,128)(2,1)S(1)} %get-tuple-element.92), channel_id=1, source_target_pairs={{0,12},{4,0},{8,4},{12,8},{1,13},{5,1},{9,5},{13,9},{2,14},{6,2},{... | collective-permute-start | bytes 196616 | tf_op jit(solution)/shard_map/ppermute | solution.py:704
  319.2 15.1 %collective-permute-start.15 = (bf16[64,4608]{1,0:T(8,128)(2,1)}, bf16[64,4608]{1,0:T(8,128)(2,1)}, u32[]{:S(2)}, u32[]{:S(2)}) collective-permute-start(bf16[64,4608]{1,0:T(8,128)(2,1)} %after.2), channel_id=1, source_target_pairs={{0,32},{32,0},{1,33},{33,1},{2,34},{34,2},{3,35},{35,3},{4,36},{36... | collective-permute-start | bytes 1769480 | tf_op jit(solution)/shard_map/ppermute | solution.py:51
  322.6 11.7 %collective-permute-start.22 = (bf16[64,896]{1,0:T(8,128)(2,1)S(1)}, bf16[64,896]{1,0:T(8,128)(2,1)S(1)}, u32[]{:S(2)}, u32[]{:S(2)}) collective-permute-start(bf16[64,896]{1,0:T(8,128)(2,1)S(1)} %pad_maximum_fusion.near_in), channel_id=1, source_target_pairs={{0,32},{32,0},{1,33},{33,1},{2,34},{34,2},{3,35},{35,3},{4,36},{36... | collective-permute-start | bytes 344072 | tf_op jit(solution)/shard_map/ppermute | solution.py:51
  334.3 0.6 copy-start.6
  335.0 6.2 %copy-start.7 = (bf16[64,896]{1,0:T(8,128)(2,1)S(1)}, bf16[64,896]{1,0:T(8,128)(2,1)}, u32[]{:S(2)}) copy-start(bf16[64,896]{1,0:T(8,128)(2,1)} %copy-done.6) | copy-start | bytes 344068
  335.0 12.0 %copy-start.1 = (bf16[1,256,1024]{2,1,0:T(8,128)(2,1)S(1)}, bf16[1,256,1024]{2,1,0:T(8,128)(2,1)}, u32[]{:S(2)}) copy-start(bf16[1,256,1024]{2,1,0:T(8,128)(2,1)} %param.20) | copy-start | bytes 1572868
  336.2 8.9 %collective-permute-start.23 = (f32[64,4608]{1,0:T(8,128)S(1)}, f32[64,4608]{1,0:T(8,128)S(1)}, u32[]{:S(2)}, u32[]{:S(2)}) collective-permute-start(f32[64,4608]{1,0:T(8,128)S(1)} %convert_add_fusion.first_in), channel_id=1, source_target_pairs={{0,16},{16,0},{1,17},{17,1},{2,18},{18,2},{3,19},{19,3},{4,20},{20... | collective-permute-start | bytes 3538952 | tf_op jit(solution)/shard_map/ppermute | solution.py:47
  341.1 2.6 collective-permute-start.24
  341.2 2.7 collective-permute-start.25
Sparse Core Ops, SparseCore 0:
  11.4 96.4 all-gather.1
  218.5 94.0 reduce-scatter.1
where the time goes:
time: 359 us; the launch traced here: 354 us
  waiting for transfers between devices  195 us (54%)
  Pallas kernels  90.6 us (25%)
  starting transfers between devices  36.8 us (10%)
  between operations  14.9 us (4%)
  local copies, waits for them, and re-layouts  11.2 us (3%)
  other arithmetic  5.27 us (1%)
    all_gather x1, waiting for transfers between devices, gather_weights(): gathered = lax.all_gather(packed, ('z', 'y', 'core'), axis=0, tiled=True)  96.6 us
    ppermute x3, waiting for transfers between devices, swap_far(): return lax.ppermute(value, 'far', [(0, 1), (1, 0)])  50.2 us
    pallas_call x2, Pallas kernels, layer_forward(): pl.pallas_call(functools.partial(forward_kernel, keep), grid=(8,), in_spe...  33.7 us
    ppermute x12, waiting for transfers between devices, send_around(): lax.ppermute(blocks[k], axis, [(i, (i + k) % 4) for i in range(4)])  17.2 us
    pallas_call x1, Pallas kernels, layer_through(): pl.pallas_call(through_kernel, grid=(8,), in_specs=[whole((ROWS, WIDTH)),...  17.2 us
    ppermute x12, starting transfers between devices, send_around(): lax.ppermute(blocks[k], axis, [(i, (i + k) % 4) for i in range(4)])  15.5 us
    pallas_call x1, Pallas kernels, hidden_backward(): pl.pallas_call(hidden_kernel, grid=(4,), in_specs=[pl.BlockSpec(memory_sp...  12.3 us
    ppermute x1, waiting for transfers between devices, on_device(): back = lax.ppermute(early_grad, 'section', [(1, 0)])  11.8 us
  transfers between devices with their start and end apart: 28, of which 15 were waited for; matrix products, arithmetic and copies ran while one was open for 1% of the time, Pallas kernels for 8%

commit v1 on v0

--- a/solution.py
+++ b/solution.py
@@ -25,7 +25,7 @@
 GATHERED = 12416
 Z_AT, O_AT, FIRST_HALF = 2048, 2560, 3072
 DOWN_AT, OUTPUT_AT, FIRST_ALL = 2048, 4096, 4608
-EXTRA_AT, LAST_ALL, FAR_HALF, CUT = 1536, 1792, 896, 384
+QUARTER, LAST_ALL, CUT = 768, 896, 384
 
 F32 = jnp.float32
 BF16 = jnp.bfloat16
@@ -45,6 +45,10 @@
 
 def swap_cores(value):
     return lax.ppermute(value, "core", [(0, 1), (1, 0)])
+
+
+def swap_both(value):
+    return lax.ppermute(value, ("far", "core"), [(0, 3), (1, 2), (2, 1), (3, 0)])
 
 
 def swap_far(value):
@@ -265,7 +269,7 @@
     return grad
 
 
-def attention_step(keep, core, grad, column_ref, p_ref, z_ref, p_grad_ref, total_ref, kept):
+def attention_step(keep, device, grad, column_ref, p_ref, z_ref, p_grad_ref, total_ref, kept):
     rounded = grad.astype(BF16)
     z_ref[...] = dot_back(rounded, column_ref[...]).astype(BF16)
     for seq in range(ROWS // LEN):
@@ -295,12 +299,15 @@
                 at = part * WIDTH + pair * 128
                 p_grad_ref[rows, at : at + 128] = grads[part].astype(BF16)
     if keep:
-        mine_ref, theirs_ref, pair_grads_ref = kept
-        for half in range(2):
-            put_half(
-                core, half, mine_ref, theirs_ref, pl.ds(0, EXTRA_AT),
-                p_grad_ref[:, half * EXTRA_AT : (half + 1) * EXTRA_AT],
-            )
+        *quarter_refs, pair_grads_ref = kept
+        for owner in range(4):
+            values = p_grad_ref[:, owner * QUARTER : (owner + 1) * QUARTER]
+            for own in range(4):
+
+                @pl.when(device == own)
+                def _():
+                    quarter_refs[owner ^ own][...] = values
+
         pair_grads_ref[0:1] = column_sums(p_grad_ref[:, :WIDTH].astype(F32))
         pair_grads_ref[1:2] = column_sums(p_grad_ref[:, 2 * WIDTH :].astype(F32))
     total_ref[...] = grad
@@ -441,17 +448,17 @@
 
 
 def attention_kernel(
-    core_ref, branch_ref, column_ref, p_ref,
-    x_grad_ref, mine_ref, theirs_ref, pair_grads_ref, z_ref, p_grad_ref, total_ref
+    device_ref, branch_ref, column_ref, p_ref,
+    x_grad_ref, mine_ref, far_ref, core_ref, both_ref, pair_grads_ref, z_ref, p_grad_ref, total_ref
 ):
     step = pl.program_id(0)
-    kept = (mine_ref, theirs_ref, pair_grads_ref)
+    kept = (mine_ref, far_ref, core_ref, both_ref, pair_grads_ref)
 
     @pl.when(step == 0)
     def _():
         pair_grads_ref[...] = jnp.zeros_like(pair_grads_ref)
         attention_step(
-            True, core_ref[0], branch_ref[...], column_ref, p_ref, z_ref, p_grad_ref, total_ref, kept
+            True, device_ref[0], branch_ref[...], column_ref, p_ref, z_ref, p_grad_ref, total_ref, kept
         )
 
     @pl.when(step >= 1)
@@ -463,7 +470,7 @@
         x_grad_ref[...] = total_ref[...].astype(BF16)
 
 
-def attention_backward(core, branch, gathered, p):
+def attention_backward(device, branch, gathered, p):
     return pl.pallas_call(
         attention_kernel,
         grid=(4,),
@@ -473,18 +480,8 @@
             pl.BlockSpec((WIDTH, BLOCK), lambda step: (0, jnp.where(step < 1, 3, step - 1))),
             whole((ROWS, 3 * WIDTH)),
         ],
-        out_specs=[
-            whole((ROWS, WIDTH)),
-            whole((ROWS, EXTRA_AT)),
-            whole((ROWS, EXTRA_AT)),
-            whole((8, WIDTH)),
-        ],
-        out_shape=[
-            shaped(ROWS, WIDTH),
-            shaped(ROWS, EXTRA_AT),
-            shaped(ROWS, EXTRA_AT),
-            shaped(8, WIDTH, kind=F32),
-        ],
+        out_specs=[whole((ROWS, WIDTH))] + [whole((ROWS, QUARTER))] * 4 + [whole((8, WIDTH))],
+        out_shape=[shaped(ROWS, WIDTH)] + [shaped(ROWS, QUARTER)] * 4 + [shaped(8, WIDTH, kind=F32)],
         scratch_shapes=[
             pltpu.VMEM((ROWS, WIDTH), BF16),
             pltpu.VMEM((ROWS, 3 * WIDTH), BF16),
@@ -493,7 +490,7 @@
         compiler_params=pltpu.CompilerParams(vmem_limit_bytes=LIMIT),
         cost_estimate=cost(0.5),
         name="attention_backward",
-    )(core, branch, gathered, p)
+    )(device, branch, gathered, p)
 
 
 def product(left_refs, right_refs, at=0, end=None):
@@ -534,70 +531,39 @@
     )(*own, own_half, *other, other_half)
 
 
-def last_grads_kernel(far_ref, x_ref, left_ref, x2_ref, right_ref, extra_ref, near_out, far_out):
-    both = (left_ref, right_ref)
-    low = product((x_ref, x2_ref), both, 0, FAR_HALF)
-    high = product((x_ref, x2_ref), both, FAR_HALF, EXTRA_AT)
-    at = EXTRA_AT - FAR_HALF
-
-    def put(low_ref, high_ref):
-        low_ref[...] = low
-        high_ref[:, :at] = high
-        high_ref[:, at : at + 128] = extra_ref[...]
-        high_ref[:, at + 128 :] = jnp.zeros((256, LAST_ALL - EXTRA_AT - 128), BF16)
-
-    @pl.when(far_ref[0] == 0)
-    def _():
-        put(near_out, far_out)
-
-    @pl.when(far_ref[0] != 0)
-    def _():
-        put(far_out, near_out)
-
-
-def last_grads(far, own, own_half, other, other_half, extra):
-    tokens = [NARROW, whole((ROWS, EXTRA_AT))]
-    rows = lambda step: (step, 0)
-    return pl.pallas_call(
+def last_grads_kernel(place_ref, *refs):
+    lefts, rights, extra_ref = refs[:4], refs[4:8], refs[8]
+    left_out, right_out, block_ref = refs[9:13], refs[13:17], refs[17]
+
+    def part(rows, columns):
+        return sum(
+            dot_rows(left[:, rows], right[:, columns]) for left, right in zip(lefts, rights)
+        ).astype(BF16)
+
+    for k in range(4):
+        rows = pl.ds(pl.multiple_of(lax.rem(place_ref[0] + k, 4) * 256, 256), 256)
+        left_out[k][...] = part(rows, slice(0, CUT))
+    for z in range(4):
+        rows = slice(z * 256, z * 256 + 256)
+        block_ref[:, : QUARTER - CUT] = part(rows, slice(CUT, QUARTER))
+        block_ref[:, QUARTER - CUT :] = extra_ref[rows]
+        for k in range(4):
+            y = pl.multiple_of(lax.rem(place_ref[1] + k, 4) * 64, 64)
+            right_out[k][z] = block_ref[pl.ds(y, 64)]
+
+
+def last_grads(place, lefts, rights, extra):
+    vmem = pl.BlockSpec(memory_space=pltpu.VMEM)
+    results = pl.pallas_call(
         last_grads_kernel,
-        grid=(4,),
-        in_specs=[
-            pl.BlockSpec(memory_space=pltpu.SMEM), *tokens, *tokens, pl.BlockSpec((256, 128), rows)
-        ],
-        out_specs=[pl.BlockSpec((256, FAR_HALF), rows)] * 2,
-        out_shape=[shaped(WIDTH, FAR_HALF)] * 2,
+        in_specs=[pl.BlockSpec(memory_space=pltpu.SMEM)] + [vmem] * 9,
+        out_specs=[vmem] * 8,
+        out_shape=[shaped(256, CUT)] * 4 + [shaped(4, 64, LAST_ALL - CUT)] * 4,
+        scratch_shapes=[pltpu.VMEM((256, LAST_ALL - CUT), BF16)],
         compiler_params=pltpu.CompilerParams(vmem_limit_bytes=LIMIT),
         cost_estimate=cost(0.35),
         name="last_grads",
-    )(far, own, own_half, other, other_half, extra)
-
-
-def split_kernel(place_ref, near_ref, far_ref, *refs):
-    left_out, right_out = refs[:4], refs[4:8]
-    for k in range(4):
-        rows = pl.ds(pl.multiple_of(lax.rem(place_ref[0] + k, 4) * 256, 256), 256)
-        left_out[k][...] = (
-            near_ref[rows, :CUT].astype(F32) + far_ref[rows, :CUT].astype(F32)
-        ).astype(BF16)
-        for z in range(4):
-            at = z * 256 + lax.rem(place_ref[1] + k, 4) * 64
-            rows = pl.ds(pl.multiple_of(at, 64), 64)
-            right_out[k][z] = (
-                near_ref[rows, CUT:].astype(F32) + far_ref[rows, CUT:].astype(F32)
-            ).astype(BF16)
-
-
-def split(place, near, far):
-    vmem = pl.BlockSpec(memory_space=pltpu.VMEM)
-    results = pl.pallas_call(
-        split_kernel,
-        in_specs=[pl.BlockSpec(memory_space=pltpu.SMEM), vmem, vmem],
-        out_specs=[vmem] * 8,
-        out_shape=[shaped(256, CUT)] * 4 + [shaped(4, 64, FAR_HALF - CUT)] * 4,
-        compiler_params=pltpu.CompilerParams(vmem_limit_bytes=LIMIT),
-        cost_estimate=cost(0.1),
-        name="split",
-    )(place, near, far)
+    )(place, *lefts, *rights, extra)
     return results[:4], results[4:]
 
 
@@ -638,9 +604,9 @@
     project_ref, output_ref, up_ref, down_ref
 ):
     def put(half, first, low, high):
-        at = half * EXTRA_AT
-        project_ref[:, at : at + FAR_HALF] = low[...].astype(F32)
-        project_ref[:, at + FAR_HALF : at + EXTRA_AT] = high[:, : EXTRA_AT - FAR_HALF].astype(F32)
+        at = half * 2 * QUARTER
+        project_ref[:, at : at + QUARTER] = low[:, :QUARTER].astype(F32)
+        project_ref[:, at + QUARTER : at + 2 * QUARTER] = high[:, :QUARTER].astype(F32)
         output_ref[:, half * 512 : (half + 1) * 512] = first[:, OUTPUT_AT:]
         up_ref[:, half * 2048 : (half + 1) * 2048] = first[:, :DOWN_AT]
         for group in range(4):
@@ -724,18 +690,17 @@
 
 def scatter_direct(place, lefts, rights):
     lefts, rights = halfway(place, send_around(lefts, "z"), send_around(rights, "y"))
-    middle = lefts[0]
 
     def total(parts):
         return sum(part.astype(F32) for part in parts).astype(BF16)
 
     owned = jnp.concatenate([total(send_around(lefts, "y")), total(send_around(rights, "z"))], 1)
-    return lax.optimization_barrier(owned), middle
-
-
-def over_replicas(owned, earlier):
+    return lax.optimization_barrier(owned)
+
+
+def over_replicas(owned):
     owned = lax.optimization_barrier(owned)
-    total = owned.astype(F32) + after(swap_far(owned), earlier).astype(F32)
+    total = owned.astype(F32) + swap_far(owned).astype(F32)
     total = lax.optimization_barrier(total)
     return total, swap_cores(total)
 
@@ -749,9 +714,14 @@
         core, upstream, gathered, pairs, kept
     )
     packed = first_grads((hidden, e, c), mine, (hidden_2, e_2, c_2), swap_cores(theirs))
+    packed, rows16 = lax.optimization_barrier((packed, rows16))
+    rows16_far = swap_far(rows16)
+    rows16_both = swap_cores(rows16_far)
     owned = lax.psum_scatter(packed, ("z", "y"), scatter_dimension=0, tiled=True)
 
-    rows_grad, mine, theirs, more_grads = attention_backward(core, branch, gathered, kept[0])
+    rows_grad, mine, for_far, for_core, for_both, more_grads = attention_backward(
+        core * 2 + far, branch, gathered, kept[0]
+    )
     pair_grads = pair_grads + more_grads
     rows = jnp.concatenate(
         [
@@ -761,20 +731,17 @@
         1,
     ).astype(BF16)
     extra = jnp.concatenate([rows, jnp.zeros((16, 58, 128), BF16)], 1).reshape(WIDTH, 128)
-    near_part, far_part = last_grads(far, rows16, mine, rows16_2, swap_cores(theirs), extra)
-    near, middle = scatter_direct(place, *split(place, near_part, swap_far(far_part)))
+    quarters = (mine, swap_cores(for_core), swap_far(for_far), swap_both(for_both))
+    blocks = last_grads(place, (rows16, rows16_2, rows16_far, rows16_both), quarters, extra)
+    near = scatter_direct(place, *blocks)
     away = swap_far(near)
     near2, away2 = swap_cores(near), swap_cores(away)
-    first, first2 = over_replicas(after(owned, middle), away)
+    first, first2 = over_replicas(after(owned, away))
     project, output, upward, downward = finish(
         core, far, first, first2, near, near2, away, away2
     )
-    at = EXTRA_AT - FAR_HALF
-    sums = [
-        (one[:6, at : at + 128].astype(F32) + two[:6, at : at + 128].astype(F32))
-        for one, two in ((near, near2), (away, away2))
-    ]
-    vectors = jnp.where(far[0] == 1, *sums).reshape(768)
+    ends = [part[:6, QUARTER:].astype(F32) for part in (near, away, near2, away2)]
+    vectors = ((ends[0] + ends[1]) + (ends[2] + ends[3])).reshape(768)
     narrow = [vectors[64 * k : 64 * (k + 1)][None] for k in range(8)]
     query, value, output_b, down_b, gain_one, shift_one, gain_two, shift_two = narrow
     return rows_grad, (

time: 359 us -> 350 us (0.975)
  waiting for transfers between devices: 195 us -> 187 us
  starting transfers between devices: 36.8 us -> 41.7 us
  local copies, waits for them, and re-layouts: 11.2 us -> 6.98 us
    ppermute x3 -> x4, waiting for transfers between devices: 50.2 us -> 34 us  [swap_far(): return lax.ppermute(value, 'far', [(0, 1), (1, 0)])]
    ppermute x0 -> x1, waiting for transfers between devices: none -> 8.54 us  [swap_both(): lax.ppermute(value, ('far', 'core'), [(0, 3), (1, 2), (2, 1), (3, 0)])]
    reduce_scatter x1, waiting for transfers between devices: 0.01 us -> 4.35 us  [gradients(): lax.psum_scatter(packed, ('z', 'y'), scatter_dimension=0, tiled=True)]
    unnamed x48 -> x40, local copies, waits for them, and re-layouts: 8.3 us -> 4.07 us
    ppermute x3 -> x4, starting transfers between devices: 7.1 us -> 10.5 us  [swap_far(): return lax.ppermute(value, 'far', [(0, 1), (1, 0)])]
    ppermute x9 -> x10, waiting for transfers between devices: 8.72 us -> 6.54 us  [swap_cores(): return lax.ppermute(value, 'core', [(0, 1), (1, 0)])]
    ppermute x9 -> x10, starting transfers between devices: 9.6 us -> 9.82 us  [swap_cores(): return lax.ppermute(value, 'core', [(0, 1), (1, 0)])]
  transfers between devices with their start and end apart: 28 -> 31, of which waited for: 15 -> 22; matrix products, arithmetic and copies ran while one was open for 1% -> 1% of each run, Pallas kernels for 8% -> 8%
where the time goes in v1:
time: 350 us; the launch traced here: 345 us
  waiting for transfers between devices  187 us (53%)
  Pallas kernels  89.9 us (26%)
  starting transfers between devices  41.7 us (12%)
  between operations  14.9 us (4%)
  local copies, waits for them, and re-layouts  6.98 us (2%)
  other arithmetic  4.46 us (1%)
    all_gather x1, waiting for transfers between devices, gather_weights(): gathered = lax.all_gather(packed, ('z', 'y', 'core'), axis=0, tiled=True)  96.6 us
    ppermute x4, waiting for transfers between devices, swap_far(): return lax.ppermute(value, 'far', [(0, 1), (1, 0)])  34 us
    pallas_call x2, Pallas kernels, layer_forward(): pl.pallas_call(functools.partial(forward_kernel, keep), grid=(8,), in_spe...  33.7 us
    pallas_call x1, Pallas kernels, layer_through(): pl.pallas_call(through_kernel, grid=(8,), in_specs=[whole((ROWS, WIDTH)),...  17.2 us
    ppermute x12, starting transfers between devices, send_around(): lax.ppermute(blocks[k], axis, [(i, (i + k) % 4) for i in range(4)])  16 us
    ppermute x12, waiting for transfers between devices, send_around(): lax.ppermute(blocks[k], axis, [(i, (i + k) % 4) for i in range(4)])  14.4 us
    pallas_call x1, Pallas kernels, hidden_backward(): pl.pallas_call(hidden_kernel, grid=(4,), in_specs=[pl.BlockSpec(memory_sp...  12.3 us
    ppermute x1, waiting for transfers between devices, on_device(): back = lax.ppermute(early_grad, 'section', [(1, 0)])  11.8 us
  transfers between devices with their start and end apart: 31, of which 22 were waited for; matrix products, arithmetic and copies ran while one was open for 1% of the time, Pallas kernels for 8%

profile of v1, /device:TPU:1, one launch (start us, length us, event | category | flops | bytes accessed | tf_op | source)
XLA Modules:
  0.0 345.0 jit_solution(18030785342127431316)
XLA Ops:
  7.3 0.9 copy-done
  8.3 0.7 reduce
  9.0 1.1 fusion.3
  10.3 0.9 fusion.1
  11.3 96.6 %all-gather.2.cloned.1.call-done.column_ref.row_ref = bf16[1024,12416]{1,0:T(8,128)(2,1)} async-done(((bf16[32,12416]{1,0:T(8,128)(2,1)}), bf16[1024,12416]{1,0:T(8,128)(2,1)}) %all-gather.2.cloned.1.call-update) | async-done | bytes 25427984 | tf_op jit(solution)/shard_map/all_gather | solution.py:658
  107.9 1.0 slice.93
  109.4 15.8 %layer_forward.2 = bf16[256,1024]{1,0:T(8,128)(2,1)S(1)} custom-call(bf16[256,1024]{1,0:T(8,128)(2,1)S(1)} %bitcast.61, bf16[1024,12416]{1,0:T(8,128)(2,1)} %all-gather.2.cloned.1.call-done.column_ref.row_ref, bf16[1024,12416]{1,0:T(8,128)(2,1)} %all-gather.2.cloned.1.call-done.column_ref.row_ref, f32[1,8192]{1,0:T(1,128)S(1)} %constant_dynamic-update-slice_fusion.bias_ref, ...), custom_call_target="tpu_custom_call" | custom-call | flops 6442450944 | bytes 33554432 | tf_op jit(solution)/shard_map/layer_forward/pallas_call | solution.py:189
  125.2 3.3 collective-permute-start
  128.5 10.8 %collective-permute-done = bf16[256,1024]{1,0:T(8,128)(2,1)S(1)} collective-permute-done((bf16[256,1024]{1,0:T(8,128)(2,1)S(1)}, bf16[256,1024]{1,0:T(8,128)(2,1)S(1)}, u32[]{:S(2)}, u32[]{:S(2)}) %collective-permute-start) | collective-permute-done | bytes 524320 | tf_op jit(solution)/shard_map/ppermute | solution.py:804
  139.5 17.8 %layer_forward.3 = (bf16[256,1024]{1,0:T(8,128)(2,1)}, bf16[256,3072]{1,0:T(8,128)(2,1)S(1)}, bf16[256,1024]{1,0:T(8,128)(2,1)S(1)}, bf16[256,1024]{1,0:T(8,128)...) custom-call(bf16[256,1024]{1,0:T(8,128)(2,1)S(1)} %broadcast_select_, ...), custom_call_target="tpu_custom_call" | custom-call | flops 6442450944 | bytes 33554432 | tf_op jit(solution)/shard_map/layer_forward/pallas_call | solution.py:189
  157.3 17.2 %layer_through.1 = bf16[256,1024]{1,0:T(8,128)(2,1)S(1)} custom-call(bf16[256,1024]{1,0:T(8,128)(2,1)S(1)} %bitcast.62, bf16[1024,12416]{1,0:T(8,128)(2,1)} %all-gather.2.cloned.1.call-done.column_ref.row_ref, bf16[1024,12416]{1,0:T(8,128)(2,1)} %all-gather.2.cloned.1.call-done.column_ref.row_ref, f32[8,1024]{1,0:T(8,128)S(1)} %reshape.101.pairs_ref, ...), custom_call_target="tpu_custom_call" | custom-call | flops 6442450944 | bytes 33554432 | tf_op jit(solution)/shard_map/layer_through/pallas_call | solution.py:363
  174.5 1.3 collective-permute-start.1
  175.8 1.4 collective-permute-start.3
  177.2 11.8 %collective-permute-done.1 = bf16[256,1024]{1,0:T(8,128)(2,1)S(1)} collective-permute-done((bf16[256,1024]{1,0:T(8,128)(2,1)S(1)}, bf16[256,1024]{1,0:T(8,128)(2,1)S(1)}, u32[]{:S(2)}, u32[]{:S(2)}) %collective-permute-start.1) | collective-permute-done | bytes 524320 | tf_op jit(solution)/shard_map/ppermute | solution.py:814
  189.1 12.3 %hidden_backward.1 = (f32[256,1024]{1,0:T(8,128)S(1)}, bf16[256,3072]{1,0:T(8,128)(2,1)S(1)}, bf16[256,3072]{1,0:T(8,128)(2,1)}, f32[8,1024]{1,0:T(8,128)S(1)}, f32[1,4096]{1,0:T(1,128)S(1)}) custom-call(s32[1]{0:T(128)} %bitcast.20.core_ref, bf16[256,1024]{1,0:T(8,128)(2,1)S(1)} %broadcast_select_fusion.upstream_ref, ...), custom_call_target="tpu_custom_call" | custom-call | flops 3865470464 | bytes 20132660 | tf_op jit(solution)/shard_map/hidden_backward/pallas_call | solution.py:414
  201.4 1.8 collective-permute-start.5
  203.3 0.5 collective-permute-start.4
  203.8 3.1 collective-permute-done.2.h2_ref
  206.9 0.7 collective-permute-done.4.c2_ref
  207.7 0.3 collective-permute-done.5.right_ref
  208.0 1.3 copy-done.9
  209.3 9.0 %first_grads.1 = bf16[1024,4608]{1,0:T(8,128)(2,1)} custom-call(bf16[256,1024]{1,0:T(8,128)(2,1)S(1)} %get-tuple-element.67.h_ref, bf16[256,4096]{1,0:T(8,128)(2,1)} %get-tuple-element.68.e_ref, bf16[256,1024]{1,0:T(8,128)(2,1)S(1)} %get-tuple-element.69.c_ref, bf16[256,3072]{1,0:T(8,128)(2,1)S(1)} %get-tuple-element.70.left_ref, ...), custom_call_target="tpu_custom_call" | custom-call | flops 4509715456 | bytes 23488102 | tf_op jit(solution)/shard_map/first_grads/pallas_call | solution.py:522
  218.4 2.5 collective-permute-start.7
  221.0 0.7 collective-permute-start.6
  221.6 11.6 %collective-permute-done.7.refs_2_ = bf16[256,1024]{1,0:T(8,128)(2,1)} collective-permute-done((bf16[256,1024]{1,0:T(8,128)(2,1)S(1)}, bf16[256,1024]{1,0:T(8,128)(2,1)}, u32[]{:S(2)}, u32[]{:S(2)}) %collective-permute-start.7) | collective-permute-done | bytes 524320 | tf_op jit(solution)/shard_map/ppermute | solution.py:55
  233.2 1.2 collective-permute-start.8
  234.4 10.8 %attention_backward.1 = (bf16[256,1024]{1,0:T(8,128)(2,1)}, bf16[256,768]{1,0:T(8,128)(2,1)S(1)}, bf16[256,768]{1,0:T(8,128)(2,1)}, bf16[256,768]{1,0:T(8,128)(2...) custom-call(s32[1]{0:T(128)S(6)} %add.50.device_ref, f32[256,1024]{1,0:T(8,128)S(1)} %get-tuple-element.65.branch_ref, ...), custom_call_target="tpu_custom_call" | custom-call | flops 3221225472 | bytes 16777216 | tf_op jit(solution)/shard_map/attention_backward/pallas_call | solution.py:474
  245.2 0.8 copy-done.6
  245.9 2.5 collective-permute-start.10
  248.4 0.7 collective-permute-start.11
  249.1 0.4 collective-permute-start.9
  249.9 8.5 %collective-permute-done.10.refs_6_ = bf16[256,768]{1,0:T(8,128)(2,1)S(1)} collective-permute-done((bf16[256,768]{1,0:T(8,128)(2,1)}, bf16[256,768]{1,0:T(8,128)(2,1)S(1)}, u32[]{:S(2)}, u32[]{:S(2)}) %collective-permute-start.10) | collective-permute-done | bytes 393248 | tf_op jit(solution)/shard_map/ppermute | solution.py:55
  258.4 8.5 %collective-permute-done.11.refs_7_ = bf16[256,768]{1,0:T(8,128)(2,1)S(1)} collective-permute-done((bf16[256,768]{1,0:T(8,128)(2,1)}, bf16[256,768]{1,0:T(8,128)(2,1)S(1)}, u32[]{:S(2)}, u32[]{:S(2)}) %collective-permute-start.11) | collective-permute-done | bytes 393248 | tf_op jit(solution)/shard_map/ppermute | solution.py:51
  266.9 1.0 copy-done.7
  267.9 4.1 %last_grads.1 = (bf16[256,384]{1,0:T(8,128)(2,1)S(1)}, bf16[256,384]{1,0:T(8,128)(2,1)S(1)}, bf16[256,384]{1,0:T(8,128)(2,1)S(1)}, bf16[256,384]{1,0:T(8,128)(2,...) custom-call(s32[2]{0:T(128)S(1)} %pad_add_fusion.place_ref, ...), custom_call_target="tpu_custom_call" | custom-call | flops 2254857728 | bytes 11744051 | tf_op jit(solution)/shard_map/last_grads/pallas_call | solution.py:557
  272.0 0.6 collective-permute-start.12
  272.6 0.6 collective-permute-start.15
  273.3 2.5 collective-permute-start.16
  275.7 1.1 collective-permute-start.17
  276.8 1.7 collective-permute-start.13
  278.6 2.8 collective-permute-done.12.refs_1_
  281.3 1.0 collective-permute-start.14
  282.3 4.0 %collective-permute-done.13.refs_2_ = bf16[256,384]{1,0:T(8,128)(2,1)S(1)} collective-permute-done((bf16[256,384]{1,0:T(8,128)(2,1)S(1)}, bf16[256,384]{1,0:T(8,128)(2,1)S(1)}, u32[]{:S(2)}, u32[]{:S(2)}) %collective-permute-start.13) | collective-permute-done | bytes 196640 | tf_op jit(solution)/shard_map/ppermute | solution.py:670
  286.3 1.9 collective-permute-done.14.refs_3_
  288.2 1.4 collective-permute-done.16.refs_6_
  289.6 1.0 halfway.1
  290.6 3.1 collective-permute-start.18
  293.7 2.6 collective-permute-start.19
  296.3 2.7 collective-permute-start.22
  299.1 2.0 collective-permute-done.20
  301.2 0.9 collective-permute-done.21
  302.1 1.3 collective-permute-done.22
  303.5 2.9 collective-permute-start.24
  306.3 2.4 collective-permute-done.24.earlier_ref.away_in
  308.7 4.4 %reduce-scatter.2.cloned.1.call-done.value_ref = bf16[64,4608]{1,0:T(8,128)(2,1)} async-done(((bf16[1024,4608]{1,0:T(8,128)(2,1)}), bf16[64,4608]{1,0:T(8,128)(2,1)}) %reduce-scatter.2.cloned.1.call-update) | async-done | bytes 589840 | tf_op jit(solution)/shard_map/reduce_scatter | solution.py:720
  313.0 2.7 collective-permute-start.25
  315.7 11.5 %collective-permute-done.25 = bf16[64,4608]{1,0:T(8,128)(2,1)S(1)} collective-permute-done((bf16[64,4608]{1,0:T(8,128)(2,1)}, bf16[64,4608]{1,0:T(8,128)(2,1)S(1)}, u32[]{:S(2)}, u32[]{:S(2)}) %collective-permute-start.25) | collective-permute-done | bytes 589856 | tf_op jit(solution)/shard_map/ppermute | solution.py:55
  327.3 1.2 convert_add_fusion.first_in
  328.5 3.3 collective-permute-start.26
  331.9 0.4 collective-permute-start.28
  332.3 2.1 collective-permute-done.27.near2_in
  334.6 0.6 slice.87
  335.2 0.6 slice_bitcast_fusion
  335.8 1.9 finish.1
  (84 shorter events, 1.9 us)
Async XLA Ops:
  7.2 1.1 copy-start
  7.2 2.9 copy-start.14
  7.2 2.9 copy-start.15
  7.2 2.9 copy-start.16
  7.2 2.9 copy-start.17
  7.2 2.9 copy-start.10
  7.3 2.9 copy-start.11
  7.3 2.9 copy-start.12
  7.3 2.9 copy-start.13
  7.3 100.6 %all-gather.2.cloned.1.call-start = ((), (), s32[]{:S(2)}) async-start(), calls=%async_computation.1 | async-start | bytes 26222592 | tf_op jit(solution)/shard_map/all_gather | solution.py:658
  10.3 99.1 %copy-start.2 = (bf16[2,1,128,1024]{3,2,1,0:T(8,128)(2,1)S(1)}, bf16[2,1,128,1024]{3,2,1,0:T(8,128)(2,1)}, u32[]{:S(2)}) copy-start(bf16[2,1,128,1024]{3,2,1,0:T(8,128)(2,1)} %param.15) | copy-start | bytes 1572868
  11.2 301.8 %reduce-scatter.2.cloned.1.call-start = ((), (), s32[]{:S(2)}) async-start(), calls=%async_computation.2 | async-start | bytes 10027008 | tf_op jit(solution)/shard_map/reduce_scatter | solution.py:720
  125.2 14.2 %collective-permute-start = (bf16[256,1024]{1,0:T(8,128)(2,1)S(1)}, bf16[256,1024]{1,0:T(8,128)(2,1)S(1)}, u32[]{:S(2)}, u32[]{:S(2)}) collective-permute-start(bf16[256,1024]{1,0:T(8,128)(2,1)S(1)} %layer_forward.2), channel_id=1, source_target_pairs={{0,64},{1,65},{2,66},{3,67},{4,68},{5,69},{6,70},{7,71},{8,72},{9,... | collective-permute-start | bytes 1572872 | tf_op jit(solution)/shard_map/ppermute | solution.py:804
  139.5 17.9 %copy-start.3 = (bf16[2,1,128,1024]{3,2,1,0:T(8,128)(2,1)S(1)}, bf16[2,1,128,1024]{3,2,1,0:T(8,128)(2,1)}, u32[]{:S(2)}) copy-start(bf16[2,1,128,1024]{3,2,1,0:T(8,128)(2,1)} %param.16) | copy-start | bytes 1572868
  157.3 18.5 %copy-start.8 = (bf16[256,4096]{1,0:T(8,128)(2,1)S(1)}, bf16[256,4096]{1,0:T(8,128)(2,1)}, u32[]{:S(2)}) copy-start(bf16[256,4096]{1,0:T(8,128)(2,1)} %get-tuple-element.68.e_ref) | copy-start | bytes 6291460
  174.5 14.5 %collective-permute-start.1 = (bf16[256,1024]{1,0:T(8,128)(2,1)S(1)}, bf16[256,1024]{1,0:T(8,128)(2,1)S(1)}, u32[]{:S(2)}, u32[]{:S(2)}) collective-permute-start(bf16[256,1024]{1,0:T(8,128)(2,1)S(1)} %layer_through.1), channel_id=1, source_target_pairs={{64,0},{65,1},{66,2},{67,3},{68,4},{69,5},{70,6},{71,7},{72,8},{73... | collective-permute-start | bytes 1572872 | tf_op jit(solution)/shard_map/ppermute | solution.py:814
  175.8 32.2 %collective-permute-start.3 = (bf16[256,4096]{1,0:T(8,128)(2,1)S(1)}, bf16[256,4096]{1,0:T(8,128)(2,1)S(1)}, u32[]{:S(2)}, u32[]{:S(2)}) collective-permute-start(bf16[256,4096]{1,0:T(8,128)(2,1)S(1)} %copy-done.8), channel_id=1, source_target_pairs={{0,16},{16,0},{1,17},{17,1},{2,18},{18,2},{3,19},{19,3},{4,20},{20... | collective-permute-start | bytes 6291464 | tf_op jit(solution)/shard_map/ppermute | solution.py:47
  201.4 6.6 %collective-permute-start.5 = (bf16[256,3072]{1,0:T(8,128)(2,1)}, bf16[256,3072]{1,0:T(8,128)(2,1)S(1)}, u32[]{:S(2)}, u32[]{:S(2)}) collective-permute-start(bf16[256,3072]{1,0:T(8,128)(2,1)} %get-tuple-element.71), channel_id=1, source_target_pairs={{0,16},{16,0},{1,17},{17,1},{2,18},{18,2},{3,19},{19,3},{4,20},{20... | collective-permute-start | bytes 4718600 | tf_op jit(solution)/shard_map/ppermute | solution.py:47
  203.3 3.7 %collective-permute-start.2 = (bf16[256,1024]{1,0:T(8,128)(2,1)S(1)}, bf16[256,1024]{1,0:T(8,128)(2,1)S(1)}, u32[]{:S(2)}, u32[]{:S(2)}) collective-permute-start(bf16[256,1024]{1,0:T(8,128)(2,1)S(1)} %get-tuple-element.67.h_ref), channel_id=1, source_target_pairs={{0,16},{16,0},{1,17},{17,1},{2,18},{18,2},{3,19},{19,3},{4,20},{20... | collective-permute-start | bytes 1572872 | tf_op jit(solution)/shard_map/ppermute | solution.py:47
  203.3 4.4 %collective-permute-start.4 = (bf16[256,1024]{1,0:T(8,128)(2,1)S(1)}, bf16[256,1024]{1,0:T(8,128)(2,1)S(1)}, u32[]{:S(2)}, u32[]{:S(2)}) collective-permute-start(bf16[256,1024]{1,0:T(8,128)(2,1)S(1)} %get-tuple-element.69.c_ref), channel_id=1, source_target_pairs={{0,16},{16,0},{1,17},{17,1},{2,18},{18,2},{3,19},{19,3},{4,20},{20... | collective-permute-start | bytes 1572872 | tf_op jit(solution)/shard_map/ppermute | solution.py:47
  208.0 1.3 copy-start.9
  218.4 14.8 %collective-permute-start.7 = (bf16[256,1024]{1,0:T(8,128)(2,1)S(1)}, bf16[256,1024]{1,0:T(8,128)(2,1)}, u32[]{:S(2)}, u32[]{:S(2)}) collective-permute-start(bf16[256,1024]{1,0:T(8,128)(2,1)S(1)} %broadcast_select_fusion.1.x_ref.refs_0_), channel_id=1, source_target_pairs={{0,32},{32,0},{1,33},{33,1},{2,34},{34,2},{3,35},{35,3},{4,36},{36... | collective-permute-start | bytes 1572872 | tf_op jit(solution)/shard_map/ppermute | solution.py:55
  221.0 28.9 %collective-permute-start.6 = (bf16[256,1024]{1,0:T(8,128)(2,1)S(1)}, bf16[256,1024]{1,0:T(8,128)(2,1)}, u32[]{:S(2)}, u32[]{:S(2)}) collective-permute-start(bf16[256,1024]{1,0:T(8,128)(2,1)S(1)} %broadcast_select_fusion.1.x_ref.refs_0_), channel_id=1, source_target_pairs={{0,16},{16,0},{1,17},{17,1},{2,18},{18,2},{3,19},{19,3},{4,20},{20... | collective-permute-start | bytes 1572872 | tf_op jit(solution)/shard_map/ppermute | solution.py:47
  233.2 33.7 %collective-permute-start.8 = (bf16[256,1024]{1,0:T(8,128)(2,1)}, bf16[256,1024]{1,0:T(8,128)(2,1)}, u32[]{:S(2)}, u32[]{:S(2)}) collective-permute-start(bf16[256,1024]{1,0:T(8,128)(2,1)} %collective-permute-done.7.refs_2_), channel_id=1, source_target_pairs={{0,16},{16,0},{1,17},{17,1},{2,18},{18,2},{3,19},{19,3},{4,20},{20... | collective-permute-start | bytes 1572872 | tf_op jit(solution)/shard_map/ppermute | solution.py:47
  245.2 0.8 copy-start.6
  245.9 12.4 %collective-permute-start.10 = (bf16[256,768]{1,0:T(8,128)(2,1)}, bf16[256,768]{1,0:T(8,128)(2,1)S(1)}, u32[]{:S(2)}, u32[]{:S(2)}) collective-permute-start(bf16[256,768]{1,0:T(8,128)(2,1)} %get-tuple-element.76), channel_id=1, source_target_pairs={{0,32},{32,0},{1,33},{33,1},{2,34},{34,2},{3,35},{35,3},{4,36},{36... | collective-permute-start | bytes 1179656 | tf_op jit(solution)/shard_map/ppermute | solution.py:55
  248.4 18.5 %collective-permute-start.11 = (bf16[256,768]{1,0:T(8,128)(2,1)}, bf16[256,768]{1,0:T(8,128)(2,1)S(1)}, u32[]{:S(2)}, u32[]{:S(2)}) collective-permute-start(bf16[256,768]{1,0:T(8,128)(2,1)} %get-tuple-element.77), channel_id=1, source_target_pairs={{0,48},{16,32},{32,16},{48,0},{1,49},{17,33},{33,17},{49,1},{2,50}... | collective-permute-start | bytes 1179656 | tf_op jit(solution)/shard_map/ppermute | solution.py:51
  249.1 17.8 %collective-permute-start.9 = (bf16[256,768]{1,0:T(8,128)(2,1)}, bf16[256,768]{1,0:T(8,128)(2,1)S(1)}, u32[]{:S(2)}, u32[]{:S(2)}) collective-permute-start(bf16[256,768]{1,0:T(8,128)(2,1)} %get-tuple-element.75), channel_id=1, source_target_pairs={{0,16},{16,0},{1,17},{17,1},{2,18},{18,2},{3,19},{19,3},{4,20},{20... | collective-permute-start | bytes 1179656 | tf_op jit(solution)/shard_map/ppermute | solution.py:47
  266.9 1.0 copy-start.7
  272.0 9.3 %collective-permute-start.12 = (bf16[256,384]{1,0:T(8,128)(2,1)S(1)}, bf16[256,384]{1,0:T(8,128)(2,1)S(1)}, u32[]{:S(2)}, u32[]{:S(2)}) collective-permute-start(bf16[256,384]{1,0:T(8,128)(2,1)S(1)} %get-tuple-element.82), channel_id=1, source_target_pairs={{0,4},{4,8},{8,12},{12,0},{1,5},{5,9},{9,13},{13,1},{2,6},{6,10},{... | collective-permute-start | bytes 589832 | tf_op jit(solution)/shard_map/ppermute | solution.py:670
  272.6 15.6 %collective-permute-start.15 = (bf16[4,64,512]{2,1,0:T(8,128)(2,1)S(1)}, bf16[4,64,512]{2,1,0:T(8,128)(2,1)S(1)}, u32[]{:S(2)}, u32[]{:S(2)}) collective-permute-start(bf16[4,64,512]{2,1,0:T(8,128)(2,1)S(1)} %get-tuple-element.86), channel_id=1, source_target_pairs={{0,1},{1,2},{2,3},{3,0},{4,5},{5,6},{6,7},{7,4},{8,9},{9,10},{10,1... | collective-permute-start | bytes 786440 | tf_op jit(solution)/shard_map/ppermute | solution.py:670
  273.3 16.3 %collective-permute-start.16 = (bf16[4,64,512]{2,1,0:T(8,128)(2,1)S(1)}, bf16[4,64,512]{2,1,0:T(8,128)(2,1)S(1)}, u32[]{:S(2)}, u32[]{:S(2)}) collective-permute-start(bf16[4,64,512]{2,1,0:T(8,128)(2,1)S(1)} %get-tuple-element.87), channel_id=1, source_target_pairs={{0,2},{1,3},{2,0},{3,1},{4,6},{5,7},{6,4},{7,5},{8,10},{9,11},{10,... | collective-permute-start | bytes 786440 | tf_op jit(solution)/shard_map/ppermute | solution.py:670
  275.7 13.9 %collective-permute-start.17 = (bf16[4,64,512]{2,1,0:T(8,128)(2,1)S(1)}, bf16[4,64,512]{2,1,0:T(8,128)(2,1)S(1)}, u32[]{:S(2)}, u32[]{:S(2)}) collective-permute-start(bf16[4,64,512]{2,1,0:T(8,128)(2,1)S(1)} %get-tuple-element.88), channel_id=1, source_target_pairs={{0,3},{1,0},{2,1},{3,2},{4,7},{5,4},{6,5},{7,6},{8,11},{9,8},{10,9... | collective-permute-start | bytes 786440 | tf_op jit(solution)/shard_map/ppermute | solution.py:670
  276.8 9.5 %collective-permute-start.13 = (bf16[256,384]{1,0:T(8,128)(2,1)S(1)}, bf16[256,384]{1,0:T(8,128)(2,1)S(1)}, u32[]{:S(2)}, u32[]{:S(2)}) collective-permute-start(bf16[256,384]{1,0:T(8,128)(2,1)S(1)} %get-tuple-element.83), channel_id=1, source_target_pairs={{0,8},{4,12},{8,0},{12,4},{1,9},{5,13},{9,1},{13,5},{2,10},{6,14},... | collective-permute-start | bytes 589832 | tf_op jit(solution)/shard_map/ppermute | solution.py:670
  281.3 6.9 %collective-permute-start.14 = (bf16[256,384]{1,0:T(8,128)(2,1)S(1)}, bf16[256,384]{1,0:T(8,128)(2,1)S(1)}, u32[]{:S(2)}, u32[]{:S(2)}) collective-permute-start(bf16[256,384]{1,0:T(8,128)(2,1)S(1)} %get-tuple-element.84), channel_id=1, source_target_pairs={{0,12},{4,0},{8,4},{12,8},{1,13},{5,1},{9,5},{13,9},{2,14},{6,2},{... | collective-permute-start | bytes 589832 | tf_op jit(solution)/shard_map/ppermute | solution.py:670
  290.6 8.4 %collective-permute-start.18 = (bf16[64,384]{1,0:T(8,128)(2,1)S(1)}, bf16[64,384]{1,0:T(8,128)(2,1)S(1)}, u32[]{:S(2)}, u32[]{:S(2)}) collective-permute-start(bf16[64,384]{1,0:T(8,128)(2,1)S(1)} %get-tuple-element.90), channel_id=1, source_target_pairs={{0,1},{1,2},{2,3},{3,0},{4,5},{5,6},{6,7},{7,4},{8,9},{9,10},{10,1... | collective-permute-start | bytes 147464 | tf_op jit(solution)/shard_map/ppermute | solution.py:670
  293.7 5.5 %collective-permute-start.19 = (bf16[64,384]{1,0:T(8,128)(2,1)S(1)}, bf16[64,384]{1,0:T(8,128)(2,1)S(1)}, u32[]{:S(2)}, u32[]{:S(2)}) collective-permute-start(bf16[64,384]{1,0:T(8,128)(2,1)S(1)} %get-tuple-element.91), channel_id=1, source_target_pairs={{0,2},{1,3},{2,0},{3,1},{4,6},{5,7},{6,4},{7,5},{8,10},{9,11},{10,... | collective-permute-start | bytes 147464 | tf_op jit(solution)/shard_map/ppermute | solution.py:670
  296.3 4.8 %collective-permute-start.20 = (bf16[64,384]{1,0:T(8,128)(2,1)S(1)}, bf16[64,384]{1,0:T(8,128)(2,1)S(1)}, u32[]{:S(2)}, u32[]{:S(2)}) collective-permute-start(bf16[64,384]{1,0:T(8,128)(2,1)S(1)} %get-tuple-element.92), channel_id=1, source_target_pairs={{0,3},{1,0},{2,1},{3,2},{4,7},{5,4},{6,5},{7,6},{8,11},{9,8},{10,9... | collective-permute-start | bytes 147464 | tf_op jit(solution)/shard_map/ppermute | solution.py:670
  296.3 5.8 %collective-permute-start.21 = (bf16[64,512]{1,0:T(8,128)(2,1)S(1)}, bf16[64,512]{1,0:T(8,128)(2,1)S(1)}, u32[]{:S(2)}, u32[]{:S(2)}) collective-permute-start(bf16[64,512]{1,0:T(8,128)(2,1)S(1)} %get-tuple-element.94), channel_id=1, source_target_pairs={{0,4},{4,8},{8,12},{12,0},{1,5},{5,9},{9,13},{13,1},{2,6},{6,10},{... | collective-permute-start | bytes 196616 | tf_op jit(solution)/shard_map/ppermute | solution.py:670
  296.3 7.1 %collective-permute-start.22 = (bf16[64,512]{1,0:T(8,128)(2,1)S(1)}, bf16[64,512]{1,0:T(8,128)(2,1)S(1)}, u32[]{:S(2)}, u32[]{:S(2)}) collective-permute-start(bf16[64,512]{1,0:T(8,128)(2,1)S(1)} %get-tuple-element.95), channel_id=1, source_target_pairs={{0,8},{4,12},{8,0},{12,4},{1,9},{5,13},{9,1},{13,5},{2,10},{6,14},... | collective-permute-start | bytes 196616 | tf_op jit(solution)/shard_map/ppermute | solution.py:670
  299.0 4.4 %collective-permute-start.23 = (bf16[64,512]{1,0:T(8,128)(2,1)S(1)}, bf16[64,512]{1,0:T(8,128)(2,1)S(1)}, u32[]{:S(2)}, u32[]{:S(2)}) collective-permute-start(bf16[64,512]{1,0:T(8,128)(2,1)S(1)} %get-tuple-element.96), channel_id=1, source_target_pairs={{0,12},{4,0},{8,4},{12,8},{1,13},{5,1},{9,5},{13,9},{2,14},{6,2},{... | collective-permute-start | bytes 196616 | tf_op jit(solution)/shard_map/ppermute | solution.py:670
  303.5 5.2 %collective-permute-start.24 = (bf16[64,896]{1,0:T(8,128)(2,1)S(1)}, bf16[64,896]{1,0:T(8,128)(2,1)S(1)}, u32[]{:S(2)}, u32[]{:S(2)}) collective-permute-start(bf16[64,896]{1,0:T(8,128)(2,1)S(1)} %pad_maximum_fusion.near_in), channel_id=1, source_target_pairs={{0,32},{32,0},{1,33},{33,1},{2,34},{34,2},{3,35},{35,3},{4,36},{36... | collective-permute-start | bytes 344072 | tf_op jit(solution)/shard_map/ppermute | solution.py:55
  308.7 4.4 %copy-start.4 = (bf16[64,896]{1,0:T(8,128)(2,1)}, bf16[64,896]{1,0:T(8,128)(2,1)S(1)}, u32[]{:S(2)}) copy-start(bf16[64,896]{1,0:T(8,128)(2,1)S(1)} %collective-permute-done.24.earlier_ref.away_in) | copy-start | bytes 344068
  313.0 18.9 %copy-start.5 = (bf16[64,896]{1,0:T(8,128)(2,1)S(1)}, bf16[64,896]{1,0:T(8,128)(2,1)}, u32[]{:S(2)}) copy-start(bf16[64,896]{1,0:T(8,128)(2,1)} %copy-done.4) | copy-start | bytes 344068
  313.0 14.2 %collective-permute-start.25 = (bf16[64,4608]{1,0:T(8,128)(2,1)}, bf16[64,4608]{1,0:T(8,128)(2,1)S(1)}, u32[]{:S(2)}, u32[]{:S(2)}) collective-permute-start(bf16[64,4608]{1,0:T(8,128)(2,1)} %after.1), channel_id=1, source_target_pairs={{0,32},{32,0},{1,33},{33,1},{2,34},{34,2},{3,35},{35,3},{4,36},{36... | collective-permute-start | bytes 1769480 | tf_op jit(solution)/shard_map/ppermute | solution.py:55
  327.3 10.4 %copy-start.1 = (bf16[1,256,1024]{2,1,0:T(8,128)(2,1)S(1)}, bf16[1,256,1024]{2,1,0:T(8,128)(2,1)}, u32[]{:S(2)}) copy-start(bf16[1,256,1024]{2,1,0:T(8,128)(2,1)} %param.20) | copy-start | bytes 1572868
  328.5 7.3 %collective-permute-start.26 = (f32[64,4608]{1,0:T(8,128)S(1)}, f32[64,4608]{1,0:T(8,128)S(1)}, u32[]{:S(2)}, u32[]{:S(2)}) collective-permute-start(f32[64,4608]{1,0:T(8,128)S(1)} %convert_add_fusion.first_in), channel_id=1, source_target_pairs={{0,16},{16,0},{1,17},{17,1},{2,18},{18,2},{3,19},{19,3},{4,20},{20... | collective-permute-start | bytes 3538952 | tf_op jit(solution)/shard_map/ppermute | solution.py:47
  331.8 2.6 collective-permute-start.27
  331.9 2.7 collective-permute-start.28
Sparse Core Ops, SparseCore 0:
  11.4 96.4 all-gather.1
  218.5 94.4 reduce-scatter.1

commit v2 on v1

--- a/solution.py
+++ b/solution.py
@@ -705,17 +705,16 @@
     return total, swap_cores(total)
 
 
-def gradients(core, own, other, upstream, gathered, pairs, kept):
+def gradients(core, first_section, result, own, other, upstream, gathered, pairs, kept):
     rows16, c, hidden, e = own
-    rows16_2, c_2, hidden_2, e_2 = other
+    rows16_2, c_2, hidden_2, e_2, rows16_far = other
     place = jnp.stack([lax.axis_index("z"), lax.axis_index("y")]).astype(jnp.int32)
     far = lax.axis_index("far").astype(jnp.int32).reshape(1)
     branch, mine, theirs, pair_grads, up_grads = hidden_backward(
         core, upstream, gathered, pairs, kept
     )
     packed = first_grads((hidden, e, c), mine, (hidden_2, e_2, c_2), swap_cores(theirs))
-    packed, rows16 = lax.optimization_barrier((packed, rows16))
-    rows16_far = swap_far(rows16)
+    packed, rows16_far = lax.optimization_barrier((packed, rows16_far))
     rows16_both = swap_cores(rows16_far)
     owned = lax.psum_scatter(packed, ("z", "y"), scatter_dimension=0, tiled=True)
 
@@ -733,8 +732,20 @@
     extra = jnp.concatenate([rows, jnp.zeros((16, 58, 128), BF16)], 1).reshape(WIDTH, 128)
     quarters = (mine, swap_cores(for_core), swap_far(for_far), swap_both(for_both))
     blocks = last_grads(place, (rows16, rows16_2, rows16_far, rows16_both), quarters, extra)
+    seconds = jnp.concatenate([result[LEN:], rows_grad[LEN:]])
+    blocks, seconds = lax.optimization_barrier((blocks, seconds))
+    swapped = swap_far(seconds)
     near = scatter_direct(place, *blocks)
-    away = swap_far(near)
+    away, swapped = lax.optimization_barrier((swap_far(near), swapped))
+    result, rows_grad = (
+        jnp.concatenate(
+            [
+                value[:LEN],
+                jnp.where(first_section, value[LEN:], swapped[at * LEN : (at + 1) * LEN]),
+            ]
+        )
+        for at, value in enumerate((result, rows_grad))
+    )
     near2, away2 = swap_cores(near), swap_cores(away)
     first, first2 = over_replicas(after(owned, away))
     project, output, upward, downward = finish(
@@ -744,7 +755,7 @@
     vectors = ((ends[0] + ends[1]) + (ends[2] + ends[3])).reshape(768)
     narrow = [vectors[64 * k : 64 * (k + 1)][None] for k in range(8)]
     query, value, output_b, down_b, gain_one, shift_one, gain_two, shift_two = narrow
-    return rows_grad, (
+    return result, rows_grad, (
         project[None],
         output[None],
         upward[None],
@@ -758,6 +769,18 @@
         shift_one,
         gain_two,
         shift_two,
+    )
+
+
+def to_section(value, section):
+    pairs = [[(0, 2), (1, 3)], [(0, 3), (1, 2)]]
+    if section == 0:
+        pairs = [[(target, source) for source, target in each] for each in pairs]
+    return jnp.concatenate(
+        [
+            lax.ppermute(value[seq * LEN : (seq + 1) * LEN], ("section", "far"), pairs[seq])
+            for seq in range(2)
+        ]
     )
 
 
@@ -799,9 +822,10 @@
     shape = layer_input.shape
     own_rows = layer_input.reshape(-1, WIDTH)
     own_grad = cotangent.reshape(-1, WIDTH)
+    own_grad = jnp.concatenate([own_grad[:LEN], swap_far(own_grad[LEN:])])
 
     early = layer_forward(own_rows, gathered, biases, pairs, False)[0]
-    received = lax.ppermute(early, "section", [(0, 1)])
+    received = to_section(early, 1)
     rows16 = jnp.where(first_section, own_rows, received)
     result, p, c, hidden, e, slope, n_one, r_one, n_two, r_two = layer_forward(
         rows16, gathered, biases, pairs, True
@@ -809,12 +833,14 @@
     kept = (p, slope, n_one, r_one, n_two, r_two)
     own = (rows16, c, hidden, e)
     other = tuple(swap_cores(array) for array in own)
+    rows16_far, own_grad = lax.optimization_barrier((swap_far(rows16), own_grad))
+    other = (*other, rows16_far)
 
     early_grad = layer_through(own_grad, gathered, pairs, kept)
-    back = lax.ppermute(early_grad, "section", [(1, 0)])
+    back = to_section(early_grad, 0)
     upstream = jnp.where(first_section, back, own_grad)
     core = lax.axis_index("core").astype(jnp.int32).reshape(1)
-    rows_grad, grads = gradients(core, own, other, upstream, gathered, pairs, kept)
+    result, rows_grad, grads = gradients(core, first_section, result, own, other, upstream, gathered, pairs, kept)
     return (result.reshape(1, *shape), rows_grad.reshape(1, *shape), *grads)
 
 

time: 350 us -> 346 us (0.989)
  waiting for transfers between devices: 187 us -> 176 us
  starting transfers between devices: 41.7 us -> 45.9 us
    ppermute x2 -> x4, waiting for transfers between devices: 22.7 us -> 12 us  [to_section(): lax.ppermute(value[seq * LEN:(seq + 1) * LEN], ('section', 'far'), pairs[...]
    ppermute x4 -> x6, waiting for transfers between devices: 34 us -> 26.6 us  [swap_far(): return lax.ppermute(value, 'far', [(0, 1), (1, 0)])]
    ppermute x12, waiting for transfers between devices: 14.4 us -> 20.6 us  [send_around(): lax.ppermute(blocks[k], axis, [(i, (i + k) % 4) for i in range(4)])]
    reduce_scatter x1, waiting for transfers between devices: 4.35 us -> 9.59 us  [gradients(): lax.psum_scatter(packed, ('z', 'y'), scatter_dimension=0, tiled=True)]
    all_gather x1, waiting for transfers between devices: 96.6 us -> 92.9 us  [gather_weights(): gathered = lax.all_gather(packed, ('z', 'y', 'core'), axis=0, tiled=True)]
    ppermute x2 -> x4, starting transfers between devices: 4.59 us -> 8.2 us  [to_section(): lax.ppermute(value[seq * LEN:(seq + 1) * LEN], ('section', 'far'), pairs[...]
    ppermute x4 -> x6, starting transfers between devices: 10.5 us -> 12.3 us  [swap_far(): return lax.ppermute(value, 'far', [(0, 1), (1, 0)])]
  transfers between devices with their start and end apart: 31 -> 35, of which waited for: 22 -> 23; matrix products, arithmetic and copies ran while one was open for 1% -> 1% of each run, Pallas kernels for 8% -> 18%
where the time goes in v2:
time: 346 us; the launch traced here: 340 us
  waiting for transfers between devices  176 us (51%)
  Pallas kernels  89.4 us (26%)
  starting transfers between devices  45.9 us (13%)
  between operations  15 us (4%)
  local copies, waits for them, and re-layouts  7.98 us (2%)
  other arithmetic  5.83 us (2%)
    all_gather x1, waiting for transfers between devices, gather_weights(): gathered = lax.all_gather(packed, ('z', 'y', 'core'), axis=0, tiled=True)  92.9 us
    pallas_call x2, Pallas kernels, layer_forward(): pl.pallas_call(functools.partial(forward_kernel, keep), grid=(8,), in_spe...  33.4 us
    ppermute x6, waiting for transfers between devices, swap_far(): return lax.ppermute(value, 'far', [(0, 1), (1, 0)])  26.6 us
    ppermute x12, waiting for transfers between devices, send_around(): lax.ppermute(blocks[k], axis, [(i, (i + k) % 4) for i in range(4)])  20.6 us
    pallas_call x1, Pallas kernels, layer_through(): pl.pallas_call(through_kernel, grid=(8,), in_specs=[whole((ROWS, WIDTH)),...  17.2 us
    ppermute x12, starting transfers between devices, send_around(): lax.ppermute(blocks[k], axis, [(i, (i + k) % 4) for i in range(4)])  15.1 us
    pallas_call x1, Pallas kernels, hidden_backward(): pl.pallas_call(hidden_kernel, grid=(4,), in_specs=[pl.BlockSpec(memory_sp...  12.4 us
    ppermute x6, starting transfers between devices, swap_far(): return lax.ppermute(value, 'far', [(0, 1), (1, 0)])  12.3 us
  transfers between devices with their start and end apart: 35, of which 23 were waited for; matrix products, arithmetic and copies ran while one was open for 1% of the time, Pallas kernels for 18%

profile of v2, /device:TPU:1, one launch (start us, length us, event | category | flops | bytes accessed | tf_op | source)
XLA Modules:
  0.0 340.0 jit_solution(3307687033233275291)
XLA Ops:
  7.3 0.9 copy-done
  8.3 0.7 reduce
  9.0 1.1 fusion.3
  10.3 0.9 fusion.1
  11.4 3.7 %collective-permute-start.4 = (bf16[128,1024]{1,0:T(8,128)(2,1)S(1)}, bf16[128,1024]{1,0:T(8,128)(2,1)S(1)}, u32[]{:S(2)}, u32[]{:S(2)}) collective-permute-start(bf16[128,1024]{1,0:T(8,128)(2,1)S(1)} %get-tuple-element.164), channel_id=1, source_target_pairs={{0,32},{32,0},{1,33},{33,1},{2,34},{34,2},{3,35},{35,3},{4,36},{36... | collective-permute-start | bytes 786440 | tf_op jit(solution)/shard_map/ppermute | solution.py:55
  15.0 92.9 %all-gather.2.cloned.1.call-done.column_ref.row_ref = bf16[1024,12416]{1,0:T(8,128)(2,1)} async-done(((bf16[32,12416]{1,0:T(8,128)(2,1)}), bf16[1024,12416]{1,0:T(8,128)(2,1)}) %all-gather.2.cloned.1.call-update) | async-done | bytes 25427984 | tf_op jit(solution)/shard_map/all_gather | solution.py:658
  107.9 1.0 slice.151
  109.4 15.8 %layer_forward.2 = bf16[256,1024]{1,0:T(8,128)(2,1)S(1)} custom-call(bf16[256,1024]{1,0:T(8,128)(2,1)S(1)} %bitcast.63, bf16[1024,12416]{1,0:T(8,128)(2,1)} %all-gather.2.cloned.1.call-done.column_ref.row_ref, bf16[1024,12416]{1,0:T(8,128)(2,1)} %all-gather.2.cloned.1.call-done.column_ref.row_ref, f32[1,8192]{1,0:T(1,128)S(1)} %constant_dynamic-update-slice_fusion.bias_ref, ...), custom_call_target="tpu_custom_call" | custom-call | flops 6442450944 | bytes 33554432 | tf_op jit(solution)/shard_map/layer_forward/pallas_call | solution.py:189
  125.3 3.1 collective-permute-start
  128.4 2.5 collective-permute-start.1
  131.0 2.8 collective-permute-done
  133.8 2.5 collective-permute-done.1
  136.6 1.4 collective-permute-start.3
  138.0 17.6 %layer_forward.3 = (bf16[256,1024]{1,0:T(8,128)(2,1)S(1)}, bf16[256,3072]{1,0:T(8,128)(2,1)S(1)}, bf16[256,1024]{1,0:T(8,128)(2,1)S(1)}, bf16[256,1024]{1,0:T(8,...) custom-call(bf16[256,1024]{1,0:T(8,128)(2,1)S(1)} %maximum_select_fu, ...), custom_call_target="tpu_custom_call" | custom-call | flops 6442450944 | bytes 33554432 | tf_op jit(solution)/shard_map/layer_forward/pallas_call | solution.py:189
  155.6 17.2 %layer_through.1 = bf16[256,1024]{1,0:T(8,128)(2,1)S(1)} custom-call(bf16[256,1024]{1,0:T(8,128)(2,1)S(1)} %pad_maximum_fusion.upstream_ref, bf16[1024,12416]{1,0:T(8,128)(2,1)} %all-gather.2.cloned.1.call-done.column_ref.row_ref, bf16[1024,12416]{1,0:T(8,128)(2,1)} %all-gather.2.cloned.1.call-done.column_ref.row_ref, f32[8,1024]{1,0:T(8,128)S(1)} %reshape.101.pairs_ref, ...), custom_call_target="tpu_custom_call" | custom-call | flops 6442450944 | bytes 33554432 | tf_op jit(solution)/shard_map/layer_through/pallas_call | solution.py:363
  172.8 1.3 collective-permute-start.5
  174.1 1.3 collective-permute-start.6
  175.5 1.6 collective-permute-start.8
  177.1 5.1 %collective-permute-done.5 = bf16[128,1024]{1,0:T(8,128)(2,1)S(1)} collective-permute-done((bf16[128,1024]{1,0:T(8,128)(2,1)S(1)}, bf16[128,1024]{1,0:T(8,128)(2,1)S(1)}, u32[]{:S(2)}, u32[]{:S(2)}) %collective-permute-start.5) | collective-permute-done | bytes 262176 | tf_op jit(solution)/shard_map/ppermute | solution.py:781
  182.2 1.5 collective-permute-done.6
  183.9 12.4 %hidden_backward.1 = (f32[256,1024]{1,0:T(8,128)S(1)}, bf16[256,3072]{1,0:T(8,128)(2,1)S(1)}, bf16[256,3072]{1,0:T(8,128)(2,1)}, f32[8,1024]{1,0:T(8,128)S(1)}, f32[1,4096]{1,0:T(1,128)S(1)}) custom-call(s32[1]{0:T(128)} %bitcast.20.core_ref, bf16[256,1024]{1,0:T(8,128)(2,1)S(1)} %maximum_select_fusion.1.upstream_ref, ...), custom_call_target="tpu_custom_call" | custom-call | flops 3865470464 | bytes 20132660 | tf_op jit(solution)/shard_map/hidden_backward/pallas_call | solution.py:414
  196.3 1.0 copy-done.3
  197.3 2.3 collective-permute-start.10
  200.1 3.1 collective-permute-done.7.h2_ref
  203.2 0.7 collective-permute-done.9.c2_ref
  204.3 1.0 copy-done.10
  205.3 9.0 %first_grads.1 = bf16[1024,4608]{1,0:T(8,128)(2,1)} custom-call(bf16[256,1024]{1,0:T(8,128)(2,1)S(1)} %get-tuple-element.72.h_ref, bf16[256,4096]{1,0:T(8,128)(2,1)} %get-tuple-element.73.e_ref, bf16[256,1024]{1,0:T(8,128)(2,1)S(1)} %get-tuple-element.74.c_ref, bf16[256,3072]{1,0:T(8,128)(2,1)S(1)} %get-tuple-element.82.left_ref, ...), custom_call_target="tpu_custom_call" | custom-call | flops 4509715456 | bytes 23488102 | tf_op jit(solution)/shard_map/first_grads/pallas_call | solution.py:522
  214.6 1.2 copy-done.4
  215.9 10.4 %attention_backward.1 = (bf16[256,1024]{1,0:T(8,128)(2,1)S(1)}, bf16[256,768]{1,0:T(8,128)(2,1)S(1)}, bf16[256,768]{1,0:T(8,128)(2,1)}, bf16[256,768]{1,0:T(8,12...) custom-call(s32[1]{0:T(128)S(6)} %add.50.device_ref, f32[256,1024]{1,0:T(8,128)S(1)} %copy-done.4, ...), custom_call_target="tpu_custom_call" | custom-call | flops 3221225472 | bytes 16777216 | tf_op jit(solution)/shard_map/attention_backward/pallas_call | solution.py:474
  226.3 0.7 copy-done.7
  227.4 1.6 collective-permute-start.13
  228.9 1.7 collective-permute-start.14
  231.4 8.4 %collective-permute-done.13.refs_6_ = bf16[256,768]{1,0:T(8,128)(2,1)} collective-permute-done((bf16[256,768]{1,0:T(8,128)(2,1)}, bf16[256,768]{1,0:T(8,128)(2,1)}, u32[]{:S(2)}, u32[]{:S(2)}) %collective-permute-start.13) | collective-permute-done | bytes 393248 | tf_op jit(solution)/shard_map/ppermute | solution.py:55
  239.7 8.7 %collective-permute-done.14.refs_7_ = bf16[256,768]{1,0:T(8,128)(2,1)} collective-permute-done((bf16[256,768]{1,0:T(8,128)(2,1)}, bf16[256,768]{1,0:T(8,128)(2,1)}, u32[]{:S(2)}, u32[]{:S(2)}) %collective-permute-start.14) | collective-permute-done | bytes 393248 | tf_op jit(solution)/shard_map/ppermute | solution.py:51
  248.4 4.1 %last_grads.1 = (bf16[256,384]{1,0:T(8,128)(2,1)S(1)}, bf16[256,384]{1,0:T(8,128)(2,1)S(1)}, bf16[256,384]{1,0:T(8,128)(2,1)S(1)}, bf16[256,384]{1,0:T(8,128)(2,...) custom-call(s32[2]{0:T(128)S(1)} %pad_add_fusion.place_ref, ...), custom_call_target="tpu_custom_call" | custom-call | flops 2254857728 | bytes 11744051 | tf_op jit(solution)/shard_map/last_grads/pallas_call | solution.py:557
  252.6 0.6 collective-permute-start.15
  253.2 0.7 collective-permute-start.18
  253.9 2.5 collective-permute-start.19
  256.4 1.1 collective-permute-start.20
  257.5 1.9 collective-permute-start.16
  259.4 4.4 %collective-permute-done.15.refs_1_ = bf16[256,384]{1,0:T(8,128)(2,1)S(1)} collective-permute-done((bf16[256,384]{1,0:T(8,128)(2,1)S(1)}, bf16[256,384]{1,0:T(8,128)(2,1)S(1)}, u32[]{:S(2)}, u32[]{:S(2)}) %collective-permute-start.15) | collective-permute-done | bytes 196640 | tf_op jit(solution)/shard_map/ppermute | solution.py:670
  263.9 1.8 collective-permute-start.17
  265.7 8.0 %collective-permute-done.16.refs_2_ = bf16[256,384]{1,0:T(8,128)(2,1)S(1)} collective-permute-done((bf16[256,384]{1,0:T(8,128)(2,1)S(1)}, bf16[256,384]{1,0:T(8,128)(2,1)S(1)}, u32[]{:S(2)}, u32[]{:S(2)}) %collective-permute-start.16) | collective-permute-done | bytes 196640 | tf_op jit(solution)/shard_map/ppermute | solution.py:670
  273.7 2.0 collective-permute-done.17.refs_3_
  275.7 3.0 collective-permute-done.19.refs_6_
  278.7 1.0 halfway.1
  279.7 1.1 collective-permute-start.22
  280.8 2.0 collective-permute-start.23
  282.7 2.2 collective-permute-start.28
  285.1 3.1 collective-permute-start.25
  288.5 1.1 collective-permute-done.24
  289.6 1.2 collective-permute-done.25
  290.8 0.8 collective-permute-done.26
  291.7 0.8 collective-permute-start.27
  292.4 6.1 %collective-permute-done.27.earlier_ref.away_in = bf16[64,896]{1,0:T(8,128)(2,1)S(1)} collective-permute-done((bf16[64,896]{1,0:T(8,128)(2,1)S(1)}, bf16[64,896]{1,0:T(8,128)(2,1)S(1)}, u32[]{:S(2)}, u32[]{:S(2)}) %collective-permute-start.27) | collective-permute-done | bytes 114720 | tf_op jit(solution)/shard_map/ppermute | solution.py:55
  298.5 9.6 %reduce-scatter.2.cloned.1.call-done.value_ref = bf16[64,4608]{1,0:T(8,128)(2,1)} async-done(((bf16[1024,4608]{1,0:T(8,128)(2,1)}), bf16[64,4608]{1,0:T(8,128)(2,1)}) %reduce-scatter.2.cloned.1.call-update) | async-done | bytes 589840 | tf_op jit(solution)/shard_map/reduce_scatter | solution.py:719
  308.1 2.7 collective-permute-start.29
  310.8 12.1 %collective-permute-done.29 = bf16[64,4608]{1,0:T(8,128)(2,1)S(1)} collective-permute-done((bf16[64,4608]{1,0:T(8,128)(2,1)}, bf16[64,4608]{1,0:T(8,128)(2,1)S(1)}, u32[]{:S(2)}, u32[]{:S(2)}) %collective-permute-start.29) | collective-permute-done | bytes 589856 | tf_op jit(solution)/shard_map/ppermute | solution.py:55
  322.9 1.2 convert_add_fusion.first_in
  324.1 2.7 collective-permute-start.30
  327.4 1.0 pad_maximum_fusion.2
  328.5 1.0 collective-permute-done.31.near2_in
  330.2 0.6 slice_bitcast_fusion.2
  330.8 1.9 finish.1
  (105 shorter events, 5.4 us)
Async XLA Ops:
  7.2 1.1 copy-start
  7.2 2.9 copy-start.16
  7.2 2.9 copy-start.17
  7.2 2.9 copy-start.18
  7.2 2.9 copy-start.19
  7.2 2.9 copy-start.12
  7.3 2.9 copy-start.13
  7.3 2.9 copy-start.14
  7.3 2.9 copy-start.15
  7.3 100.6 %all-gather.2.cloned.1.call-start = ((), (), s32[]{:S(2)}) async-start(), calls=%async_computation.1 | async-start | bytes 26222592 | tf_op jit(solution)/shard_map/all_gather | solution.py:658
  10.1 1.2 copy-start.11
  11.2 98.2 %copy-start.2 = (bf16[2,1,128,1024]{3,2,1,0:T(8,128)(2,1)S(1)}, bf16[2,1,128,1024]{3,2,1,0:T(8,128)(2,1)}, u32[]{:S(2)}) copy-start(bf16[2,1,128,1024]{3,2,1,0:T(8,128)(2,1)} %param.15) | copy-start | bytes 1572868
  11.3 296.8 %reduce-scatter.2.cloned.1.call-start = ((), (), s32[]{:S(2)}) async-start(), calls=%async_computation.2 | async-start | bytes 10027008 | tf_op jit(solution)/shard_map/reduce_scatter | solution.py:719
  11.4 119.6 %collective-permute-start.4 = (bf16[128,1024]{1,0:T(8,128)(2,1)S(1)}, bf16[128,1024]{1,0:T(8,128)(2,1)S(1)}, u32[]{:S(2)}, u32[]{:S(2)}) collective-permute-start(bf16[128,1024]{1,0:T(8,128)(2,1)S(1)} %get-tuple-element.164), channel_id=1, source_target_pairs={{0,32},{32,0},{1,33},{33,1},{2,34},{34,2},{3,35},{35,3},{4,36},{36... | collective-permute-start | bytes 786440 | tf_op jit(solution)/shard_map/ppermute | solution.py:55
  125.3 8.5 %collective-permute-start = (bf16[128,1024]{1,0:T(8,128)(2,1)S(1)}, bf16[128,1024]{1,0:T(8,128)(2,1)S(1)}, u32[]{:S(2)}, u32[]{:S(2)}) collective-permute-start(bf16[128,1024]{1,0:T(8,128)(2,1)S(1)} %get-tuple-element.165), channel_id=1, source_target_pairs={{0,64},{32,96},{1,65},{33,97},{2,66},{34,98},{3,67},{35,99},{4,68}... | collective-permute-start | bytes 786440 | tf_op jit(solution)/shard_map/ppermute | solution.py:781
  128.4 7.9 %collective-permute-start.1 = (bf16[128,1024]{1,0:T(8,128)(2,1)S(1)}, bf16[128,1024]{1,0:T(8,128)(2,1)S(1)}, u32[]{:S(2)}, u32[]{:S(2)}) collective-permute-start(bf16[128,1024]{1,0:T(8,128)(2,1)S(1)} %get-tuple-element.166), channel_id=1, source_target_pairs={{0,96},{32,64},{1,97},{33,65},{2,98},{34,66},{3,99},{35,67},{4,100... | collective-permute-start | bytes 786440 | tf_op jit(solution)/shard_map/ppermute | solution.py:781
  136.6 19.1 %collective-permute-start.3 = (bf16[256,1024]{1,0:T(8,128)(2,1)S(1)}, bf16[256,1024]{1,0:T(8,128)(2,1)}, u32[]{:S(2)}, u32[]{:S(2)}) collective-permute-start(bf16[256,1024]{1,0:T(8,128)(2,1)S(1)} %maximum_select_fusion.x_ref.refs_0_), channel_id=1, source_target_pairs={{0,32},{32,0},{1,33},{33,1},{2,34},{34,2},{3,35},{35,3},{4,36},{36... | collective-permute-start | bytes 1572872 | tf_op jit(solution)/shard_map/ppermute | solution.py:55
  155.6 19.8 %copy-start.9 = (bf16[256,4096]{1,0:T(8,128)(2,1)S(1)}, bf16[256,4096]{1,0:T(8,128)(2,1)}, u32[]{:S(2)}) copy-start(bf16[256,4096]{1,0:T(8,128)(2,1)} %get-tuple-element.73.e_ref) | copy-start | bytes 6291460
  172.8 9.3 %collective-permute-start.5 = (bf16[128,1024]{1,0:T(8,128)(2,1)S(1)}, bf16[128,1024]{1,0:T(8,128)(2,1)S(1)}, u32[]{:S(2)}, u32[]{:S(2)}) collective-permute-start(bf16[128,1024]{1,0:T(8,128)(2,1)S(1)} %get-tuple-element.161), channel_id=1, source_target_pairs={{64,0},{96,32},{65,1},{97,33},{66,2},{98,34},{67,3},{99,35},{68,4}... | collective-permute-start | bytes 786440 | tf_op jit(solution)/shard_map/ppermute | solution.py:781
  174.1 9.6 %collective-permute-start.6 = (bf16[128,1024]{1,0:T(8,128)(2,1)S(1)}, bf16[128,1024]{1,0:T(8,128)(2,1)S(1)}, u32[]{:S(2)}, u32[]{:S(2)}) collective-permute-start(bf16[128,1024]{1,0:T(8,128)(2,1)S(1)} %get-tuple-element.162), channel_id=1, source_target_pairs={{96,0},{64,32},{97,1},{65,33},{98,2},{66,34},{99,3},{67,35},{100,4... | collective-permute-start | bytes 786440 | tf_op jit(solution)/shard_map/ppermute | solution.py:781
  175.5 28.5 %collective-permute-start.8 = (bf16[256,4096]{1,0:T(8,128)(2,1)S(1)}, bf16[256,4096]{1,0:T(8,128)(2,1)S(1)}, u32[]{:S(2)}, u32[]{:S(2)}) collective-permute-start(bf16[256,4096]{1,0:T(8,128)(2,1)S(1)} %copy-done.9), channel_id=1, source_target_pairs={{0,16},{16,0},{1,17},{17,1},{2,18},{18,2},{3,19},{19,3},{4,20},{20... | collective-permute-start | bytes 6291464 | tf_op jit(solution)/shard_map/ppermute | solution.py:47
  196.3 1.0 copy-start.3
  197.3 7.0 %collective-permute-start.10 = (bf16[256,3072]{1,0:T(8,128)(2,1)}, bf16[256,3072]{1,0:T(8,128)(2,1)S(1)}, u32[]{:S(2)}, u32[]{:S(2)}) collective-permute-start(bf16[256,3072]{1,0:T(8,128)(2,1)} %get-tuple-element.83), channel_id=1, source_target_pairs={{0,16},{16,0},{1,17},{17,1},{2,18},{18,2},{3,19},{19,3},{4,20},{20... | collective-permute-start | bytes 4718600 | tf_op jit(solution)/shard_map/ppermute | solution.py:47
  199.6 3.7 %collective-permute-start.7 = (bf16[256,1024]{1,0:T(8,128)(2,1)S(1)}, bf16[256,1024]{1,0:T(8,128)(2,1)S(1)}, u32[]{:S(2)}, u32[]{:S(2)}) collective-permute-start(bf16[256,1024]{1,0:T(8,128)(2,1)S(1)} %get-tuple-element.72.h_ref), channel_id=1, source_target_pairs={{0,16},{16,0},{1,17},{17,1},{2,18},{18,2},{3,19},{19,3},{4,20},{20... | collective-permute-start | bytes 1572872 | tf_op jit(solution)/shard_map/ppermute | solution.py:47
  199.6 4.4 %collective-permute-start.9 = (bf16[256,1024]{1,0:T(8,128)(2,1)S(1)}, bf16[256,1024]{1,0:T(8,128)(2,1)S(1)}, u32[]{:S(2)}, u32[]{:S(2)}) collective-permute-start(bf16[256,1024]{1,0:T(8,128)(2,1)S(1)} %get-tuple-element.74.c_ref), channel_id=1, source_target_pairs={{0,16},{16,0},{1,17},{17,1},{2,18},{18,2},{3,19},{19,3},{4,20},{20... | collective-permute-start | bytes 1572872 | tf_op jit(solution)/shard_map/ppermute | solution.py:47
  204.0 1.3 copy-start.10
  214.4 16.9 %collective-permute-start.2 = (bf16[256,1024]{1,0:T(8,128)(2,1)S(1)}, bf16[256,1024]{1,0:T(8,128)(2,1)}, u32[]{:S(2)}, u32[]{:S(2)}) collective-permute-start(bf16[256,1024]{1,0:T(8,128)(2,1)S(1)} %maximum_select_fusion.x_ref.refs_0_), channel_id=1, source_target_pairs={{0,16},{16,0},{1,17},{17,1},{2,18},{18,2},{3,19},{19,3},{4,20},{20... | collective-permute-start | bytes 1572872 | tf_op jit(solution)/shard_map/ppermute | solution.py:47
  214.6 1.2 copy-start.4
  226.3 0.7 copy-start.7
  227.0 21.4 %copy-start.8 = (bf16[256,768]{1,0:T(8,128)(2,1)S(1)}, bf16[256,768]{1,0:T(8,128)(2,1)}, u32[]{:S(2)}) copy-start(bf16[256,768]{1,0:T(8,128)(2,1)} %copy-done.7) | copy-start | bytes 1179652
  227.0 4.4 %collective-permute-start.12 = (bf16[256,768]{1,0:T(8,128)(2,1)}, bf16[256,768]{1,0:T(8,128)(2,1)S(1)}, u32[]{:S(2)}, u32[]{:S(2)}) collective-permute-start(bf16[256,768]{1,0:T(8,128)(2,1)} %get-tuple-element.88), channel_id=1, source_target_pairs={{0,16},{16,0},{1,17},{17,1},{2,18},{18,2},{3,19},{19,3},{4,20},{20... | collective-permute-start | bytes 1179656 | tf_op jit(solution)/shard_map/ppermute | solution.py:47
  227.4 12.4 %collective-permute-start.13 = (bf16[256,768]{1,0:T(8,128)(2,1)}, bf16[256,768]{1,0:T(8,128)(2,1)}, u32[]{:S(2)}, u32[]{:S(2)}) collective-permute-start(bf16[256,768]{1,0:T(8,128)(2,1)} %get-tuple-element.89), channel_id=1, source_target_pairs={{0,32},{32,0},{1,33},{33,1},{2,34},{34,2},{3,35},{35,3},{4,36},{36... | collective-permute-start | bytes 1179656 | tf_op jit(solution)/shard_map/ppermute | solution.py:55
  228.9 19.5 %collective-permute-start.14 = (bf16[256,768]{1,0:T(8,128)(2,1)}, bf16[256,768]{1,0:T(8,128)(2,1)}, u32[]{:S(2)}, u32[]{:S(2)}) collective-permute-start(bf16[256,768]{1,0:T(8,128)(2,1)} %get-tuple-element.90), channel_id=1, source_target_pairs={{0,48},{16,32},{32,16},{48,0},{1,49},{17,33},{33,17},{49,1},{2,50}... | collective-permute-start | bytes 1179656 | tf_op jit(solution)/shard_map/ppermute | solution.py:51
  230.6 17.8 %collective-permute-start.11 = (bf16[256,1024]{1,0:T(8,128)(2,1)}, bf16[256,1024]{1,0:T(8,128)(2,1)S(1)}, u32[]{:S(2)}, u32[]{:S(2)}) collective-permute-start(bf16[256,1024]{1,0:T(8,128)(2,1)} %collective-permute-done.3.refs_2_), channel_id=1, source_target_pairs={{0,16},{16,0},{1,17},{17,1},{2,18},{18,2},{3,19},{19,3},{4,20},{20... | collective-permute-start | bytes 1572872 | tf_op jit(solution)/shard_map/ppermute | solution.py:47
  252.6 11.3 %collective-permute-start.15 = (bf16[256,384]{1,0:T(8,128)(2,1)S(1)}, bf16[256,384]{1,0:T(8,128)(2,1)S(1)}, u32[]{:S(2)}, u32[]{:S(2)}) collective-permute-start(bf16[256,384]{1,0:T(8,128)(2,1)S(1)} %get-tuple-element.104), channel_id=1, source_target_pairs={{0,4},{4,8},{8,12},{12,0},{1,5},{5,9},{9,13},{13,1},{2,6},{6,10},{... | collective-permute-start | bytes 589832 | tf_op jit(solution)/shard_map/ppermute | solution.py:670
  253.2 22.5 %collective-permute-start.18 = (bf16[4,64,512]{2,1,0:T(8,128)(2,1)S(1)}, bf16[4,64,512]{2,1,0:T(8,128)(2,1)S(1)}, u32[]{:S(2)}, u32[]{:S(2)}) collective-permute-start(bf16[4,64,512]{2,1,0:T(8,128)(2,1)S(1)} %get-tuple-element.108), channel_id=1, source_target_pairs={{0,1},{1,2},{2,3},{3,0},{4,5},{5,6},{6,7},{7,4},{8,9},{9,10},{10,1... | collective-permute-start | bytes 786440 | tf_op jit(solution)/shard_map/ppermute | solution.py:670
  253.9 24.8 %collective-permute-start.19 = (bf16[4,64,512]{2,1,0:T(8,128)(2,1)S(1)}, bf16[4,64,512]{2,1,0:T(8,128)(2,1)S(1)}, u32[]{:S(2)}, u32[]{:S(2)}) collective-permute-start(bf16[4,64,512]{2,1,0:T(8,128)(2,1)S(1)} %get-tuple-element.109), channel_id=1, source_target_pairs={{0,2},{1,3},{2,0},{3,1},{4,6},{5,7},{6,4},{7,5},{8,10},{9,11},{10,... | collective-permute-start | bytes 786440 | tf_op jit(solution)/shard_map/ppermute | solution.py:670
  256.4 22.3 %collective-permute-start.20 = (bf16[4,64,512]{2,1,0:T(8,128)(2,1)S(1)}, bf16[4,64,512]{2,1,0:T(8,128)(2,1)S(1)}, u32[]{:S(2)}, u32[]{:S(2)}) collective-permute-start(bf16[4,64,512]{2,1,0:T(8,128)(2,1)S(1)} %get-tuple-element.110), channel_id=1, source_target_pairs={{0,3},{1,0},{2,1},{3,2},{4,7},{5,4},{6,5},{7,6},{8,11},{9,8},{10,9... | collective-permute-start | bytes 786440 | tf_op jit(solution)/shard_map/ppermute | solution.py:670
  257.5 16.2 %collective-permute-start.16 = (bf16[256,384]{1,0:T(8,128)(2,1)S(1)}, bf16[256,384]{1,0:T(8,128)(2,1)S(1)}, u32[]{:S(2)}, u32[]{:S(2)}) collective-permute-start(bf16[256,384]{1,0:T(8,128)(2,1)S(1)} %get-tuple-element.105), channel_id=1, source_target_pairs={{0,8},{4,12},{8,0},{12,4},{1,9},{5,13},{9,1},{13,5},{2,10},{6,14},... | collective-permute-start | bytes 589832 | tf_op jit(solution)/shard_map/ppermute | solution.py:670
  263.9 11.8 %collective-permute-start.17 = (bf16[256,384]{1,0:T(8,128)(2,1)S(1)}, bf16[256,384]{1,0:T(8,128)(2,1)S(1)}, u32[]{:S(2)}, u32[]{:S(2)}) collective-permute-start(bf16[256,384]{1,0:T(8,128)(2,1)S(1)} %get-tuple-element.106), channel_id=1, source_target_pairs={{0,12},{4,0},{8,4},{12,8},{1,13},{5,1},{9,5},{13,9},{2,14},{6,2},{... | collective-permute-start | bytes 589832 | tf_op jit(solution)/shard_map/ppermute | solution.py:670
  279.6 5.5 %collective-permute-start.21 = (bf16[64,384]{1,0:T(8,128)(2,1)S(1)}, bf16[64,384]{1,0:T(8,128)(2,1)S(1)}, u32[]{:S(2)}, u32[]{:S(2)}) collective-permute-start(bf16[64,384]{1,0:T(8,128)(2,1)S(1)} %get-tuple-element.112), channel_id=1, source_target_pairs={{0,1},{1,2},{2,3},{3,0},{4,5},{5,6},{6,7},{7,4},{8,9},{9,10},{10,1... | collective-permute-start | bytes 147464 | tf_op jit(solution)/shard_map/ppermute | solution.py:670
  279.7 8.5 %collective-permute-start.22 = (bf16[64,384]{1,0:T(8,128)(2,1)S(1)}, bf16[64,384]{1,0:T(8,128)(2,1)S(1)}, u32[]{:S(2)}, u32[]{:S(2)}) collective-permute-start(bf16[64,384]{1,0:T(8,128)(2,1)S(1)} %get-tuple-element.113), channel_id=1, source_target_pairs={{0,2},{1,3},{2,0},{3,1},{4,6},{5,7},{6,4},{7,5},{8,10},{9,11},{10,... | collective-permute-start | bytes 147464 | tf_op jit(solution)/shard_map/ppermute | solution.py:670
  280.8 7.7 %collective-permute-start.23 = (bf16[64,384]{1,0:T(8,128)(2,1)S(1)}, bf16[64,384]{1,0:T(8,128)(2,1)S(1)}, u32[]{:S(2)}, u32[]{:S(2)}) collective-permute-start(bf16[64,384]{1,0:T(8,128)(2,1)S(1)} %get-tuple-element.114), channel_id=1, source_target_pairs={{0,3},{1,0},{2,1},{3,2},{4,7},{5,4},{6,5},{7,6},{8,11},{9,8},{10,9... | collective-permute-start | bytes 147464 | tf_op jit(solution)/shard_map/ppermute | solution.py:670
  282.7 15.8 %collective-permute-start.28 = (bf16[256,1024]{1,0:T(8,128)(2,1)S(1)}, bf16[256,1024]{1,0:T(8,128)(2,1)S(1)}, u32[]{:S(2)}, u32[]{:S(2)}) collective-permute-start(bf16[256,1024]{1,0:T(8,128)(2,1)S(1)} %pad_maximum_fusion.1), channel_id=1, source_target_pairs={{0,32},{32,0},{1,33},{33,1},{2,34},{34,2},{3,35},{35,3},{4,36},{36... | collective-permute-start | bytes 1572872 | tf_op jit(solution)/shard_map/ppermute | solution.py:55
  285.0 4.6 %collective-permute-start.24 = (bf16[64,512]{1,0:T(8,128)(2,1)S(1)}, bf16[64,512]{1,0:T(8,128)(2,1)S(1)}, u32[]{:S(2)}, u32[]{:S(2)}) collective-permute-start(bf16[64,512]{1,0:T(8,128)(2,1)S(1)} %get-tuple-element.116), channel_id=1, source_target_pairs={{0,4},{4,8},{8,12},{12,0},{1,5},{5,9},{9,13},{13,1},{2,6},{6,10},{... | collective-permute-start | bytes 196616 | tf_op jit(solution)/shard_map/ppermute | solution.py:670
  285.1 5.7 %collective-permute-start.25 = (bf16[64,512]{1,0:T(8,128)(2,1)S(1)}, bf16[64,512]{1,0:T(8,128)(2,1)S(1)}, u32[]{:S(2)}, u32[]{:S(2)}) collective-permute-start(bf16[64,512]{1,0:T(8,128)(2,1)S(1)} %get-tuple-element.117), channel_id=1, source_target_pairs={{0,8},{4,12},{8,0},{12,4},{1,9},{5,13},{9,1},{13,5},{2,10},{6,14},... | collective-permute-start | bytes 196616 | tf_op jit(solution)/shard_map/ppermute | solution.py:670
  288.2 3.4 %collective-permute-start.26 = (bf16[64,512]{1,0:T(8,128)(2,1)S(1)}, bf16[64,512]{1,0:T(8,128)(2,1)S(1)}, u32[]{:S(2)}, u32[]{:S(2)}) collective-permute-start(bf16[64,512]{1,0:T(8,128)(2,1)S(1)} %get-tuple-element.118), channel_id=1, source_target_pairs={{0,12},{4,0},{8,4},{12,8},{1,13},{5,1},{9,5},{13,9},{2,14},{6,2},{... | collective-permute-start | bytes 196616 | tf_op jit(solution)/shard_map/ppermute | solution.py:670
  291.7 6.8 %collective-permute-start.27 = (bf16[64,896]{1,0:T(8,128)(2,1)S(1)}, bf16[64,896]{1,0:T(8,128)(2,1)S(1)}, u32[]{:S(2)}, u32[]{:S(2)}) collective-permute-start(bf16[64,896]{1,0:T(8,128)(2,1)S(1)} %pad_maximum_fusion.4.near_in), channel_id=1, source_target_pairs={{0,32},{32,0},{1,33},{33,1},{2,34},{34,2},{3,35},{35,3},{4,36},{36... | collective-permute-start | bytes 344072 | tf_op jit(solution)/shard_map/ppermute | solution.py:55
  298.5 9.6 %copy-start.5 = (bf16[64,896]{1,0:T(8,128)(2,1)}, bf16[64,896]{1,0:T(8,128)(2,1)S(1)}, u32[]{:S(2)}) copy-start(bf16[64,896]{1,0:T(8,128)(2,1)S(1)} %collective-permute-done.27.earlier_ref.away_in) | copy-start | bytes 344068
  308.1 18.8 %copy-start.6 = (bf16[64,896]{1,0:T(8,128)(2,1)S(1)}, bf16[64,896]{1,0:T(8,128)(2,1)}, u32[]{:S(2)}) copy-start(bf16[64,896]{1,0:T(8,128)(2,1)} %copy-done.5) | copy-start | bytes 344068
  308.1 14.8 %collective-permute-start.29 = (bf16[64,4608]{1,0:T(8,128)(2,1)}, bf16[64,4608]{1,0:T(8,128)(2,1)S(1)}, u32[]{:S(2)}, u32[]{:S(2)}) collective-permute-start(bf16[64,4608]{1,0:T(8,128)(2,1)} %after.1), channel_id=1, source_target_pairs={{0,32},{32,0},{1,33},{33,1},{2,34},{34,2},{3,35},{35,3},{4,36},{36... | collective-permute-start | bytes 1769480 | tf_op jit(solution)/shard_map/ppermute | solution.py:55
  324.1 6.7 %collective-permute-start.30 = (f32[64,4608]{1,0:T(8,128)S(1)}, f32[64,4608]{1,0:T(8,128)S(1)}, u32[]{:S(2)}, u32[]{:S(2)}) collective-permute-start(f32[64,4608]{1,0:T(8,128)S(1)} %convert_add_fusion.first_in), channel_id=1, source_target_pairs={{0,16},{16,0},{1,17},{17,1},{2,18},{18,2},{3,19},{19,3},{4,20},{20... | collective-permute-start | bytes 3538952 | tf_op jit(solution)/shard_map/ppermute | solution.py:47
  326.8 2.6 collective-permute-start.31
  326.9 2.7 collective-permute-start.32
  327.4 5.3 %copy-start.1 = (bf16[1,256,1024]{2,1,0:T(8,128)(2,1)S(1)}, bf16[1,256,1024]{2,1,0:T(8,128)(2,1)}, u32[]{:S(2)}) copy-start(bf16[1,256,1024]{2,1,0:T(8,128)(2,1)} %param.20) | copy-start | bytes 1572868
Sparse Core Ops, SparseCore 0:
  11.4 96.4 all-gather.1
  214.5 93.5 reduce-scatter.1

commit v3 on v2

--- a/solution.py
+++ b/solution.py
@@ -600,10 +600,11 @@
 
 
 def finish_kernel(
-    core_ref, far_ref, first_in, first2_in, near_in, near2_in, away_in, away2_in,
+    core_ref, far_ref, first_in, first_far_in, first2_in, first2_far_in, near_in, near2_in, away_in, away2_in,
     project_ref, output_ref, up_ref, down_ref
 ):
-    def put(half, first, low, high):
+    def put(half, firsts, low, high):
+        first = firsts[0][...].astype(F32) + firsts[1][...].astype(F32)
         at = half * 2 * QUARTER
         project_ref[:, at : at + QUARTER] = low[:, :QUARTER].astype(F32)
         project_ref[:, at + QUARTER : at + 2 * QUARTER] = high[:, :QUARTER].astype(F32)
@@ -621,8 +622,8 @@
             @pl.when((core_ref[0] == core) & (far_ref[0] == far))
             def _():
                 for half, first, near, away in (
-                    (core, first_in, near_in, away_in),
-                    (1 - core, first2_in, near2_in, away2_in),
+                    (core, (first_in, first_far_in), near_in, away_in),
+                    (1 - core, (first2_in, first2_far_in), near2_in, away2_in),
                 ):
                     put(half, first, *((near, away) if far == 0 else (away, near)))
 
@@ -632,7 +633,7 @@
     smem = pl.BlockSpec(memory_space=pltpu.SMEM)
     return pl.pallas_call(
         finish_kernel,
-        in_specs=[smem, smem] + [vmem] * 6,
+        in_specs=[smem, smem] + [vmem] * 8,
         out_specs=[vmem] * 4,
         out_shape=[
             shaped(64, 3 * WIDTH, kind=F32),
@@ -700,9 +701,8 @@
 
 def over_replicas(owned):
     owned = lax.optimization_barrier(owned)
-    total = owned.astype(F32) + swap_far(owned).astype(F32)
-    total = lax.optimization_barrier(total)
-    return total, swap_cores(total)
+    far = swap_far(owned)
+    return owned, far, swap_cores(owned), swap_cores(far)
 
 
 def gradients(core, first_section, result, own, other, upstream, gathered, pairs, kept):
@@ -747,9 +747,9 @@
         for at, value in enumerate((result, rows_grad))
     )
     near2, away2 = swap_cores(near), swap_cores(away)
-    first, first2 = over_replicas(after(owned, away))
+    firsts = over_replicas(after(owned, away))
     project, output, upward, downward = finish(
-        core, far, first, first2, near, near2, away, away2
+        core, far, *firsts, near, near2, away, away2
     )
     ends = [part[:6, QUARTER:].astype(F32) for part in (near, away, near2, away2)]
     vectors = ((ends[0] + ends[1]) + (ends[2] + ends[3])).reshape(768)

time: 346 us -> 343 us (level)
  waiting for transfers between devices: 176 us -> 171 us
    ppermute x6, waiting for transfers between devices: 26.6 us -> 23 us  [swap_far(): return lax.ppermute(value, 'far', [(0, 1), (1, 0)])]
    ppermute x10 -> x11, starting transfers between devices: 8.45 us -> 10.4 us  [swap_cores(): return lax.ppermute(value, 'core', [(0, 1), (1, 0)])]
  transfers between devices with their start and end apart: 35 -> 36, of which waited for: 23 -> 21; matrix products, arithmetic and copies ran while one was open for 1% -> 1% of each run, Pallas kernels for 18% -> 18%
where the time goes in v3:
time: 343 us; the launch traced here: 337 us
  waiting for transfers between devices  171 us (50%)
  Pallas kernels  89.4 us (26%)
  starting transfers between devices  48.8 us (14%)
  between operations  15.1 us (4%)
  local copies, waits for them, and re-layouts  7.97 us (2%)
  other arithmetic  4.65 us (1%)
    all_gather x1, waiting for transfers between devices, gather_weights(): gathered = lax.all_gather(packed, ('z', 'y', 'core'), axis=0, tiled=True)  92.9 us
    pallas_call x2, Pallas kernels, layer_forward(): pl.pallas_call(functools.partial(forward_kernel, keep), grid=(8,), in_spe...  33.4 us
    ppermute x6, waiting for transfers between devices, swap_far(): return lax.ppermute(value, 'far', [(0, 1), (1, 0)])  23 us
    ppermute x12, waiting for transfers between devices, send_around(): lax.ppermute(blocks[k], axis, [(i, (i + k) % 4) for i in range(4)])  20.8 us
    pallas_call x1, Pallas kernels, layer_through(): pl.pallas_call(through_kernel, grid=(8,), in_specs=[whole((ROWS, WIDTH)),...  17.2 us
    ppermute x12, starting transfers between devices, send_around(): lax.ppermute(blocks[k], axis, [(i, (i + k) % 4) for i in range(4)])  15.1 us
    ppermute x6, starting transfers between devices, swap_far(): return lax.ppermute(value, 'far', [(0, 1), (1, 0)])  13.3 us
    pallas_call x1, Pallas kernels, hidden_backward(): pl.pallas_call(hidden_kernel, grid=(4,), in_specs=[pl.BlockSpec(memory_sp...  12.4 us
  transfers between devices with their start and end apart: 36, of which 21 were waited for; matrix products, arithmetic and copies ran while one was open for 1% of the time, Pallas kernels for 18%

profile of v3, /device:TPU:1, one launch (start us, length us, event | category | flops | bytes accessed | tf_op | source)
XLA Modules:
  0.0 337.1 jit_solution(8865640103348101276)
XLA Ops:
  7.3 0.9 copy-done
  8.3 0.7 reduce
  9.0 1.1 fusion.3
  10.3 0.9 fusion.1
  11.4 3.7 %collective-permute-start.4 = (bf16[128,1024]{1,0:T(8,128)(2,1)S(1)}, bf16[128,1024]{1,0:T(8,128)(2,1)S(1)}, u32[]{:S(2)}, u32[]{:S(2)}) collective-permute-start(bf16[128,1024]{1,0:T(8,128)(2,1)S(1)} %get-tuple-element.164), channel_id=1, source_target_pairs={{0,32},{32,0},{1,33},{33,1},{2,34},{34,2},{3,35},{35,3},{4,36},{36... | collective-permute-start | bytes 786440 | tf_op jit(solution)/shard_map/ppermute | solution.py:55
  15.0 92.9 %all-gather.2.cloned.1.call-done.column_ref.row_ref = bf16[1024,12416]{1,0:T(8,128)(2,1)} async-done(((bf16[32,12416]{1,0:T(8,128)(2,1)}), bf16[1024,12416]{1,0:T(8,128)(2,1)}) %all-gather.2.cloned.1.call-update) | async-done | bytes 25427984 | tf_op jit(solution)/shard_map/all_gather | solution.py:659
  107.9 1.0 slice.151
  109.4 15.8 %layer_forward.2 = bf16[256,1024]{1,0:T(8,128)(2,1)S(1)} custom-call(bf16[256,1024]{1,0:T(8,128)(2,1)S(1)} %bitcast.63, bf16[1024,12416]{1,0:T(8,128)(2,1)} %all-gather.2.cloned.1.call-done.column_ref.row_ref, bf16[1024,12416]{1,0:T(8,128)(2,1)} %all-gather.2.cloned.1.call-done.column_ref.row_ref, f32[1,8192]{1,0:T(1,128)S(1)} %constant_dynamic-update-slice_fusion.bias_ref, ...), custom_call_target="tpu_custom_call" | custom-call | flops 6442450944 | bytes 33554432 | tf_op jit(solution)/shard_map/layer_forward/pallas_call | solution.py:189
  125.3 3.1 collective-permute-start
  128.4 2.5 collective-permute-start.1
  131.0 2.8 collective-permute-done
  133.8 2.5 collective-permute-done.1
  136.6 1.4 collective-permute-start.3
  138.0 17.6 %layer_forward.3 = (bf16[256,1024]{1,0:T(8,128)(2,1)S(1)}, bf16[256,3072]{1,0:T(8,128)(2,1)S(1)}, bf16[256,1024]{1,0:T(8,128)(2,1)S(1)}, bf16[256,1024]{1,0:T(8,...) custom-call(bf16[256,1024]{1,0:T(8,128)(2,1)S(1)} %maximum_select_fu, ...), custom_call_target="tpu_custom_call" | custom-call | flops 6442450944 | bytes 33554432 | tf_op jit(solution)/shard_map/layer_forward/pallas_call | solution.py:189
  155.6 17.2 %layer_through.1 = bf16[256,1024]{1,0:T(8,128)(2,1)S(1)} custom-call(bf16[256,1024]{1,0:T(8,128)(2,1)S(1)} %pad_maximum_fusion.upstream_ref, bf16[1024,12416]{1,0:T(8,128)(2,1)} %all-gather.2.cloned.1.call-done.column_ref.row_ref, bf16[1024,12416]{1,0:T(8,128)(2,1)} %all-gather.2.cloned.1.call-done.column_ref.row_ref, f32[8,1024]{1,0:T(8,128)S(1)} %reshape.101.pairs_ref, ...), custom_call_target="tpu_custom_call" | custom-call | flops 6442450944 | bytes 33554432 | tf_op jit(solution)/shard_map/layer_through/pallas_call | solution.py:363
  172.8 1.3 collective-permute-start.5
  174.1 1.3 collective-permute-start.6
  175.4 1.6 collective-permute-start.8
  177.1 5.1 %collective-permute-done.5 = bf16[128,1024]{1,0:T(8,128)(2,1)S(1)} collective-permute-done((bf16[128,1024]{1,0:T(8,128)(2,1)S(1)}, bf16[128,1024]{1,0:T(8,128)(2,1)S(1)}, u32[]{:S(2)}, u32[]{:S(2)}) %collective-permute-start.5) | collective-permute-done | bytes 262176 | tf_op jit(solution)/shard_map/ppermute | solution.py:781
  182.2 1.5 collective-permute-done.6
  183.9 12.4 %hidden_backward.1 = (f32[256,1024]{1,0:T(8,128)S(1)}, bf16[256,3072]{1,0:T(8,128)(2,1)S(1)}, bf16[256,3072]{1,0:T(8,128)(2,1)}, f32[8,1024]{1,0:T(8,128)S(1)}, f32[1,4096]{1,0:T(1,128)S(1)}) custom-call(s32[1]{0:T(128)} %bitcast.20.core_ref, bf16[256,1024]{1,0:T(8,128)(2,1)S(1)} %maximum_select_fusion.1.upstream_ref, ...), custom_call_target="tpu_custom_call" | custom-call | flops 3865470464 | bytes 20132660 | tf_op jit(solution)/shard_map/hidden_backward/pallas_call | solution.py:414
  196.3 1.0 copy-done.6
  197.3 2.3 collective-permute-start.10
  200.0 3.1 collective-permute-done.7.h2_ref
  203.2 0.7 collective-permute-done.9.c2_ref
  204.3 1.0 copy-done.13
  205.2 9.0 %first_grads.1 = bf16[1024,4608]{1,0:T(8,128)(2,1)} custom-call(bf16[256,1024]{1,0:T(8,128)(2,1)S(1)} %get-tuple-element.72.h_ref, bf16[256,4096]{1,0:T(8,128)(2,1)} %get-tuple-element.73.e_ref, bf16[256,1024]{1,0:T(8,128)(2,1)S(1)} %get-tuple-element.74.c_ref, bf16[256,3072]{1,0:T(8,128)(2,1)S(1)} %get-tuple-element.82.left_ref, ...), custom_call_target="tpu_custom_call" | custom-call | flops 4509715456 | bytes 23488102 | tf_op jit(solution)/shard_map/first_grads/pallas_call | solution.py:522
  214.5 1.2 copy-done.7
  215.8 10.4 %attention_backward.1 = (bf16[256,1024]{1,0:T(8,128)(2,1)S(1)}, bf16[256,768]{1,0:T(8,128)(2,1)S(1)}, bf16[256,768]{1,0:T(8,128)(2,1)}, bf16[256,768]{1,0:T(8,12...) custom-call(s32[1]{0:T(128)S(6)} %add.47.device_ref, f32[256,1024]{1,0:T(8,128)S(1)} %copy-done.7, ...), custom_call_target="tpu_custom_call" | custom-call | flops 3221225472 | bytes 16777216 | tf_op jit(solution)/shard_map/attention_backward/pallas_call | solution.py:474
  226.1 0.7 copy-done.10
  227.3 1.6 collective-permute-start.13
  228.8 1.7 collective-permute-start.14
  231.3 8.4 %collective-permute-done.13.refs_6_ = bf16[256,768]{1,0:T(8,128)(2,1)} collective-permute-done((bf16[256,768]{1,0:T(8,128)(2,1)}, bf16[256,768]{1,0:T(8,128)(2,1)}, u32[]{:S(2)}, u32[]{:S(2)}) %collective-permute-start.13) | collective-permute-done | bytes 393248 | tf_op jit(solution)/shard_map/ppermute | solution.py:55
  239.7 8.7 %collective-permute-done.14.refs_7_ = bf16[256,768]{1,0:T(8,128)(2,1)} collective-permute-done((bf16[256,768]{1,0:T(8,128)(2,1)}, bf16[256,768]{1,0:T(8,128)(2,1)}, u32[]{:S(2)}, u32[]{:S(2)}) %collective-permute-start.14) | collective-permute-done | bytes 393248 | tf_op jit(solution)/shard_map/ppermute | solution.py:51
  248.4 4.1 %last_grads.1 = (bf16[256,384]{1,0:T(8,128)(2,1)S(1)}, bf16[256,384]{1,0:T(8,128)(2,1)S(1)}, bf16[256,384]{1,0:T(8,128)(2,1)S(1)}, bf16[256,384]{1,0:T(8,128)(2,...) custom-call(s32[2]{0:T(128)S(1)} %pad_add_fusion.place_ref, ...), custom_call_target="tpu_custom_call" | custom-call | flops 2254857728 | bytes 11744051 | tf_op jit(solution)/shard_map/last_grads/pallas_call | solution.py:557
  252.5 0.6 collective-permute-start.15
  253.1 0.7 collective-permute-start.18
  253.8 2.4 collective-permute-start.19
  256.3 1.2 collective-permute-start.20
  257.4 2.0 collective-permute-start.16
  259.4 4.8 %collective-permute-done.15.refs_1_ = bf16[256,384]{1,0:T(8,128)(2,1)S(1)} collective-permute-done((bf16[256,384]{1,0:T(8,128)(2,1)S(1)}, bf16[256,384]{1,0:T(8,128)(2,1)S(1)}, u32[]{:S(2)}, u32[]{:S(2)}) %collective-permute-start.15) | collective-permute-done | bytes 196640 | tf_op jit(solution)/shard_map/ppermute | solution.py:671
  264.2 1.4 collective-permute-start.17
  265.6 8.0 %collective-permute-done.16.refs_2_ = bf16[256,384]{1,0:T(8,128)(2,1)S(1)} collective-permute-done((bf16[256,384]{1,0:T(8,128)(2,1)S(1)}, bf16[256,384]{1,0:T(8,128)(2,1)S(1)}, u32[]{:S(2)}, u32[]{:S(2)}) %collective-permute-start.16) | collective-permute-done | bytes 196640 | tf_op jit(solution)/shard_map/ppermute | solution.py:671
  273.6 1.9 collective-permute-done.17.refs_3_
  275.5 3.1 collective-permute-done.19.refs_6_
  278.6 1.0 halfway.1
  279.7 1.0 collective-permute-start.22
  280.6 2.0 collective-permute-start.23
  282.6 2.1 collective-permute-start.28
  284.9 3.2 collective-permute-start.25
  288.1 0.6 collective-permute-start.26
  288.7 0.6 collective-permute-done.24
  289.4 1.4 collective-permute-done.25
  290.7 0.8 collective-permute-done.26
  291.6 1.7 collective-permute-start.27
  293.3 5.1 %collective-permute-done.27.earlier_ref.away_in = bf16[64,896]{1,0:T(8,128)(2,1)S(1)} collective-permute-done((bf16[64,896]{1,0:T(8,128)(2,1)S(1)}, bf16[64,896]{1,0:T(8,128)(2,1)S(1)}, u32[]{:S(2)}, u32[]{:S(2)}) %collective-permute-start.27) | collective-permute-done | bytes 114720 | tf_op jit(solution)/shard_map/ppermute | solution.py:55
  298.4 9.6 %reduce-scatter.2.cloned.1.call-done.value_ref = bf16[64,4608]{1,0:T(8,128)(2,1)} async-done(((bf16[1024,4608]{1,0:T(8,128)(2,1)}), bf16[64,4608]{1,0:T(8,128)(2,1)}) %reduce-scatter.2.cloned.1.call-update) | async-done | bytes 589840 | tf_op jit(solution)/shard_map/reduce_scatter | solution.py:719
  308.0 2.8 collective-permute-start.29
  310.7 2.0 collective-permute-start.32
  313.2 9.5 %collective-permute-done.29.first_far_in = bf16[64,4608]{1,0:T(8,128)(2,1)S(1)} collective-permute-done((bf16[64,4608]{1,0:T(8,128)(2,1)}, bf16[64,4608]{1,0:T(8,128)(2,1)S(1)}, u32[]{:S(2)}, u32[]{:S(2)}) %collective-permute-start.29) | collective-permute-done | bytes 589856 | tf_op jit(solution)/shard_map/ppermute | solution.py:55
  322.8 2.7 collective-permute-start.31
  325.6 1.0 pad_maximum_fusion.2
  327.2 0.6 slice_bitcast_fusion.2
  327.8 2.0 finish.1
  (112 shorter events, 5.1 us)
Async XLA Ops:
  7.2 1.1 copy-start
  7.2 2.9 copy-start.19
  7.2 2.9 copy-start.20
  7.2 2.9 copy-start.21
  7.2 2.9 copy-start.22
  7.2 2.9 copy-start.15
  7.3 2.9 copy-start.16
  7.3 2.9 copy-start.17
  7.3 2.9 copy-start.18
  7.3 100.6 %all-gather.2.cloned.1.call-start = ((), (), s32[]{:S(2)}) async-start(), calls=%async_computation.1 | async-start | bytes 26222592 | tf_op jit(solution)/shard_map/all_gather | solution.py:659
  10.1 1.2 copy-start.14
  11.2 98.2 %copy-start.3 = (bf16[2,1,128,1024]{3,2,1,0:T(8,128)(2,1)S(1)}, bf16[2,1,128,1024]{3,2,1,0:T(8,128)(2,1)}, u32[]{:S(2)}) copy-start(bf16[2,1,128,1024]{3,2,1,0:T(8,128)(2,1)} %param.15) | copy-start | bytes 1572868
  11.3 296.7 %reduce-scatter.2.cloned.1.call-start = ((), (), s32[]{:S(2)}) async-start(), calls=%async_computation.2 | async-start | bytes 10027008 | tf_op jit(solution)/shard_map/reduce_scatter | solution.py:719
  11.4 119.6 %collective-permute-start.4 = (bf16[128,1024]{1,0:T(8,128)(2,1)S(1)}, bf16[128,1024]{1,0:T(8,128)(2,1)S(1)}, u32[]{:S(2)}, u32[]{:S(2)}) collective-permute-start(bf16[128,1024]{1,0:T(8,128)(2,1)S(1)} %get-tuple-element.164), channel_id=1, source_target_pairs={{0,32},{32,0},{1,33},{33,1},{2,34},{34,2},{3,35},{35,3},{4,36},{36... | collective-permute-start | bytes 786440 | tf_op jit(solution)/shard_map/ppermute | solution.py:55
  125.3 8.5 %collective-permute-start = (bf16[128,1024]{1,0:T(8,128)(2,1)S(1)}, bf16[128,1024]{1,0:T(8,128)(2,1)S(1)}, u32[]{:S(2)}, u32[]{:S(2)}) collective-permute-start(bf16[128,1024]{1,0:T(8,128)(2,1)S(1)} %get-tuple-element.165), channel_id=1, source_target_pairs={{0,64},{32,96},{1,65},{33,97},{2,66},{34,98},{3,67},{35,99},{4,68}... | collective-permute-start | bytes 786440 | tf_op jit(solution)/shard_map/ppermute | solution.py:781
  128.4 7.9 %collective-permute-start.1 = (bf16[128,1024]{1,0:T(8,128)(2,1)S(1)}, bf16[128,1024]{1,0:T(8,128)(2,1)S(1)}, u32[]{:S(2)}, u32[]{:S(2)}) collective-permute-start(bf16[128,1024]{1,0:T(8,128)(2,1)S(1)} %get-tuple-element.166), channel_id=1, source_target_pairs={{0,96},{32,64},{1,97},{33,65},{2,98},{34,66},{3,99},{35,67},{4,100... | collective-permute-start | bytes 786440 | tf_op jit(solution)/shard_map/ppermute | solution.py:781
  136.6 19.1 %collective-permute-start.3 = (bf16[256,1024]{1,0:T(8,128)(2,1)S(1)}, bf16[256,1024]{1,0:T(8,128)(2,1)}, u32[]{:S(2)}, u32[]{:S(2)}) collective-permute-start(bf16[256,1024]{1,0:T(8,128)(2,1)S(1)} %maximum_select_fusion.x_ref.refs_0_), channel_id=1, source_target_pairs={{0,32},{32,0},{1,33},{33,1},{2,34},{34,2},{3,35},{35,3},{4,36},{36... | collective-permute-start | bytes 1572872 | tf_op jit(solution)/shard_map/ppermute | solution.py:55
  155.6 19.8 %copy-start.12 = (bf16[256,4096]{1,0:T(8,128)(2,1)S(1)}, bf16[256,4096]{1,0:T(8,128)(2,1)}, u32[]{:S(2)}) copy-start(bf16[256,4096]{1,0:T(8,128)(2,1)} %get-tuple-element.73.e_ref) | copy-start | bytes 6291460
  172.8 9.3 %collective-permute-start.5 = (bf16[128,1024]{1,0:T(8,128)(2,1)S(1)}, bf16[128,1024]{1,0:T(8,128)(2,1)S(1)}, u32[]{:S(2)}, u32[]{:S(2)}) collective-permute-start(bf16[128,1024]{1,0:T(8,128)(2,1)S(1)} %get-tuple-element.161), channel_id=1, source_target_pairs={{64,0},{96,32},{65,1},{97,33},{66,2},{98,34},{67,3},{99,35},{68,4}... | collective-permute-start | bytes 786440 | tf_op jit(solution)/shard_map/ppermute | solution.py:781
  174.1 9.6 %collective-permute-start.6 = (bf16[128,1024]{1,0:T(8,128)(2,1)S(1)}, bf16[128,1024]{1,0:T(8,128)(2,1)S(1)}, u32[]{:S(2)}, u32[]{:S(2)}) collective-permute-start(bf16[128,1024]{1,0:T(8,128)(2,1)S(1)} %get-tuple-element.162), channel_id=1, source_target_pairs={{96,0},{64,32},{97,1},{65,33},{98,2},{66,34},{99,3},{67,35},{100,4... | collective-permute-start | bytes 786440 | tf_op jit(solution)/shard_map/ppermute | solution.py:781
  175.4 28.5 %collective-permute-start.8 = (bf16[256,4096]{1,0:T(8,128)(2,1)S(1)}, bf16[256,4096]{1,0:T(8,128)(2,1)S(1)}, u32[]{:S(2)}, u32[]{:S(2)}) collective-permute-start(bf16[256,4096]{1,0:T(8,128)(2,1)S(1)} %copy-done.12), channel_id=1, source_target_pairs={{0,16},{16,0},{1,17},{17,1},{2,18},{18,2},{3,19},{19,3},{4,20},{20... | collective-permute-start | bytes 6291464 | tf_op jit(solution)/shard_map/ppermute | solution.py:47
  196.3 1.0 copy-start.6
  197.3 7.0 %collective-permute-start.10 = (bf16[256,3072]{1,0:T(8,128)(2,1)}, bf16[256,3072]{1,0:T(8,128)(2,1)S(1)}, u32[]{:S(2)}, u32[]{:S(2)}) collective-permute-start(bf16[256,3072]{1,0:T(8,128)(2,1)} %get-tuple-element.83), channel_id=1, source_target_pairs={{0,16},{16,0},{1,17},{17,1},{2,18},{18,2},{3,19},{19,3},{4,20},{20... | collective-permute-start | bytes 4718600 | tf_op jit(solution)/shard_map/ppermute | solution.py:47
  199.5 3.7 %collective-permute-start.7 = (bf16[256,1024]{1,0:T(8,128)(2,1)S(1)}, bf16[256,1024]{1,0:T(8,128)(2,1)S(1)}, u32[]{:S(2)}, u32[]{:S(2)}) collective-permute-start(bf16[256,1024]{1,0:T(8,128)(2,1)S(1)} %get-tuple-element.72.h_ref), channel_id=1, source_target_pairs={{0,16},{16,0},{1,17},{17,1},{2,18},{18,2},{3,19},{19,3},{4,20},{20... | collective-permute-start | bytes 1572872 | tf_op jit(solution)/shard_map/ppermute | solution.py:47
  199.5 4.4 %collective-permute-start.9 = (bf16[256,1024]{1,0:T(8,128)(2,1)S(1)}, bf16[256,1024]{1,0:T(8,128)(2,1)S(1)}, u32[]{:S(2)}, u32[]{:S(2)}) collective-permute-start(bf16[256,1024]{1,0:T(8,128)(2,1)S(1)} %get-tuple-element.74.c_ref), channel_id=1, source_target_pairs={{0,16},{16,0},{1,17},{17,1},{2,18},{18,2},{3,19},{19,3},{4,20},{20... | collective-permute-start | bytes 1572872 | tf_op jit(solution)/shard_map/ppermute | solution.py:47
  203.9 1.3 copy-start.13
  214.4 16.9 %collective-permute-start.2 = (bf16[256,1024]{1,0:T(8,128)(2,1)S(1)}, bf16[256,1024]{1,0:T(8,128)(2,1)}, u32[]{:S(2)}, u32[]{:S(2)}) collective-permute-start(bf16[256,1024]{1,0:T(8,128)(2,1)S(1)} %maximum_select_fusion.x_ref.refs_0_), channel_id=1, source_target_pairs={{0,16},{16,0},{1,17},{17,1},{2,18},{18,2},{3,19},{19,3},{4,20},{20... | collective-permute-start | bytes 1572872 | tf_op jit(solution)/shard_map/ppermute | solution.py:47
  214.5 1.2 copy-start.7
  226.1 0.7 copy-start.10
  226.9 25.6 %copy-start.4 = (bf16[256,1024]{1,0:T(8,128)(2,1)}, bf16[256,1024]{1,0:T(8,128)(2,1)S(1)}, u32[]{:S(2)}) copy-start(bf16[256,1024]{1,0:T(8,128)(2,1)S(1)} %get-tuple-element.102) | copy-start | bytes 1572868
  226.9 21.5 %copy-start.11 = (bf16[256,768]{1,0:T(8,128)(2,1)S(1)}, bf16[256,768]{1,0:T(8,128)(2,1)}, u32[]{:S(2)}) copy-start(bf16[256,768]{1,0:T(8,128)(2,1)} %copy-done.10) | copy-start | bytes 1179652
  226.9 4.4 %collective-permute-start.12 = (bf16[256,768]{1,0:T(8,128)(2,1)}, bf16[256,768]{1,0:T(8,128)(2,1)S(1)}, u32[]{:S(2)}, u32[]{:S(2)}) collective-permute-start(bf16[256,768]{1,0:T(8,128)(2,1)} %get-tuple-element.88), channel_id=1, source_target_pairs={{0,16},{16,0},{1,17},{17,1},{2,18},{18,2},{3,19},{19,3},{4,20},{20... | collective-permute-start | bytes 1179656 | tf_op jit(solution)/shard_map/ppermute | solution.py:47
  227.3 12.4 %collective-permute-start.13 = (bf16[256,768]{1,0:T(8,128)(2,1)}, bf16[256,768]{1,0:T(8,128)(2,1)}, u32[]{:S(2)}, u32[]{:S(2)}) collective-permute-start(bf16[256,768]{1,0:T(8,128)(2,1)} %get-tuple-element.89), channel_id=1, source_target_pairs={{0,32},{32,0},{1,33},{33,1},{2,34},{34,2},{3,35},{35,3},{4,36},{36... | collective-permute-start | bytes 1179656 | tf_op jit(solution)/shard_map/ppermute | solution.py:55
  228.8 19.5 %collective-permute-start.14 = (bf16[256,768]{1,0:T(8,128)(2,1)}, bf16[256,768]{1,0:T(8,128)(2,1)}, u32[]{:S(2)}, u32[]{:S(2)}) collective-permute-start(bf16[256,768]{1,0:T(8,128)(2,1)} %get-tuple-element.90), channel_id=1, source_target_pairs={{0,48},{16,32},{32,16},{48,0},{1,49},{17,33},{33,17},{49,1},{2,50}... | collective-permute-start | bytes 1179656 | tf_op jit(solution)/shard_map/ppermute | solution.py:51
  230.6 17.8 %collective-permute-start.11 = (bf16[256,1024]{1,0:T(8,128)(2,1)}, bf16[256,1024]{1,0:T(8,128)(2,1)S(1)}, u32[]{:S(2)}, u32[]{:S(2)}) collective-permute-start(bf16[256,1024]{1,0:T(8,128)(2,1)} %collective-permute-done.3.refs_2_), channel_id=1, source_target_pairs={{0,16},{16,0},{1,17},{17,1},{2,18},{18,2},{3,19},{19,3},{4,20},{20... | collective-permute-start | bytes 1572872 | tf_op jit(solution)/shard_map/ppermute | solution.py:47
  252.5 11.7 %collective-permute-start.15 = (bf16[256,384]{1,0:T(8,128)(2,1)S(1)}, bf16[256,384]{1,0:T(8,128)(2,1)S(1)}, u32[]{:S(2)}, u32[]{:S(2)}) collective-permute-start(bf16[256,384]{1,0:T(8,128)(2,1)S(1)} %get-tuple-element.104), channel_id=1, source_target_pairs={{0,4},{4,8},{8,12},{12,0},{1,5},{5,9},{9,13},{13,1},{2,6},{6,10},{... | collective-permute-start | bytes 589832 | tf_op jit(solution)/shard_map/ppermute | solution.py:671
  253.1 22.4 %collective-permute-start.18 = (bf16[4,64,512]{2,1,0:T(8,128)(2,1)S(1)}, bf16[4,64,512]{2,1,0:T(8,128)(2,1)S(1)}, u32[]{:S(2)}, u32[]{:S(2)}) collective-permute-start(bf16[4,64,512]{2,1,0:T(8,128)(2,1)S(1)} %get-tuple-element.108), channel_id=1, source_target_pairs={{0,1},{1,2},{2,3},{3,0},{4,5},{5,6},{6,7},{7,4},{8,9},{9,10},{10,1... | collective-permute-start | bytes 786440 | tf_op jit(solution)/shard_map/ppermute | solution.py:671
  253.8 24.8 %collective-permute-start.19 = (bf16[4,64,512]{2,1,0:T(8,128)(2,1)S(1)}, bf16[4,64,512]{2,1,0:T(8,128)(2,1)S(1)}, u32[]{:S(2)}, u32[]{:S(2)}) collective-permute-start(bf16[4,64,512]{2,1,0:T(8,128)(2,1)S(1)} %get-tuple-element.109), channel_id=1, source_target_pairs={{0,2},{1,3},{2,0},{3,1},{4,6},{5,7},{6,4},{7,5},{8,10},{9,11},{10,... | collective-permute-start | bytes 786440 | tf_op jit(solution)/shard_map/ppermute | solution.py:671
  256.3 22.3 %collective-permute-start.20 = (bf16[4,64,512]{2,1,0:T(8,128)(2,1)S(1)}, bf16[4,64,512]{2,1,0:T(8,128)(2,1)S(1)}, u32[]{:S(2)}, u32[]{:S(2)}) collective-permute-start(bf16[4,64,512]{2,1,0:T(8,128)(2,1)S(1)} %get-tuple-element.110), channel_id=1, source_target_pairs={{0,3},{1,0},{2,1},{3,2},{4,7},{5,4},{6,5},{7,6},{8,11},{9,8},{10,9... | collective-permute-start | bytes 786440 | tf_op jit(solution)/shard_map/ppermute | solution.py:671
  257.4 16.2 %collective-permute-start.16 = (bf16[256,384]{1,0:T(8,128)(2,1)S(1)}, bf16[256,384]{1,0:T(8,128)(2,1)S(1)}, u32[]{:S(2)}, u32[]{:S(2)}) collective-permute-start(bf16[256,384]{1,0:T(8,128)(2,1)S(1)} %get-tuple-element.105), channel_id=1, source_target_pairs={{0,8},{4,12},{8,0},{12,4},{1,9},{5,13},{9,1},{13,5},{2,10},{6,14},... | collective-permute-start | bytes 589832 | tf_op jit(solution)/shard_map/ppermute | solution.py:671
  264.2 11.3 %collective-permute-start.17 = (bf16[256,384]{1,0:T(8,128)(2,1)S(1)}, bf16[256,384]{1,0:T(8,128)(2,1)S(1)}, u32[]{:S(2)}, u32[]{:S(2)}) collective-permute-start(bf16[256,384]{1,0:T(8,128)(2,1)S(1)} %get-tuple-element.106), channel_id=1, source_target_pairs={{0,12},{4,0},{8,4},{12,8},{1,13},{5,1},{9,5},{13,9},{2,14},{6,2},{... | collective-permute-start | bytes 589832 | tf_op jit(solution)/shard_map/ppermute | solution.py:671
  279.6 45.9 %copy-start.5 = (bf16[256,1024]{1,0:T(8,128)(2,1)S(1)}, bf16[256,1024]{1,0:T(8,128)(2,1)}, u32[]{:S(2)}) copy-start(bf16[256,1024]{1,0:T(8,128)(2,1)} %copy-done.4) | copy-start | bytes 1572868
  279.6 5.4 %collective-permute-start.21 = (bf16[64,384]{1,0:T(8,128)(2,1)S(1)}, bf16[64,384]{1,0:T(8,128)(2,1)S(1)}, u32[]{:S(2)}, u32[]{:S(2)}) collective-permute-start(bf16[64,384]{1,0:T(8,128)(2,1)S(1)} %get-tuple-element.112), channel_id=1, source_target_pairs={{0,1},{1,2},{2,3},{3,0},{4,5},{5,6},{6,7},{7,4},{8,9},{9,10},{10,1... | collective-permute-start | bytes 147464 | tf_op jit(solution)/shard_map/ppermute | solution.py:671
  279.7 8.4 %collective-permute-start.22 = (bf16[64,384]{1,0:T(8,128)(2,1)S(1)}, bf16[64,384]{1,0:T(8,128)(2,1)S(1)}, u32[]{:S(2)}, u32[]{:S(2)}) collective-permute-start(bf16[64,384]{1,0:T(8,128)(2,1)S(1)} %get-tuple-element.113), channel_id=1, source_target_pairs={{0,2},{1,3},{2,0},{3,1},{4,6},{5,7},{6,4},{7,5},{8,10},{9,11},{10,... | collective-permute-start | bytes 147464 | tf_op jit(solution)/shard_map/ppermute | solution.py:671
  280.6 8.1 %collective-permute-start.23 = (bf16[64,384]{1,0:T(8,128)(2,1)S(1)}, bf16[64,384]{1,0:T(8,128)(2,1)S(1)}, u32[]{:S(2)}, u32[]{:S(2)}) collective-permute-start(bf16[64,384]{1,0:T(8,128)(2,1)S(1)} %get-tuple-element.114), channel_id=1, source_target_pairs={{0,3},{1,0},{2,1},{3,2},{4,7},{5,4},{6,5},{7,6},{8,11},{9,8},{10,9... | collective-permute-start | bytes 147464 | tf_op jit(solution)/shard_map/ppermute | solution.py:671
  282.6 15.8 %collective-permute-start.28 = (bf16[256,1024]{1,0:T(8,128)(2,1)S(1)}, bf16[256,1024]{1,0:T(8,128)(2,1)S(1)}, u32[]{:S(2)}, u32[]{:S(2)}) collective-permute-start(bf16[256,1024]{1,0:T(8,128)(2,1)S(1)} %pad_maximum_fusion.1), channel_id=1, source_target_pairs={{0,32},{32,0},{1,33},{33,1},{2,34},{34,2},{3,35},{35,3},{4,36},{36... | collective-permute-start | bytes 1572872 | tf_op jit(solution)/shard_map/ppermute | solution.py:55
  284.7 4.6 %collective-permute-start.24 = (bf16[64,512]{1,0:T(8,128)(2,1)S(1)}, bf16[64,512]{1,0:T(8,128)(2,1)S(1)}, u32[]{:S(2)}, u32[]{:S(2)}) collective-permute-start(bf16[64,512]{1,0:T(8,128)(2,1)S(1)} %get-tuple-element.116), channel_id=1, source_target_pairs={{0,4},{4,8},{8,12},{12,0},{1,5},{5,9},{9,13},{13,1},{2,6},{6,10},{... | collective-permute-start | bytes 196616 | tf_op jit(solution)/shard_map/ppermute | solution.py:671
  284.9 5.8 %collective-permute-start.25 = (bf16[64,512]{1,0:T(8,128)(2,1)S(1)}, bf16[64,512]{1,0:T(8,128)(2,1)S(1)}, u32[]{:S(2)}, u32[]{:S(2)}) collective-permute-start(bf16[64,512]{1,0:T(8,128)(2,1)S(1)} %get-tuple-element.117), channel_id=1, source_target_pairs={{0,8},{4,12},{8,0},{12,4},{1,9},{5,13},{9,1},{13,5},{2,10},{6,14},... | collective-permute-start | bytes 196616 | tf_op jit(solution)/shard_map/ppermute | solution.py:671
  288.1 3.4 %collective-permute-start.26 = (bf16[64,512]{1,0:T(8,128)(2,1)S(1)}, bf16[64,512]{1,0:T(8,128)(2,1)S(1)}, u32[]{:S(2)}, u32[]{:S(2)}) collective-permute-start(bf16[64,512]{1,0:T(8,128)(2,1)S(1)} %get-tuple-element.118), channel_id=1, source_target_pairs={{0,12},{4,0},{8,4},{12,8},{1,13},{5,1},{9,5},{13,9},{2,14},{6,2},{... | collective-permute-start | bytes 196616 | tf_op jit(solution)/shard_map/ppermute | solution.py:671
  291.6 6.8 %collective-permute-start.27 = (bf16[64,896]{1,0:T(8,128)(2,1)S(1)}, bf16[64,896]{1,0:T(8,128)(2,1)S(1)}, u32[]{:S(2)}, u32[]{:S(2)}) collective-permute-start(bf16[64,896]{1,0:T(8,128)(2,1)S(1)} %pad_maximum_fusion.4.near_in), channel_id=1, source_target_pairs={{0,32},{32,0},{1,33},{33,1},{2,34},{34,2},{3,35},{35,3},{4,36},{36... | collective-permute-start | bytes 344072 | tf_op jit(solution)/shard_map/ppermute | solution.py:55
  298.4 9.6 %copy-start.8 = (bf16[64,896]{1,0:T(8,128)(2,1)}, bf16[64,896]{1,0:T(8,128)(2,1)S(1)}, u32[]{:S(2)}) copy-start(bf16[64,896]{1,0:T(8,128)(2,1)S(1)} %collective-permute-done.27.earlier_ref.away_in) | copy-start | bytes 344068
  308.0 14.8 %collective-permute-start.29 = (bf16[64,4608]{1,0:T(8,128)(2,1)}, bf16[64,4608]{1,0:T(8,128)(2,1)S(1)}, u32[]{:S(2)}, u32[]{:S(2)}) collective-permute-start(bf16[64,4608]{1,0:T(8,128)(2,1)} %after.1.first_in), channel_id=1, source_target_pairs={{0,32},{32,0},{1,33},{33,1},{2,34},{34,2},{3,35},{35,3},{4,36},{36... | collective-permute-start | bytes 1769480 | tf_op jit(solution)/shard_map/ppermute | solution.py:55
  310.7 15.9 %collective-permute-start.32 = (bf16[64,896]{1,0:T(8,128)(2,1)S(1)}, bf16[64,896]{1,0:T(8,128)(2,1)S(1)}, u32[]{:S(2)}, u32[]{:S(2)}) collective-permute-start(bf16[64,896]{1,0:T(8,128)(2,1)S(1)} %pad_maximum_fusion.4.near_in), channel_id=1, source_target_pairs={{0,16},{16,0},{1,17},{17,1},{2,18},{18,2},{3,19},{19,3},{4,20},{20... | collective-permute-start | bytes 344072 | tf_op jit(solution)/shard_map/ppermute | solution.py:47
  312.7 13.9 %collective-permute-start.33 = (bf16[64,896]{1,0:T(8,128)(2,1)}, bf16[64,896]{1,0:T(8,128)(2,1)S(1)}, u32[]{:S(2)}, u32[]{:S(2)}) collective-permute-start(bf16[64,896]{1,0:T(8,128)(2,1)} %copy-done.8), channel_id=1, source_target_pairs={{0,16},{16,0},{1,17},{17,1},{2,18},{18,2},{3,19},{19,3},{4,20},{20... | collective-permute-start | bytes 344072 | tf_op jit(solution)/shard_map/ppermute | solution.py:47
  312.7 15.1 %collective-permute-start.30 = (bf16[64,4608]{1,0:T(8,128)(2,1)}, bf16[64,4608]{1,0:T(8,128)(2,1)S(1)}, u32[]{:S(2)}, u32[]{:S(2)}) collective-permute-start(bf16[64,4608]{1,0:T(8,128)(2,1)} %after.1.first_in), channel_id=1, source_target_pairs={{0,16},{16,0},{1,17},{17,1},{2,18},{18,2},{3,19},{19,3},{4,20},{20... | collective-permute-start | bytes 1769480 | tf_op jit(solution)/shard_map/ppermute | solution.py:47
  322.8 5.0 %collective-permute-start.31 = (bf16[64,4608]{1,0:T(8,128)(2,1)S(1)}, bf16[64,4608]{1,0:T(8,128)(2,1)S(1)}, u32[]{:S(2)}, u32[]{:S(2)}) collective-permute-start(bf16[64,4608]{1,0:T(8,128)(2,1)S(1)} %collective-permute-done.29.first_far_in), channel_id=1, source_target_pairs={{0,16},{16,0},{1,17},{17,1},{2,18},{18,2},{3,19},{19,3},{4,20},{20... | collective-permute-start | bytes 1769480 | tf_op jit(solution)/shard_map/ppermute | solution.py:47
  325.5 1.1 copy-start.9
  325.5 2.3 copy-start.2
  325.6 4.2 %copy-start.1 = (bf16[1,256,1024]{2,1,0:T(8,128)(2,1)S(1)}, bf16[1,256,1024]{2,1,0:T(8,128)(2,1)}, u32[]{:S(2)}) copy-start(bf16[1,256,1024]{2,1,0:T(8,128)(2,1)} %param.20) | copy-start | bytes 1572868
Sparse Core Ops, SparseCore 0:
  11.4 96.4 all-gather.1
  214.4 93.5 reduce-scatter.1
